TPU v7x, 32 devices: a whole 2x2x4 slice. The times are simulated.
32 devices in a mesh: dp: 4 (over y, x), expert: 8 (over z, core).
Axes of the slice: x: 2, y: 2, z: 4, core: 2. Of those that a mesh axis runs over, the one named last changes fastest.
Arguments:
- tokens: bfloat16 [2048, 4096], P('expert', 'dp'), may hold values from -6 to 6
- gate_weight: bfloat16 [64, 4096, 768], P('expert', 'dp'), may hold values from -0.09375 to 0.09375
- up_weight: bfloat16 [64, 4096, 768], P('expert', 'dp'), may hold values from -0.09375 to 0.09375
- down_weight: bfloat16 [64, 768, 4096], P('expert', None, 'dp'), may hold values from -0.21875 to 0.21875
- routes: int32 [2048, 8], P('expert'), may hold values from 0 to 63, all different within a row; in each aligned block of 256 rows (0 to 255, 256 to 511, ...) at most 40 rows name the same one
- gate_levels: int32 [2048, 8], P('expert'), may hold values from 1 to 255
- log_ratio: float32 [2048], P('expert'), may hold values from -3 to 3
- cotangent: bfloat16 [2048, 4096], P('expert', 'dp'), may hold values from -6 to 6
Outputs:
- mixed_out: bfloat16 [2048, 4096], P('expert', 'dp')
- token_grad: bfloat16 [2048, 4096], P('expert', 'dp')
- gate_grad: float32 [2048, 8], P('expert')
Inputs may be any that keep to these rules, and one draw needn't show every extreme that they name: `routes`: each row names 8 different experts; within the rows of one index of expert (aligned blocks of 256 rows) no expert is named more than 40 times, a bound that some block reaches.
All inputs are finite; a program needn't handle non-finite values.
Results may differ from a plain program's by a relative error of at most 0.014.
Values may be sent and summed in bfloat16 or wider, within the bound.
No kernel may reach another device: no remote copies, remote signals or barrier semaphores. Data moves between devices by JAX's collectives and lax.ppermute only.
A program may use at most 192 MiB of HBM per device.

v0:
```python
import jax
import jax.numpy as jnp
from jax import lax
from jax.sharding import PartitionSpec as P

EXPERTS = 64
TOPK = 8
CAP = 40


clip_ratio = 2.0


def on_device(
    tokens, gate_weight, up_weight, down_weight, routes, gate_levels, log_ratio, cotangent
):
    local_tokens = tokens.shape[0]
    feature_slice = tokens.shape[1]
    hidden = gate_weight.shape[2]
    per_device = gate_weight.shape[0]
    peer_count = lax.axis_size("expert")
    slots_total = EXPERTS * CAP
    pick_ids = routes.reshape(-1)
    onehot_table = (pick_ids[:, None] == jnp.arange(EXPERTS, dtype=jnp.int32)[None, :]).astype(
        jnp.int32
    )
    earlier = jnp.cumsum(onehot_table, axis=0) - onehot_table
    position = jnp.sum(earlier * onehot_table, axis=1)
    target = pick_ids * CAP + position

    def pack_rows(values):
        packed = jnp.zeros((slots_total, feature_slice), jnp.bfloat16).at[target].set(values)
        return packed.reshape(peer_count, per_device * CAP, feature_slice)

    received = lax.all_to_all(
        pack_rows(jnp.repeat(tokens, TOPK, axis=0)),
        "expert",
        split_axis=0,
        concat_axis=0,
        tiled=True,
    )
    arrived = received.reshape(peer_count, per_device, CAP, feature_slice)
    gate_part = jnp.einsum(
        "sjcd,jdf->sjcf", arrived, gate_weight, preferred_element_type=jnp.float32
    ).reshape(-1, hidden)
    up_part = jnp.einsum(
        "sjcd,jdf->sjcf", arrived, up_weight, preferred_element_type=jnp.float32
    ).reshape(-1, hidden)
    gate_share, up_share = (
        lax.psum_scatter(gate_part, "dp", scatter_dimension=0, tiled=True),
        lax.psum_scatter(up_part, "dp", scatter_dimension=0, tiled=True),
    )
    activated = lax.all_gather(
        (jax.nn.silu(gate_share) * up_share).astype(jnp.bfloat16), "dp", axis=0, tiled=True
    )
    expert_out = jnp.einsum(
        "sjcf,jfd->sjcd",
        activated.reshape(peer_count, per_device, CAP, hidden),
        down_weight,
        preferred_element_type=jnp.float32,
    ).astype(jnp.bfloat16)
    returned = lax.all_to_all(
        expert_out.reshape(peer_count, per_device * CAP, feature_slice),
        "expert",
        split_axis=0,
        concat_axis=0,
        tiled=True,
    )
    picked = (
        returned.reshape(slots_total, feature_slice)[target]
        .reshape(local_tokens, TOPK, feature_slice)
        .astype(jnp.float32)
    )
    levels = gate_levels.astype(jnp.float32)
    fractions = levels / jnp.sum(levels, axis=1, keepdims=True)
    mixed_out = jnp.sum(fractions[:, :, None] * picked, axis=1).astype(jnp.bfloat16)
    ratio_weight = jnp.minimum(jnp.exp(log_ratio), clip_ratio)
    weighted = (ratio_weight[:, None] * cotangent.astype(jnp.float32)).astype(jnp.bfloat16)
    weighted_wide = weighted.astype(jnp.float32)[:, None, :]
    gate_grad = lax.psum(jnp.sum(weighted_wide * picked, axis=2), "dp")
    pick_grad = (
        (fractions[:, :, None] * weighted_wide).astype(jnp.bfloat16).reshape(-1, feature_slice)
    )
    back_rows = lax.all_to_all(
        pack_rows(pick_grad), "expert", split_axis=0, concat_axis=0, tiled=True
    )
    back_rows = back_rows.reshape(peer_count, per_device, CAP, feature_slice)
    hidden_part = jnp.einsum(
        "sjcd,jfd->sjcf", back_rows, down_weight, preferred_element_type=jnp.float32
    ).reshape(-1, hidden)
    hidden_grad = lax.psum_scatter(hidden_part, "dp", scatter_dimension=0, tiled=True)
    sigmoid_gate = jax.nn.sigmoid(gate_share)
    gate_back = (
        hidden_grad * up_share * sigmoid_gate * (1.0 + gate_share * (1.0 - sigmoid_gate))
    ).astype(jnp.bfloat16)
    up_back = (hidden_grad * gate_share * sigmoid_gate).astype(jnp.bfloat16)
    gate_rows, up_rows = (
        lax.all_gather(gate_back, "dp", axis=0, tiled=True),
        lax.all_gather(up_back, "dp", axis=0, tiled=True),
    )
    gate_rows = gate_rows.reshape(peer_count, per_device, CAP, hidden)
    up_rows = up_rows.reshape(peer_count, per_device, CAP, hidden)
    input_part = jnp.einsum(
        "sjcf,jdf->sjcd", gate_rows, gate_weight, preferred_element_type=jnp.float32
    )
    input_part = (
        input_part
        + jnp.einsum("sjcf,jdf->sjcd", up_rows, up_weight, preferred_element_type=jnp.float32)
    ).astype(jnp.bfloat16)
    input_back = lax.all_to_all(
        input_part.reshape(peer_count, per_device * CAP, feature_slice),
        "expert",
        split_axis=0,
        concat_axis=0,
        tiled=True,
    )
    back_picked = input_back.reshape(slots_total, feature_slice)[target].reshape(
        local_tokens, TOPK, feature_slice
    )
    token_grad = jnp.sum(back_picked.astype(jnp.float32), axis=1).astype(jnp.bfloat16)
    return (mixed_out, token_grad, gate_grad)


def solution(mesh):
    in_specs = (
        P("expert", "dp"),
        P("expert", "dp", None),
        P("expert", "dp", None),
        P("expert", None, "dp"),
        P("expert", None),
        P("expert", None),
        P("expert"),
        P("expert", "dp"),
    )
    out_specs = (P("expert", "dp"), P("expert", "dp"), P("expert", None))
    return jax.shard_map(
        on_device, mesh=mesh, in_specs=in_specs, out_specs=out_specs, check_vma=False
    )
```

profile of v0, /device:TPU:8, one launch (start us, length us, event | category | flops | bytes accessed | tf_op | source)
XLA Modules:
  0.0 839.7 jit_solution(4727136546185766451)
XLA Ops:
  11.7 18.1 %reduce-window.6 = s32[64,16,128]{2,1,0:T(8,128)S(1)} reduce-window(s32[64,16,128]{2,1,0:T(8,128)S(1)} %fusion.58, s32[]{:T(128)} %constant.10.clone.1), window={size=1x1x128 pad=0_0x0_0x127_0}, to_apply=%region_1.2 | reduce-window | flops 16646144 | bytes 1048580 | tf_op jit(solution)/shard_map/reduce-window
  31.4 13.8 %scatter_custom_fusion.1 = bf16[2560,1024]{1,0:T(8,128)(2,1)} fusion(s32[2048]{0:T(1024)S(1)} %bitcast.109, f32[256,1024]{1,0:T(8,128)S(1)} %fusion.54, f32[2048]{0:T(1024)S(1)} %mul.96, bf16[]{:T(256)} %constant.8.clone.1), kind=kCustom, calls=%fused_computation.28 | custom fusion | flops 4194304 | bytes 6299650 | tf_op jit(solution)/shard_map/scatter | solution.py:32
  45.2 119.6 %all_to_all.20 = bf16[8,320,1024]{2,1,0:T(8,128)(2,1)} all-to-all(bf16[8,320,1024]{2,1,0:T(8,128)(2,1)} %bitcast.98), channel_id=1, replica_groups=mesh['dp'=4,'expert'=8] {'expert'}, dimensions={0} | all-to-all | bytes 10485760 | tf_op jit(solution)/shard_map/all_to_all | solution.py:84
  164.8 13.6 %fusion.28 = f32[8,8,40,768]{3,2,0,1:T(8,128)} fusion(bf16[8,768,1024]{2,1,0:T(8,128)(2,1)} %param.11, bf16[8,8,40,1024]{3,2,1,0:T(8,128)(2,1)} %bitcast.103), kind=kOutput, calls=%fused_computation.37 | convolution fusion | flops 4026531840 | bytes 25690112 | tf_op jit(solution)/shard_map/sjcd,jfd->sjcf/dot_general | solution.py:88
  178.3 7.1 copy.44
  185.7 13.0 %scatter_custom_fusion = bf16[2560,1024]{1,0:T(8,128)(2,1)} fusion(s32[2048]{0:T(1024)S(1)} %bitcast.110, bf16[]{:T(256)} %constant.8.clone.1, bf16[256,1024]{1,0:T(8,128)(2,1)S(1)} %copy-done), kind=kCustom, calls=%fused_computation.30 | custom fusion | bytes 5767170 | tf_op jit(solution)/shard_map/scatter | solution.py:32
  198.7 121.1 %all_to_all.21 = bf16[8,320,1024]{2,1,0:T(8,128)(2,1)} all-to-all(bf16[8,320,1024]{2,1,0:T(8,128)(2,1)} %bitcast.99), channel_id=1, replica_groups=mesh['dp'=4,'expert'=8] {'expert'}, dimensions={0} | all-to-all | bytes 10485760 | tf_op jit(solution)/shard_map/all_to_all | solution.py:35
  319.8 9.1 %fusion.38 = f32[8,8,40,768]{3,2,0,1:T(8,128)S(1)} fusion(bf16[8,1024,768]{2,1,0:T(8,128)(2,1)} %param.10, bf16[8,8,40,1024]{3,2,1,0:T(8,128)(2,1)} %bitcast.101), kind=kOutput, calls=%fused_computation.39 | convolution fusion | flops 4026531840 | bytes 25690112 | tf_op jit(solution)/shard_map/sjcd,jdf->sjcf/dot_general | solution.py:46
  332.8 9.2 %fusion.33 = f32[8,8,40,768]{3,2,0,1:T(8,128)S(1)} fusion(bf16[8,1024,768]{2,1,0:T(8,128)(2,1)} %param.9, bf16[8,8,40,1024]{3,2,1,0:T(8,128)(2,1)} %bitcast.102), kind=kOutput, calls=%fused_computation.38 | convolution fusion | flops 4026531840 | bytes 25690112 | tf_op jit(solution)/shard_map/sjcd,jdf->sjcf/dot_general | solution.py:43
  345.9 71.1 %reduce-scatter.6.cloned.1.call-done = f32[640,768]{1,0:T(8,128)} async-done(((f32[2560,768]{1,0:T(8,128)}), f32[640,768]{1,0:T(8,128)}) %reduce-scatter.6.cloned.1.call-update) | async-done | bytes 1966096 | tf_op jit(solution)/shard_map/reduce_scatter | solution.py:51
  417.0 86.4 %reduce-scatter.4.cloned.1.call-done = f32[640,768]{1,0:T(8,128)} async-done(((f32[2560,768]{1,0:T(8,128)}), f32[640,768]{1,0:T(8,128)}) %reduce-scatter.4.cloned.1.call-update) | async-done | bytes 1966096 | tf_op jit(solution)/shard_map/reduce_scatter | solution.py:50
  509.2 50.1 %all-gather.4.cloned.1.call-done = bf16[2560,768]{1,0:T(8,128)(2,1)} async-done(((bf16[640,768]{1,0:T(8,128)(2,1)}), bf16[2560,768]{1,0:T(8,128)(2,1)}) %all-gather.4.cloned.1.call-update) | async-done | bytes 3932176 | tf_op jit(solution)/shard_map/all_gather | solution.py:53
  559.3 10.0 %convert_bitcast_fusion = bf16[8,8,40,1024]{3,2,0,1:T(8,128)(2,1)S(1)} fusion(bf16[8,768,1024]{2,1,0:T(8,128)(2,1)} %param.11, bf16[8,8,40,768]{3,2,1,0:T(8,128)(2,1)} %bitcast.112), kind=kOutput, calls=%fused_computation.25 | convolution fusion | flops 4029153280 | bytes 21757952 | tf_op jit(solution)/shard_map/sjcf,jfd->sjcd/dot_general | solution.py:56
  578.1 33.5 %all-gather.8.cloned.1.call-done = bf16[2560,768]{1,0:T(8,128)(2,1)} async-done(((bf16[640,768]{1,0:T(8,128)(2,1)}), bf16[2560,768]{1,0:T(8,128)(2,1)}) %all-gather.8.cloned.1.call-update) | async-done | bytes 3932176 | tf_op jit(solution)/shard_map/all_gather | solution.py:99
  611.5 14.0 %fusion = f32[8,8,40,1024]{3,2,1,0:T(8,128)} fusion(bf16[8,1024,768]{2,1,0:T(8,128)(2,1)} %param.10, bf16[8,8,40,768]{3,2,1,0:T(8,128)(2,1)} %bitcast.100), kind=kOutput, calls=%fused_computation.4 | convolution fusion | flops 4026531840 | bytes 27000832 | tf_op jit(solution)/shard_map/sjcf,jdf->sjcd/dot_general | solution.py:108
  625.6 38.2 %all-gather.6.cloned.1.call-done = bf16[2560,768]{1,0:T(8,128)(2,1)} async-done(((bf16[640,768]{1,0:T(8,128)(2,1)}), bf16[2560,768]{1,0:T(8,128)(2,1)}) %all-gather.6.cloned.1.call-update) | async-done | bytes 3932176 | tf_op jit(solution)/shard_map/all_gather | solution.py:98
  663.8 12.6 %fusion.15 = bf16[8,8,40,1024]{3,2,0,1:T(8,128)(2,1)} fusion(f32[8,8,40,1024]{3,2,1,0:T(8,128)} %fusion, bf16[8,1024,768]{2,1,0:T(8,128)(2,1)} %param.9, bf16[8,8,40,768]{3,2,1,0:T(8,128)(2,1)} %bitcast.104), kind=kOutput, calls=%fused_computation.23 | convolution fusion | flops 4031774720 | bytes 32243712 | tf_op jit(solution)/shard_map/sjcf,jdf->sjcd/dot_general | solution.py:103
  682.0 8.5 %all-to-all-done.1 = bf16[8,320,1024]{2,1,0:T(8,128)(2,1)} async-done(((bf16[8,320,1024]{2,1,0:T(8,128)(2,1)}), bf16[8,320,1024]{2,1,0:T(8,128)(2,1)}, u32[]{:S(2)}, u32[]{:S(2)}) %all-to-all-start.1) | async-done | bytes 5242912 | tf_op jit(solution)/shard_map/all_to_all | solution.py:62
  690.5 8.4 %all-to-all-start.3 = ((bf16[8,320,1024]{2,1,0:T(8,128)(2,1)}), bf16[8,320,1024]{2,1,0:T(8,128)(2,1)}, u32[]{:S(2)}, u32[]{:S(2)}) async-start(bf16[8,320,1024]{2,1,0:T(8,128)(2,1)} %bitcast.97), calls=%async_computation.6 | async-start | bytes 10485760 | tf_op jit(solution)/shard_map/all_to_all | solution.py:110
  698.9 14.2 %gather_fusion = bf16[2048,1024]{1,0:T(8,128)(2,1)} fusion(bf16[2560,1024]{1,0:T(8,128)(2,1)} %bitcast.21, s32[2048]{0:T(1024)S(1)} %broadcast_clamp_fusion), kind=kCustom, calls=%fused_computation | custom fusion | bytes 8396800 | tf_op jit(solution)/shard_map/gather | solution.py:70
  719.1 17.6 %psum.7 = f32[256,8]{1,0:T(8,128)S(1)} all-reduce(f32[256,8]{1,0:T(8,128)S(1)} %get-tuple-element.6), channel_id=1, replica_groups=mesh['dp'=4,'expert'=8] {'dp'}, use_global_device_ids=true, to_apply=%region_12.13 | all-reduce | flops 2048 | bytes 16384 | tf_op jit(solution)/shard_map/psum | solution.py:80
  737.4 74.5 %all-to-all-done.3 = bf16[8,320,1024]{2,1,0:T(8,128)(2,1)} async-done(((bf16[8,320,1024]{2,1,0:T(8,128)(2,1)}), bf16[8,320,1024]{2,1,0:T(8,128)(2,1)}, u32[]{:S(2)}, u32[]{:S(2)}) %all-to-all-start.3) | async-done | bytes 5242912 | tf_op jit(solution)/shard_map/all_to_all | solution.py:110
  811.9 14.2 %gather_fusion.1 = bf16[2048,1024]{1,0:T(8,128)(2,1)} fusion(bf16[2560,1024]{1,0:T(8,128)(2,1)} %bitcast.35, s32[2048]{0:T(1024)S(1)} %broadcast_clamp_fusion), kind=kCustom, calls=%fused_computation.1 | custom fusion | bytes 8396800 | tf_op jit(solution)/shard_map/gather | solution.py:117
  826.1 6.3 bitcast_reduce_fusion
  (47 shorter events, 40.8 us)
Async XLA Ops:
  7.2 178.5 %copy-start = (bf16[256,1024]{1,0:T(8,128)(2,1)S(1)}, bf16[256,1024]{1,0:T(8,128)(2,1)}, u32[]{:S(2)}) copy-start(bf16[256,1024]{1,0:T(8,128)(2,1)} %param.8) | copy-start | bytes 1572868
  7.2 24.0 %copy-start.2 = (bf16[256,1024]{1,0:T(8,128)(2,1)S(1)}, bf16[256,1024]{1,0:T(8,128)(2,1)}, u32[]{:S(2)}) copy-start(bf16[256,1024]{1,0:T(8,128)(2,1)} %param.15) | copy-start | bytes 1572868
  7.2 338.7 %reduce-scatter.8.cloned.1.call-start = ((), (), s32[]{:S(2)}) async-start(), calls=%async_computation.10 | async-start | bytes 9830400 | tf_op jit(solution)/shard_map/reduce_scatter | solution.py:91
  185.5 231.5 %reduce-scatter.6.cloned.1.call-start = ((), (), s32[]{:S(2)}) async-start(), calls=%async_computation.8 | async-start | bytes 9830400 | tf_op jit(solution)/shard_map/reduce_scatter | solution.py:51
  332.8 170.6 %reduce-scatter.4.cloned.1.call-start = ((), (), s32[]{:S(2)}) async-start(), calls=%async_computation.7 | async-start | bytes 9830400 | tf_op jit(solution)/shard_map/reduce_scatter | solution.py:50
  345.8 213.5 %all-gather.4.cloned.1.call-start = ((), (), s32[]{:S(2)}) async-start(), calls=%async_computation.9 | async-start | bytes 4915200 | tf_op jit(solution)/shard_map/all_gather | solution.py:53
  508.6 102.9 %all-gather.8.cloned.1.call-start = ((), (), s32[]{:S(2)}) async-start(), calls=%async_computation.12 | async-start | bytes 4915200 | tf_op jit(solution)/shard_map/all_gather | solution.py:99
  572.3 118.1 %all-to-all-start.1 = ((bf16[8,320,1024]{2,1,0:T(8,128)(2,1)}), bf16[8,320,1024]{2,1,0:T(8,128)(2,1)}, u32[]{:S(2)}, u32[]{:S(2)}) async-start(bf16[8,320,1024]{2,1,0:T(8,128)(2,1)} %bitcast.96), calls=%async_computation.3 | async-start | bytes 10485760 | tf_op jit(solution)/shard_map/all_to_all | solution.py:62
  577.5 86.3 %all-gather.6.cloned.1.call-start = ((), (), s32[]{:S(2)}) async-start(), calls=%async_computation.11 | async-start | bytes 4915200 | tf_op jit(solution)/shard_map/all_gather | solution.py:98
  690.5 121.4 %all-to-all-start.3 = ((bf16[8,320,1024]{2,1,0:T(8,128)(2,1)}), bf16[8,320,1024]{2,1,0:T(8,128)(2,1)}, u32[]{:S(2)}, u32[]{:S(2)}) async-start(bf16[8,320,1024]{2,1,0:T(8,128)(2,1)} %bitcast.97), calls=%async_computation.6 | async-start | bytes 10485760 | tf_op jit(solution)/shard_map/all_to_all | solution.py:110
  811.9 20.5 %copy-start.1 = (bf16[256,1024]{1,0:T(8,128)(2,1)S(1)}, bf16[256,1024]{1,0:T(8,128)(2,1)}, u32[]{:S(2)}) copy-start(bf16[256,1024]{1,0:T(8,128)(2,1)} %param.8) | copy-start | bytes 1572868
Sparse Core Ops, SparseCore 0:
  185.6 83.9 reduce-scatter.7
  332.9 84.0 reduce-scatter.5
  419.9 83.3 reduce-scatter.3
  508.7 50.4 all-gather.3
  561.0 50.5 all-gather.7
  613.2 50.5 all-gather.5
where the time goes:
time: 853 us; the launch traced here: 840 us
  waiting for transfers between devices  363 us (43%)
  blocking collectives  258 us (30%)
  matrix products  68.5 us (8%)
  local copies, waits for them, and re-layouts  67.6 us (8%)
  other arithmetic  53.2 us (6%)
  between operations  14.7 us (2%)
  starting transfers between devices  14.2 us (2%)
    all_to_all x1, blocking collectives, on_device(): lax.all_to_all(pack_rows(jnp.repeat(tokens, TOPK, axis=0)), 'expert', spl...  121 us
    all_to_all x1, blocking collectives, on_device(): lax.all_to_all(pack_rows(pick_grad), 'expert', split_axis=0, concat_axis=...  120 us
    reduce_scatter x1, waiting for transfers between devices, on_device(): lax.psum_scatter(gate_part, 'dp', scatter_dimension=0, tiled=True)  86.4 us
    all_to_all x1, waiting for transfers between devices, on_device(): lax.all_to_all(input_part.reshape(peer_count, per_device * CAP, feature_s...  74.5 us
    reduce_scatter x1, waiting for transfers between devices, on_device(): lax.psum_scatter(up_part, 'dp', scatter_dimension=0, tiled=True)  71.1 us
    all_gather x1, waiting for transfers between devices, on_device(): lax.all_gather((jax.nn.silu(gate_share) * up_share).astype(jnp.bfloat16),...  50.1 us
    all_gather x1, waiting for transfers between devices, on_device(): lax.all_gather(gate_back, 'dp', axis=0, tiled=True)  38.2 us
    all_gather x1, waiting for transfers between devices, on_device(): lax.all_gather(up_back, 'dp', axis=0, tiled=True)  33.5 us
  transfers between devices with their start and end apart: 8, of which 7 were waited for; matrix products, arithmetic and copies ran while one was open for 13% of the time, Pallas kernels for 0%

commit v1 on v0

--- a/solution.py
+++ b/solution.py
@@ -1,14 +1,324 @@
+import functools
 import jax
 import jax.numpy as jnp
 from jax import lax
+from jax.experimental import pallas as pl
+from jax.experimental.pallas import tpu as pltpu
 from jax.sharding import PartitionSpec as P
 
 EXPERTS = 64
 TOPK = 8
 CAP = 40
-
+VMEM_BYTES = 50 * 1024 * 1024
 
 clip_ratio = 2.0
+
+
+def dot_nn(a, b):
+    return lax.dot_general(a, b, (((1,), (0,)), ((), ())), preferred_element_type=jnp.float32)
+
+
+def dot_nt(a, b):
+    return lax.dot_general(a, b, (((1,), (1,)), ((), ())), preferred_element_type=jnp.float32)
+
+
+def dot_tn(a, b):
+    return lax.dot_general(a, b, (((0,), (0,)), ((), ())), preferred_element_type=jnp.float32)
+
+
+def one_hot(slots_ref, rows):
+    slots = slots_ref[0]
+    return slots == lax.broadcasted_iota(jnp.int32, (rows, slots.shape[-1]), 0)
+
+
+def whole(shape):
+    return pl.BlockSpec(shape, lambda g, me: (0,) * len(shape))
+
+
+def expert_block(shape, halves):
+    count = len(halves)
+    return pl.BlockSpec(
+        (1,) + shape,
+        lambda g, me: (2 * ((g // count) ^ me[0]) + (halves[0] + g % count), 0, 0),
+    )
+
+
+def partial_kernel(count, me, same, other, slots, w_gate, w_up, w_down,
+                   self_a, self_b, send_a, keep_a, send_b, keep_b):
+    step = pl.program_id(0)
+    part, half = step // count, step % count
+    tokens, width = same.shape
+    rows = self_a.shape[1]
+    hidden = w_gate.shape[2]
+    pick = jnp.where(one_hot(slots, rows), 1.0, 0.0).astype(jnp.bfloat16)
+    taken = dot_nn(pick[:, :tokens], same[...]) + dot_nn(pick[:, tokens:], other[...])
+    taken = taken.astype(jnp.bfloat16)
+    features = width // 2
+    gate = dot_nn(taken[:, :features], w_gate[0]).astype(jnp.bfloat16)
+    up = dot_nn(taken[:, :features], w_up[0]).astype(jnp.bfloat16)
+    back = dot_nt(taken[:, features:], w_down[0]).astype(jnp.bfloat16)
+
+    def put_a(ref, *where):
+        ref[(*where, slice(None), pl.ds(0, hidden))] = gate
+        ref[(*where, slice(None), pl.ds(hidden, hidden // 2))] = up[:, : hidden // 2]
+
+    def put_b(ref, *where):
+        ref[(*where, slice(None), pl.ds(0, hidden // 2))] = up[:, hidden // 2 :]
+        ref[(*where, slice(None), pl.ds(hidden // 2, hidden))] = back
+
+    @pl.when(part == 0)
+    def _():
+        put_a(self_a, half)
+        put_b(self_b, half)
+
+    @pl.when(part == 1)
+    def _():
+        put_a(send_a, 0, half)
+        put_b(keep_b, half)
+
+    @pl.when(part == 2)
+    def _():
+        put_a(keep_a, half)
+        put_b(send_b, 0, half)
+
+    @pl.when(part == 3)
+    def _():
+        put_a(send_a, 1, half)
+        put_b(send_b, 1, half)
+
+
+def partial_sums(me, same, other, slots, w_gate, w_up, w_down, halves):
+    count = len(halves)
+    features, hidden = w_gate.shape[1:]
+    rows, cols = 2 * CAP, 3 * hidden // 2
+    one = jax.ShapeDtypeStruct((count, rows, cols), jnp.bfloat16)
+    two = jax.ShapeDtypeStruct((2, count, rows, cols), jnp.bfloat16)
+    outs = (one, one, two, one, two, one)
+    steps = 4 * count
+    return pl.pallas_call(
+        functools.partial(partial_kernel, count),
+        grid_spec=pltpu.PrefetchScalarGridSpec(
+            num_scalar_prefetch=1,
+            grid=(steps,),
+            in_specs=[
+                whole(same.shape),
+                whole(other.shape),
+                expert_block(slots.shape[1:], halves),
+                expert_block((features, hidden), halves),
+                expert_block((features, hidden), halves),
+                expert_block((hidden, features), halves),
+            ],
+            out_specs=[whole(o.shape) for o in outs],
+        ),
+        out_shape=outs,
+        compiler_params=pltpu.CompilerParams(vmem_limit_bytes=VMEM_BYTES),
+        cost_estimate=pl.CostEstimate(
+            flops=steps * rows * 10 * features * hidden,
+            bytes_accessed=steps * features * hidden * 6,
+            transcendentals=0,
+        ),
+    )(me, same, other, slots, w_gate, w_up, w_down)
+
+
+def middle_kernel(self_a, self_b, first_a, first_b, last_a, last_b, slots, share,
+                  out_a, out_b, grad):
+    count, rows, cols = self_a.shape
+    hidden = 2 * cols // 3
+    half = hidden // 2
+    for h in range(count):
+        def total(own, first, last, lo, size):
+            cut = pl.ds(lo, size)
+            return (
+                own[h, :, cut].astype(jnp.float32)
+                + first[0, h, :, cut].astype(jnp.float32)
+                + last[h, :, cut].astype(jnp.float32)
+            )
+        hot = one_hot(slots.at[pl.ds(h, 1)], rows)
+        fraction = jnp.sum(jnp.where(hot, share[h], 0.0), axis=1, keepdims=True)
+        grads = jnp.zeros((rows, 1), jnp.float32)
+        for side in range(2):
+            lo = side * half
+            gate = total(self_a, first_a, last_a, lo, half)
+            if side == 0:
+                up = total(self_a, first_a, last_a, hidden, half)
+            else:
+                up = total(self_b, first_b, last_b, 0, half)
+            back = total(self_b, first_b, last_b, half + lo, half)
+            sig = 1.0 / (1.0 + jnp.exp(-gate))
+            silu = gate * sig
+            act = silu * up
+            grads = grads + jnp.sum(act * back, axis=1, keepdims=True)
+            hidden_grad = back * fraction
+            act_out = (act * fraction).astype(jnp.bfloat16)
+            gate_out = (hidden_grad * up * sig * (1.0 + gate * (1.0 - sig))).astype(jnp.bfloat16)
+            up_out = (hidden_grad * silu).astype(jnp.bfloat16)
+            out_a[h, :, pl.ds(lo, half)] = act_out
+            if side == 0:
+                out_a[h, :, pl.ds(hidden, half)] = gate_out
+            else:
+                out_b[h, :, pl.ds(0, half)] = gate_out
+            out_b[h, :, pl.ds(half + lo, half)] = up_out
+        grad[h] = jnp.sum(jnp.where(hot, grads, 0.0), axis=0, keepdims=True)
+
+
+def middle(self_a, self_b, first_a, first_b, last_a, last_b, slots, share):
+    outs = (
+        jax.ShapeDtypeStruct(self_a.shape, jnp.bfloat16),
+        jax.ShapeDtypeStruct(self_b.shape, jnp.bfloat16),
+        jax.ShapeDtypeStruct(share.shape, jnp.float32),
+    )
+    return pl.pallas_call(
+        middle_kernel,
+        out_shape=outs,
+        in_specs=[pl.BlockSpec(memory_space=pltpu.VMEM)] * 8,
+        out_specs=[pl.BlockSpec(memory_space=pltpu.VMEM)] * 3,
+        compiler_params=pltpu.CompilerParams(vmem_limit_bytes=VMEM_BYTES),
+        cost_estimate=pl.CostEstimate(
+            flops=40 * self_a.size, bytes_accessed=14 * self_a.size, transcendentals=self_a.size
+        ),
+    )(self_a, self_b, first_a, first_b, last_a, last_b, slots, share)
+
+
+def combine_kernel(count, me, *refs):
+    lefts, rights = refs[0:4], refs[4:8]
+    slots, w_gate, w_up, w_down, same, other, rows_in, hots, outs = refs[8:]
+    step = pl.program_id(0)
+    part, half = step // count, step % count
+    rows, cols = rows_in.shape[0], lefts[0].shape[2]
+    hidden = w_gate.shape[2]
+    features = w_gate.shape[1]
+    for v in range(4):
+        @pl.when(part == v)
+        def _():
+            rows_in[:, pl.ds(0, cols)] = lefts[v][half]
+            rows_in[:, pl.ds(cols, cols)] = rights[v][half]
+    at = pl.ds(pl.multiple_of(step * rows, 16), rows)
+    outs[at, pl.ds(0, features)] = dot_nn(rows_in[:, pl.ds(0, hidden)], w_down[0]).astype(jnp.bfloat16)
+    outs[at, pl.ds(features, features)] = (
+        dot_nt(rows_in[:, pl.ds(hidden, hidden)], w_gate[0])
+        + dot_nt(rows_in[:, pl.ds(2 * hidden, hidden)], w_up[0])
+    ).astype(jnp.bfloat16)
+    hots[at, :] = jnp.where(one_hot(slots, rows), 1.0, 0.0).astype(jnp.bfloat16)
+
+    @pl.when(step == pl.num_programs(0) - 1)
+    def _():
+        tokens, width = same.shape
+        for ref, lo in ((same, 0), (other, tokens)):
+            ref[...] = dot_tn(hots[:, pl.ds(lo, tokens)], outs[...]).astype(jnp.bfloat16)
+
+
+def combine(me, lefts, rights, slots, w_gate, w_up, w_down, halves):
+    count = len(halves)
+    features, hidden = w_gate.shape[1:]
+    rows = 2 * CAP
+    tokens = slots.shape[2] // 2
+    steps = 4 * count
+    out = jax.ShapeDtypeStruct((tokens, 2 * features), jnp.bfloat16)
+    return pl.pallas_call(
+        functools.partial(combine_kernel, count),
+        grid_spec=pltpu.PrefetchScalarGridSpec(
+            num_scalar_prefetch=1,
+            grid=(steps,),
+            in_specs=[whole(a.shape) for a in (*lefts, *rights)]
+            + [
+                expert_block(slots.shape[1:], halves),
+                expert_block((features, hidden), halves),
+                expert_block((features, hidden), halves),
+                expert_block((hidden, features), halves),
+            ],
+            out_specs=[whole(out.shape)] * 2,
+            scratch_shapes=[
+                pltpu.VMEM((rows, 3 * hidden), jnp.bfloat16),
+                pltpu.VMEM((steps * rows, 2 * tokens), jnp.bfloat16),
+                pltpu.VMEM((steps * rows, 2 * features), jnp.bfloat16),
+            ],
+        ),
+        out_shape=(out, out),
+        compiler_params=pltpu.CompilerParams(vmem_limit_bytes=VMEM_BYTES),
+        cost_estimate=pl.CostEstimate(
+            flops=steps * rows * 10 * features * hidden,
+            bytes_accessed=steps * features * hidden * 6,
+            transcendentals=0,
+        ),
+    )(me, *lefts, *rights, slots, w_gate, w_up, w_down)
+
+
+def swap(value, axis, bits):
+    count = lax.axis_size(axis)
+    return lax.ppermute(value, axis, [(n, n ^ bits) for n in range(count)])
+
+
+def grouped(tokens, gate_weight, up_weight, down_weight, routes, gate_levels, log_ratio, cotangent):
+    block, features = tokens.shape
+    per_device = gate_weight.shape[0]
+    peers = lax.axis_size("expert")
+    chips = peers // 2
+    mine = lax.axis_index("expert")
+    member = lax.axis_index("dp")
+    me = member.astype(jnp.int32).reshape(1)
+
+    ratio_weight = jnp.minimum(jnp.exp(log_ratio), clip_ratio)
+    weighted = (ratio_weight[:, None] * cotangent.astype(jnp.float32)).astype(jnp.bfloat16)
+    payload = jnp.concatenate([tokens, weighted], axis=1)
+    sames = [payload] + [swap(payload, "expert", 2 * o) for o in range(1, chips)]
+    others = [swap(p, "expert", 1) for p in sames]
+
+    picks = lax.all_gather(jnp.stack([routes, gate_levels]), "expert")
+    order = jnp.arange(peers, dtype=jnp.int32) ^ mine
+    picks = picks[order]
+    levels = picks[:, 1].astype(jnp.float32)
+    fractions = levels / jnp.sum(levels, axis=2, keepdims=True)
+    local = mine * per_device + jnp.arange(per_device, dtype=jnp.int32)
+    named = picks[:, 0][None] == local[:, None, None, None]
+    share = jnp.sum(jnp.where(named, fractions[None], 0.0), axis=3)
+    chosen = jnp.any(named, axis=3)
+    tri = (jnp.arange(block)[:, None] < jnp.arange(block)[None, :]).astype(jnp.bfloat16)
+    place = jnp.einsum(
+        "jst,tu->jsu", chosen.astype(jnp.bfloat16), tri, preferred_element_type=jnp.float32
+    ).astype(jnp.int32)
+    place = place + (jnp.arange(peers, dtype=jnp.int32) % 2 * CAP)[None, :, None]
+    slots = jnp.where(chosen, place, -1).reshape(per_device, chips, 1, 2 * block)
+    share = share.reshape(per_device, chips, 1, 2 * block)
+
+    weights = (gate_weight, up_weight, down_weight)
+    chunks = [(0, (0,))] + [(o, (0, 1)) for o in range(1, chips)] + [(0, (1,))]
+    partials, grads, totals = [], {}, []
+    for o, halves in chunks:
+        slot = slots[:, o]
+        self_a, self_b, send_a, keep_a, send_b, keep_b = partial_sums(
+            me, sames[o], others[o], slot, *weights, halves
+        )
+        first_a, first_b = swap(send_a, "dp", 1), swap(send_b, "dp", 2)
+        last_a = swap(keep_a + first_a[1], "dp", 2)
+        last_b = swap(keep_b + first_b[1], "dp", 1)
+        first = 2 * member + halves[0]
+        own_slot = lax.dynamic_slice_in_dim(slot, first, len(halves), 0)
+        own_share = lax.dynamic_slice_in_dim(share[:, o], first, len(halves), 0)
+        a, b, grad = middle(
+            self_a, self_b, first_a, first_b, last_a, last_b, own_slot, own_share
+        )
+        for n, h in enumerate(halves):
+            grads[o, h] = grad[n]
+        a_x, a_y, b_x, b_y = swap(a, "dp", 1), swap(a, "dp", 2), swap(b, "dp", 1), swap(b, "dp", 2)
+        a_d, b_d = swap(a_y, "dp", 1), swap(b_x, "dp", 2)
+        same, other = combine(
+            me, (a, a_x, a_y, a_d), (b, b_x, b_y, b_d), slot, *weights, halves
+        )
+        both = same.astype(jnp.float32) + swap(other, "expert", 1).astype(jnp.float32)
+        if o:
+            both = swap(both.astype(jnp.bfloat16), "expert", 2 * o)
+        totals.append(both)
+    total = sum(t.astype(jnp.float32) for t in totals).astype(jnp.bfloat16)
+
+    grad_all = jnp.stack([jnp.stack([grads[o, h] for o in range(chips)]) for h in range(2)])
+    grad_all = lax.all_gather(grad_all.reshape(2, peers, block), ("expert", "dp"))
+    grad_all = grad_all.reshape(peers, per_device, peers, block)
+    place_of = (jnp.arange(peers)[:, None] ^ mine) == jnp.arange(peers)[None, :]
+    to_me = jnp.sum(jnp.where(place_of[:, None, :, None], grad_all, 0.0), axis=2)
+    to_me = to_me.reshape(peers * per_device, block)
+    hit = routes[:, :, None] == jnp.arange(EXPERTS, dtype=jnp.int32)
+    gate_grad = jnp.sum(jnp.where(hit, to_me.T[:, None, :], 0.0), axis=2)
+    return total[:, :features], total[:, features:], gate_grad
 
 
 def on_device(
@@ -133,6 +443,8 @@
         P("expert", "dp"),
     )
     out_specs = (P("expert", "dp"), P("expert", "dp"), P("expert", None))
+    fits = mesh.shape["dp"] == 4 and mesh.shape["expert"] == 8
     return jax.shard_map(
-        on_device, mesh=mesh, in_specs=in_specs, out_specs=out_specs, check_vma=False
-    )
+        grouped if fits else on_device,
+        mesh=mesh, in_specs=in_specs, out_specs=out_specs, check_vma=False,
+    )

time: 853 us -> 560 us (0.66)
  waiting for transfers between devices: 363 us -> 74.6 us
  Pallas kernels: 0 us -> 162 us
  matrix products: 68.5 us -> 0.16 us
  local copies, waits for them, and re-layouts: 67.6 us -> 15.5 us
  starting transfers between devices: 14.2 us -> 62.2 us
  other arithmetic: 53.2 us -> 13.7 us
  blocking collectives: 258 us -> 225 us
  between operations: 14.7 us -> 1.24 us
    all_to_all x2 -> x0, blocking collectives: 241 us -> none  [the longest x1 121 us: on_device(): lax.all_to_all(pack_rows(jnp.repeat(tokens, TOPK, axis=0)), 'expert', spl...]
    all_gather x0 -> x2, blocking collectives: none -> 225 us  [the longest x1 130 us: grouped(): lax.all_gather(grad_all.reshape(2, peers, block), ('expert', 'dp'))]
    pallas_call x0 -> x15, Pallas kernels: none -> 162 us  [the longest x5 82.4 us: combine(): pl.pallas_call(functools.partial(combine_kernel, count), grid_spec=pltpu....]
    reduce_scatter x3 -> x0, waiting for transfers between devices: 157 us -> none  [the longest x1 86.4 us: on_device(): lax.psum_scatter(gate_part, 'dp', scatter_dimension=0, tiled=True)]
    all_gather x3 -> x0, waiting for transfers between devices: 122 us -> none  [the longest x1 50.1 us: on_device(): lax.all_gather((jax.nn.silu(gate_share) * up_share).astype(jnp.bfloat16),...]
    all_to_all x2 -> x0, waiting for transfers between devices: 83 us -> none  [the longest x1 74.5 us: on_device(): lax.all_to_all(input_part.reshape(peer_count, per_device * CAP, feature_s...]
    ppermute x0 -> x65, waiting for transfers between devices: none -> 74.6 us  [swap(): return lax.ppermute(value, axis, [(n, n ^ bits) for n in range(count)])]
    dot_general x6 -> x1, matrix products: 68.5 us -> 0.16 us  [grouped(): jnp.einsum('jst,tu->jsu', chosen.astype(jnp.bfloat16), tri, preferred_ele...]
  transfers between devices with their start and end apart: 8 -> 65, of which waited for: 7 -> 15; matrix products, arithmetic and copies ran while one was open for 13% -> 2% of each run, Pallas kernels for 0% -> 29%
where the time goes in v1:
time: 560 us; the launch traced here: 554 us
  blocking collectives  225 us (40%)
  Pallas kernels  162 us (29%)
  waiting for transfers between devices  74.6 us (13%)
  starting transfers between devices  62.2 us (11%)
  local copies, waits for them, and re-layouts  15.5 us (3%)
  other arithmetic  13.7 us (2%)
    all_gather x1, blocking collectives, grouped(): lax.all_gather(grad_all.reshape(2, peers, block), ('expert', 'dp'))  130 us
    all_gather x1, blocking collectives, grouped(): picks = lax.all_gather(jnp.stack([routes, gate_levels]), 'expert')  94.8 us
    pallas_call x5, Pallas kernels, combine(): pl.pallas_call(functools.partial(combine_kernel, count), grid_spec=pltpu....  82.4 us
    pallas_call x5, Pallas kernels, partial_sums(): pl.pallas_call(functools.partial(partial_kernel, count), grid_spec=pltpu....  77 us
    ppermute x65, waiting for transfers between devices, swap(): return lax.ppermute(value, axis, [(n, n ^ bits) for n in range(count)])  74.6 us
    ppermute x65, starting transfers between devices, swap(): return lax.ppermute(value, axis, [(n, n ^ bits) for n in range(count)])  62.2 us
  transfers between devices with their start and end apart: 65, of which 15 were waited for; matrix products, arithmetic and copies ran while one was open for 2% of the time, Pallas kernels for 29%

profile of v1, /device:TPU:8, one launch (start us, length us, event | category | flops | bytes accessed | tf_op | source)
XLA Modules:
  0.0 554.4 jit_solution(1889348609940334835)
XLA Ops:
  7.8 94.8 %all-gather = s32[16,256,8]{1,2,0:T(8,128)S(1)} all-gather(s32[2,256,8]{1,2,0:T(8,128)S(1)} %pad_add_fusion), channel_id=2, replica_groups=mesh['dp'=4,'expert'=8] {'expert'}, dimensions={0}, use_global_device_ids=true | all-gather | bytes 147456 | tf_op jit(solution)/shard_map/all_gather | solution.py:266
  106.0 10.3 %shard_map.115 = (bf16[1,80,1152]{2,1,0:T(8,128)(2,1)S(1)}, bf16[1,80,1152]{2,1,0:T(8,128)(2,1)S(1)}, bf16[2,1,80,1152]{3,2,1,0:T(8,128)(2,1)}, bf16[1,80,1152]{...) custom-call(s32[1]{0:T(128)} %bitcast.me, ...), custom_call_target="tpu_custom_call" | custom-call | flops 2516582400 | bytes 18874368 | tf_op jit(solution)/shard_map/pallas_call | solution.py:98
  124.2 9.6 %shard_map.103 = (bf16[1,80,1152]{2,1,0:T(8,128)(2,1)S(1)}, bf16[1,80,1152]{2,1,0:T(8,128)(2,1)S(1)}, bf16[2,1,80,1152]{3,2,1,0:T(8,128)(2,1)S(1)}, bf16[1,80,11...) custom-call(s32[1]{0:T(128)} %bitcast.me, ...), custom_call_target="tpu_custom_call" | custom-call | flops 2516582400 | bytes 18874368 | tf_op jit(solution)/shard_map/pallas_call | solution.py:98
  135.9 8.3 %collective-permute-done.1.first_a = bf16[2,1,80,1152]{3,2,1,0:T(8,128)(2,1)S(1)} collective-permute-done((bf16[2,1,80,1152]{3,2,1,0:T(8,128)(2,1)S(1)}, bf16[2,1,80,1152]{3,2,1,0:T(8,128)(2,1)S(1)}, u32[]{:S(2)}, u32[]{:S(2)}) %collective-permute-start.1) | collective-permute-done | bytes 368672 | tf_op jit(solution)/shard_map/ppermute | solution.py:248
  147.5 4.1 collective-permute-done.56.last_a
  155.1 2.1 collective-permute-done.4.last_b
  160.3 18.8 %shard_map.112 = (bf16[2,80,1152]{2,1,0:T(8,128)(2,1)S(1)}, bf16[2,80,1152]{2,1,0:T(8,128)(2,1)S(1)}, bf16[2,2,80,1152]{3,2,1,0:T(8,128)(2,1)S(1)}, bf16[2,80,11...) custom-call(s32[1]{0:T(128)} %bitcast.me, ...), custom_call_target="tpu_custom_call" | custom-call | flops 5033164800 | bytes 37748736 | tf_op jit(solution)/shard_map/pallas_call | solution.py:98
  180.1 18.8 %shard_map.109 = (bf16[2,80,1152]{2,1,0:T(8,128)(2,1)S(1)}, bf16[2,80,1152]{2,1,0:T(8,128)(2,1)S(1)}, bf16[2,2,80,1152]{3,2,1,0:T(8,128)(2,1)S(1)}, bf16[2,80,11...) custom-call(s32[1]{0:T(128)} %bitcast.me, ...), custom_call_target="tpu_custom_call" | custom-call | flops 5033164800 | bytes 37748736 | tf_op jit(solution)/shard_map/pallas_call | solution.py:98
  200.1 19.4 %shard_map.106 = (bf16[2,80,1152]{2,1,0:T(8,128)(2,1)S(1)}, bf16[2,80,1152]{2,1,0:T(8,128)(2,1)S(1)}, bf16[2,2,80,1152]{3,2,1,0:T(8,128)(2,1)}, bf16[2,80,1152]{...) custom-call(s32[1]{0:T(128)} %bitcast.me, ...), custom_call_target="tpu_custom_call" | custom-call | flops 5033164800 | bytes 37748736 | tf_op jit(solution)/shard_map/pallas_call | solution.py:98
  223.8 15.1 %collective-permute-done.28.first_a = bf16[2,2,80,1152]{3,2,1,0:T(8,128)(2,1)S(1)} collective-permute-done((bf16[2,2,80,1152]{3,2,1,0:T(8,128)(2,1)S(1)}, bf16[2,2,80,1152]{3,2,1,0:T(8,128)(2,1)S(1)}, u32[]{:S(2)}, u32[]{:S(2)}) %collective-permute-start.28) | collective-permute-done | bytes 737312 | tf_op jit(solution)/shard_map/ppermute | solution.py:248
  246.8 15.8 %collective-permute-done.5.refs_1_ = bf16[1,80,1152]{2,1,0:T(8,128)(2,1)S(1)} collective-permute-done((bf16[1,80,1152]{2,1,0:T(8,128)(2,1)S(1)}, bf16[1,80,1152]{2,1,0:T(8,128)(2,1)S(1)}, u32[]{:S(2)}, u32[]{:S(2)}) %collective-permute-start.5) | collective-permute-done | bytes 184352 | tf_op jit(solution)/shard_map/ppermute | solution.py:248
  275.0 3.0 collective-permute-done.44.last_a
  285.8 4.0 collective-permute-done.30.last_a
  291.9 5.8 %collective-permute-done.16.last_a = bf16[2,80,1152]{2,1,0:T(8,128)(2,1)S(1)} collective-permute-done((bf16[2,80,1152]{2,1,0:T(8,128)(2,1)}, bf16[2,80,1152]{2,1,0:T(8,128)(2,1)S(1)}, u32[]{:S(2)}, u32[]{:S(2)}) %collective-permute-start.16) | collective-permute-done | bytes 368672 | tf_op jit(solution)/shard_map/ppermute | solution.py:248
  302.0 3.6 collective-permute-done.47.refs_2_
  307.8 5.7 %collective-permute-done.50.refs_6_ = bf16[2,80,1152]{2,1,0:T(8,128)(2,1)S(1)} collective-permute-done((bf16[2,80,1152]{2,1,0:T(8,128)(2,1)S(1)}, bf16[2,80,1152]{2,1,0:T(8,128)(2,1)S(1)}, u32[]{:S(2)}, u32[]{:S(2)}) %collective-permute-start.50) | collective-permute-done | bytes 368672 | tf_op jit(solution)/shard_map/ppermute | solution.py:248
  316.6 11.4 %shard_map.105 = (bf16[256,2048]{1,0:T(8,128)(2,1)S(1)}, bf16[256,2048]{1,0:T(8,128)(2,1)}) custom-call(s32[1]{0:T(128)} %bitcast.me, bf16[1,80,1152]{2,1,0:T(8,128)(2,1)S(1)} %get-tuple-element.64.refs_0_, bf16[1,80,1152]{2,1,0:T(8,128)(2,1)S(1)} %collective-permute-done.5.refs_1_, bf16[1,80,1152]{2,1,0:T(8,128)(2,1)S(1)} %collective-permute-done.6.refs_2_, ...), custom_call_target="tpu_custom_call" | custom-call | flops 2516582400 | bytes 18874368 | tf_op jit(solution)/shard_map/pallas_call | solution.py:217
  328.0 11.5 %shard_map.117 = (bf16[256,2048]{1,0:T(8,128)(2,1)S(1)}, bf16[256,2048]{1,0:T(8,128)(2,1)}) custom-call(s32[1]{0:T(128)} %bitcast.me, bf16[1,80,1152]{2,1,0:T(8,128)(2,1)S(1)} %get-tuple-element.104.refs_0_, bf16[1,80,1152]{2,1,0:T(8,128)(2,1)S(1)} %collective-permute-done.58.refs_1_, bf16[1,80,1152]{2,1,0:T(8,128)(2,1)S(1)} %collective-permute-done.59.refs_2_, ...), custom_call_target="tpu_custom_call" | custom-call | flops 2516582400 | bytes 18874368 | tf_op jit(solution)/shard_map/pallas_call | solution.py:217
  345.4 19.8 %shard_map.114 = (bf16[256,2048]{1,0:T(8,128)(2,1)S(1)}, bf16[256,2048]{1,0:T(8,128)(2,1)}) custom-call(s32[1]{0:T(128)} %bitcast.me, bf16[2,80,1152]{2,1,0:T(8,128)(2,1)S(1)} %get-tuple-element.94.refs_0_, bf16[2,80,1152]{2,1,0:T(8,128)(2,1)S(1)} %collective-permute-done.46.refs_1_, bf16[2,80,1152]{2,1,0:T(8,128)(2,1)S(1)} %collective-permute-done.47.refs_2_, ...), custom_call_target="tpu_custom_call" | custom-call | flops 5033164800 | bytes 37748736 | tf_op jit(solution)/shard_map/pallas_call | solution.py:217
  369.2 20.0 %shard_map.111 = (bf16[256,2048]{1,0:T(8,128)(2,1)S(1)}, bf16[256,2048]{1,0:T(8,128)(2,1)}) custom-call(s32[1]{0:T(128)} %bitcast.me, bf16[2,80,1152]{2,1,0:T(8,128)(2,1)S(1)} %get-tuple-element.84.refs_0_, bf16[2,80,1152]{2,1,0:T(8,128)(2,1)S(1)} %collective-permute-done.32.refs_1_, bf16[2,80,1152]{2,1,0:T(8,128)(2,1)S(1)} %collective-permute-done.33.refs_2_, ...), custom_call_target="tpu_custom_call" | custom-call | flops 5033164800 | bytes 37748736 | tf_op jit(solution)/shard_map/pallas_call | solution.py:217
  390.0 19.8 %shard_map.108 = (bf16[256,2048]{1,0:T(8,128)(2,1)S(1)}, bf16[256,2048]{1,0:T(8,128)(2,1)}) custom-call(s32[1]{0:T(128)} %bitcast.me, bf16[2,80,1152]{2,1,0:T(8,128)(2,1)S(1)} %get-tuple-element.74.refs_0_, bf16[2,80,1152]{2,1,0:T(8,128)(2,1)S(1)} %collective-permute-done.18.refs_1_, bf16[2,80,1152]{2,1,0:T(8,128)(2,1)S(1)} %collective-permute-done.19.refs_2_, ...), custom_call_target="tpu_custom_call" | custom-call | flops 5033164800 | bytes 37748736 | tf_op jit(solution)/shard_map/pallas_call | solution.py:217
  413.5 3.2 collective-permute-start.39
  418.3 130.1 %all_gather.11 = f32[32,2,8,256]{3,2,1,0:T(8,128)S(1)} all-gather(f32[1,2,8,256]{3,2,1,0:T(8,128)S(1)} %pad_maximum_fusion.1), channel_id=1, replica_groups=mesh['dp'=4,'expert'=8] {'expert','dp'}, dimensions={0}, use_global_device_ids=true | all-gather | bytes 540672 | tf_op jit(solution)/shard_map/all_gather | solution.py:314
  549.4 3.9 add_convert_fusion
  (254 shorter events, 94.2 us)
Async XLA Ops:
  3.7 131.0 %collective-permute-start.40 = (bf16[256,2048]{1,0:T(8,128)(2,1)S(1)}, bf16[256,2048]{1,0:T(8,128)(2,1)}, u32[]{:S(2)}, u32[]{:S(2)}) collective-permute-start(bf16[256,2048]{1,0:T(8,128)(2,1)S(1)} %pad_maximum_fusion.same), channel_id=1, source_target_pairs={{0,6},{1,7},{2,4},{3,5},{4,2},{5,3},{6,0},{7,1},{8,14},{9,15},{10,... | collective-permute-start | bytes 3145736 | tf_op jit(solution)/shard_map/ppermute | solution.py:248
  5.3 130.0 %collective-permute-start.26 = (bf16[256,2048]{1,0:T(8,128)(2,1)S(1)}, bf16[256,2048]{1,0:T(8,128)(2,1)}, u32[]{:S(2)}, u32[]{:S(2)}) collective-permute-start(bf16[256,2048]{1,0:T(8,128)(2,1)S(1)} %pad_maximum_fusion.same), channel_id=1, source_target_pairs={{0,4},{1,5},{2,6},{3,7},{4,0},{5,1},{6,2},{7,3},{8,12},{9,13},{10,... | collective-permute-start | bytes 3145736 | tf_op jit(solution)/shard_map/ppermute | solution.py:248
  6.4 139.7 %collective-permute-start.12 = (bf16[256,2048]{1,0:T(8,128)(2,1)S(1)}, bf16[256,2048]{1,0:T(8,128)(2,1)S(1)}, u32[]{:S(2)}, u32[]{:S(2)}) collective-permute-start(bf16[256,2048]{1,0:T(8,128)(2,1)S(1)} %pad_maximum_fusion.same), channel_id=1, source_target_pairs={{0,2},{1,3},{2,0},{3,1},{4,6},{5,7},{6,4},{7,5},{8,10},{9,11},{10,... | collective-permute-start | bytes 3145736 | tf_op jit(solution)/shard_map/ppermute | solution.py:248
  7.8 98.1 %collective-permute-start = (bf16[256,2048]{1,0:T(8,128)(2,1)S(1)}, bf16[256,2048]{1,0:T(8,128)(2,1)S(1)}, u32[]{:S(2)}, u32[]{:S(2)}) collective-permute-start(bf16[256,2048]{1,0:T(8,128)(2,1)S(1)} %pad_maximum_fusion.same), channel_id=1, source_target_pairs={{0,1},{1,0},{2,3},{3,2},{4,5},{5,4},{6,7},{7,6},{8,9},{9,8},{10,11... | collective-permute-start | bytes 3145736 | tf_op jit(solution)/shard_map/ppermute | solution.py:248
  135.3 43.8 %collective-permute-start.27 = (bf16[256,2048]{1,0:T(8,128)(2,1)}, bf16[256,2048]{1,0:T(8,128)(2,1)S(1)}, u32[]{:S(2)}, u32[]{:S(2)}) collective-permute-start(bf16[256,2048]{1,0:T(8,128)(2,1)} %collective-permute-done.26.same), channel_id=1, source_target_pairs={{0,1},{1,0},{2,3},{3,2},{4,5},{5,4},{6,7},{7,6},{8,9},{9,8},{10,11... | collective-permute-start | bytes 3145736 | tf_op jit(solution)/shard_map/ppermute | solution.py:248
  153.5 45.5 %collective-permute-start.13 = (bf16[256,2048]{1,0:T(8,128)(2,1)S(1)}, bf16[256,2048]{1,0:T(8,128)(2,1)}, u32[]{:S(2)}, u32[]{:S(2)}) collective-permute-start(bf16[256,2048]{1,0:T(8,128)(2,1)S(1)} %collective-permute-done.12.same), channel_id=1, source_target_pairs={{0,1},{1,0},{2,3},{3,2},{4,5},{5,4},{6,7},{7,6},{8,9},{9,8},{10,11... | collective-permute-start | bytes 3145736 | tf_op jit(solution)/shard_map/ppermute | solution.py:248
  154.5 67.2 %collective-permute-start.59 = (bf16[1,80,1152]{2,1,0:T(8,128)(2,1)S(1)}, bf16[1,80,1152]{2,1,0:T(8,128)(2,1)S(1)}, u32[]{:S(2)}, u32[]{:S(2)}) collective-permute-start(bf16[1,80,1152]{2,1,0:T(8,128)(2,1)S(1)} %get-tuple-element.104.refs_0_), channel_id=1, source_target_pairs={{0,16},{8,24},{16,0},{24,8},{1,17},{9,25},{17,1},{25,9},{2,18},{10... | collective-permute-start | bytes 552968 | tf_op jit(solution)/shard_map/ppermute | solution.py:248
  157.2 65.6 %collective-permute-start.58 = (bf16[1,80,1152]{2,1,0:T(8,128)(2,1)S(1)}, bf16[1,80,1152]{2,1,0:T(8,128)(2,1)S(1)}, u32[]{:S(2)}, u32[]{:S(2)}) collective-permute-start(bf16[1,80,1152]{2,1,0:T(8,128)(2,1)S(1)} %get-tuple-element.104.refs_0_), channel_id=1, source_target_pairs={{0,8},{8,0},{16,24},{24,16},{1,9},{9,1},{17,25},{25,17},{2,10},{10... | collective-permute-start | bytes 552968 | tf_op jit(solution)/shard_map/ppermute | solution.py:248
  159.3 80.8 %collective-permute-start.62 = (bf16[1,80,1152]{2,1,0:T(8,128)(2,1)S(1)}, bf16[1,80,1152]{2,1,0:T(8,128)(2,1)S(1)}, u32[]{:S(2)}, u32[]{:S(2)}) collective-permute-start(bf16[1,80,1152]{2,1,0:T(8,128)(2,1)S(1)} %get-tuple-element.105.refs_4_), channel_id=1, source_target_pairs={{0,16},{8,24},{16,0},{24,8},{1,17},{9,25},{17,1},{25,9},{2,18},{10... | collective-permute-start | bytes 552968 | tf_op jit(solution)/shard_map/ppermute | solution.py:248
  179.2 40.3 %collective-permute-start.42 = (bf16[2,2,80,1152]{3,2,1,0:T(8,128)(2,1)S(1)}, bf16[2,2,80,1152]{3,2,1,0:T(8,128)(2,1)S(1)}, u32[]{:S(2)}, u32[]{:S(2)}) collective-permute-start(bf16[2,2,80,1152]{3,2,1,0:T(8,128)(2,1)S(1)} %get-tuple-element.90), channel_id=1, source_target_pairs={{0,8},{8,0},{16,24},{24,16},{1,9},{9,1},{17,25},{25,17},{2,10},{10... | collective-permute-start | bytes 2211848 | tf_op jit(solution)/shard_map/ppermute | solution.py:248
  238.8 28.6 %collective-permute-start.14 = (bf16[2,2,80,1152]{3,2,1,0:T(8,128)(2,1)}, bf16[2,2,80,1152]{3,2,1,0:T(8,128)(2,1)S(1)}, u32[]{:S(2)}, u32[]{:S(2)}) collective-permute-start(bf16[2,2,80,1152]{3,2,1,0:T(8,128)(2,1)} %get-tuple-element.70), channel_id=1, source_target_pairs={{0,8},{8,0},{16,24},{24,16},{1,9},{9,1},{17,25},{25,17},{2,10},{10... | collective-permute-start | bytes 2211848 | tf_op jit(solution)/shard_map/ppermute | solution.py:248
  245.0 28.9 %collective-permute-start.15 = (bf16[2,2,80,1152]{3,2,1,0:T(8,128)(2,1)S(1)}, bf16[2,2,80,1152]{3,2,1,0:T(8,128)(2,1)S(1)}, u32[]{:S(2)}, u32[]{:S(2)}) collective-permute-start(bf16[2,2,80,1152]{3,2,1,0:T(8,128)(2,1)S(1)} %get-tuple-element.71), channel_id=1, source_target_pairs={{0,16},{8,24},{16,0},{24,8},{1,17},{9,25},{17,1},{25,9},{2,18},{10... | collective-permute-start | bytes 2211848 | tf_op jit(solution)/shard_map/ppermute | solution.py:248
  301.1 39.0 %collective-permute-start.33 = (bf16[2,80,1152]{2,1,0:T(8,128)(2,1)S(1)}, bf16[2,80,1152]{2,1,0:T(8,128)(2,1)S(1)}, u32[]{:S(2)}, u32[]{:S(2)}) collective-permute-start(bf16[2,80,1152]{2,1,0:T(8,128)(2,1)S(1)} %get-tuple-element.84.refs_0_), channel_id=1, source_target_pairs={{0,16},{8,24},{16,0},{24,8},{1,17},{9,25},{17,1},{25,9},{2,18},{10... | collective-permute-start | bytes 1105928 | tf_op jit(solution)/shard_map/ppermute | solution.py:248
  305.6 35.7 %collective-permute-start.32 = (bf16[2,80,1152]{2,1,0:T(8,128)(2,1)S(1)}, bf16[2,80,1152]{2,1,0:T(8,128)(2,1)S(1)}, u32[]{:S(2)}, u32[]{:S(2)}) collective-permute-start(bf16[2,80,1152]{2,1,0:T(8,128)(2,1)S(1)} %get-tuple-element.84.refs_0_), channel_id=1, source_target_pairs={{0,8},{8,0},{16,24},{24,16},{1,9},{9,1},{17,25},{25,17},{2,10},{10... | collective-permute-start | bytes 1105928 | tf_op jit(solution)/shard_map/ppermute | solution.py:248
  306.8 35.4 %collective-permute-start.35 = (bf16[2,80,1152]{2,1,0:T(8,128)(2,1)S(1)}, bf16[2,80,1152]{2,1,0:T(8,128)(2,1)S(1)}, u32[]{:S(2)}, u32[]{:S(2)}) collective-permute-start(bf16[2,80,1152]{2,1,0:T(8,128)(2,1)S(1)} %get-tuple-element.85.refs_4_), channel_id=1, source_target_pairs={{0,8},{8,0},{16,24},{24,16},{1,9},{9,1},{17,25},{25,17},{2,10},{10... | collective-permute-start | bytes 1105928 | tf_op jit(solution)/shard_map/ppermute | solution.py:248
  313.5 29.8 %collective-permute-start.48 = (bf16[2,80,1152]{2,1,0:T(8,128)(2,1)S(1)}, bf16[2,80,1152]{2,1,0:T(8,128)(2,1)S(1)}, u32[]{:S(2)}, u32[]{:S(2)}) collective-permute-start(bf16[2,80,1152]{2,1,0:T(8,128)(2,1)S(1)} %collective-permute-done.47.refs_2_), channel_id=1, source_target_pairs={{0,8},{8,0},{16,24},{24,16},{1,9},{9,1},{17,25},{25,17},{2,10},{10... | collective-permute-start | bytes 1105928 | tf_op jit(solution)/shard_map/ppermute | solution.py:248
  314.7 29.5 %collective-permute-start.51 = (bf16[2,80,1152]{2,1,0:T(8,128)(2,1)S(1)}, bf16[2,80,1152]{2,1,0:T(8,128)(2,1)S(1)}, u32[]{:S(2)}, u32[]{:S(2)}) collective-permute-start(bf16[2,80,1152]{2,1,0:T(8,128)(2,1)S(1)} %collective-permute-done.49.refs_5_), channel_id=1, source_target_pairs={{0,16},{8,24},{16,0},{24,8},{1,17},{9,25},{17,1},{25,9},{2,18},{10... | collective-permute-start | bytes 1105928 | tf_op jit(solution)/shard_map/ppermute | solution.py:248
  340.1 25.0 %collective-permute-start.36 = (bf16[2,80,1152]{2,1,0:T(8,128)(2,1)S(1)}, bf16[2,80,1152]{2,1,0:T(8,128)(2,1)S(1)}, u32[]{:S(2)}, u32[]{:S(2)}) collective-permute-start(bf16[2,80,1152]{2,1,0:T(8,128)(2,1)S(1)} %get-tuple-element.85.refs_4_), channel_id=1, source_target_pairs={{0,16},{8,24},{16,0},{24,8},{1,17},{9,25},{17,1},{25,9},{2,18},{10... | collective-permute-start | bytes 1105928 | tf_op jit(solution)/shard_map/ppermute | solution.py:248
  369.2 40.9 %collective-permute-start.52 = (bf16[256,2048]{1,0:T(8,128)(2,1)}, bf16[256,2048]{1,0:T(8,128)(2,1)S(1)}, u32[]{:S(2)}, u32[]{:S(2)}) collective-permute-start(bf16[256,2048]{1,0:T(8,128)(2,1)} %get-tuple-element.97), channel_id=1, source_target_pairs={{0,1},{1,0},{2,3},{3,2},{4,5},{5,4},{6,7},{7,6},{8,9},{9,8},{10,11... | collective-permute-start | bytes 3145736 | tf_op jit(solution)/shard_map/ppermute | solution.py:248
  389.5 159.9 %collective-permute-start.64 = (bf16[256,2048]{1,0:T(8,128)(2,1)}, bf16[256,2048]{1,0:T(8,128)(2,1)}, u32[]{:S(2)}, u32[]{:S(2)}) collective-permute-start(bf16[256,2048]{1,0:T(8,128)(2,1)} %get-tuple-element.107), channel_id=1, source_target_pairs={{0,1},{1,0},{2,3},{3,2},{4,5},{5,4},{6,7},{7,6},{8,9},{9,8},{10,11... | collective-permute-start | bytes 3145736 | tf_op jit(solution)/shard_map/ppermute | solution.py:248
  389.7 159.7 %collective-permute-start.11 = (bf16[256,2048]{1,0:T(8,128)(2,1)}, bf16[256,2048]{1,0:T(8,128)(2,1)}, u32[]{:S(2)}, u32[]{:S(2)}) collective-permute-start(bf16[256,2048]{1,0:T(8,128)(2,1)} %get-tuple-element.67), channel_id=1, source_target_pairs={{0,1},{1,0},{2,3},{3,2},{4,5},{5,4},{6,7},{7,6},{8,9},{9,8},{10,11... | collective-permute-start | bytes 3145736 | tf_op jit(solution)/shard_map/ppermute | solution.py:248
  410.5 138.9 %collective-permute-start.53 = (bf16[256,2048]{1,0:T(8,128)(2,1)S(1)}, bf16[256,2048]{1,0:T(8,128)(2,1)}, u32[]{:S(2)}, u32[]{:S(2)}) collective-permute-start(bf16[256,2048]{1,0:T(8,128)(2,1)S(1)} %add_convert_fusion.1), channel_id=1, source_target_pairs={{0,6},{1,7},{2,4},{3,5},{4,2},{5,3},{6,0},{7,1},{8,14},{9,15},{10,... | collective-permute-start | bytes 3145736 | tf_op jit(solution)/shard_map/ppermute | solution.py:248
  413.5 135.9 %collective-permute-start.39 = (bf16[256,2048]{1,0:T(8,128)(2,1)}, bf16[256,2048]{1,0:T(8,128)(2,1)}, u32[]{:S(2)}, u32[]{:S(2)}) collective-permute-start(bf16[256,2048]{1,0:T(8,128)(2,1)} %add_convert_fusion.2), channel_id=1, source_target_pairs={{0,4},{1,5},{2,6},{3,7},{4,0},{5,1},{6,2},{7,3},{8,12},{9,13},{10,... | collective-permute-start | bytes 3145736 | tf_op jit(solution)/shard_map/ppermute | solution.py:248
  418.2 131.2 %collective-permute-start.25 = (bf16[256,2048]{1,0:T(8,128)(2,1)}, bf16[256,2048]{1,0:T(8,128)(2,1)}, u32[]{:S(2)}, u32[]{:S(2)}) collective-permute-start(bf16[256,2048]{1,0:T(8,128)(2,1)} %add_convert_fusion.3), channel_id=1, source_target_pairs={{0,2},{1,3},{2,0},{3,1},{4,6},{5,7},{6,4},{7,5},{8,10},{9,11},{10,... | collective-permute-start | bytes 3145736 | tf_op jit(solution)/shard_map/ppermute | solution.py:248
  (78 other events, 1302.1 us)

commit v2 on v1

--- a/solution.py
+++ b/solution.py
@@ -120,8 +120,8 @@
     )(me, same, other, slots, w_gate, w_up, w_down)
 
 
-def middle_kernel(self_a, self_b, first_a, first_b, last_a, last_b, slots, share,
-                  out_a, out_b, grad):
+def middle_kernel(me, self_a, self_b, first_a, first_b, last_a, last_b, slots, share,
+                  out_a, out_b):
     count, rows, cols = self_a.shape
     hidden = 2 * cols // 3
     half = hidden // 2
@@ -158,25 +158,30 @@
             else:
                 out_b[h, :, pl.ds(0, half)] = gate_out
             out_b[h, :, pl.ds(half + lo, half)] = up_out
-        grad[h] = jnp.sum(jnp.where(hot, grads, 0.0), axis=0, keepdims=True)
-
-
-def middle(self_a, self_b, first_a, first_b, last_a, last_b, slots, share):
+        lane = lax.broadcasted_iota(jnp.int32, (rows, 2 * EXPERTS), 1)
+        high = grads.astype(jnp.bfloat16).astype(jnp.float32)
+        spread = jnp.where(lane == me[0] + h, high, 0.0)
+        spread = jnp.where(lane == me[0] + h + EXPERTS, grads - high, spread)
+        out_a[h, :, pl.ds(cols, 2 * EXPERTS)] = spread.astype(jnp.bfloat16)
+
+
+def middle(first, self_a, self_b, first_a, first_b, last_a, last_b, slots, share):
+    count, rows, cols = self_a.shape
     outs = (
-        jax.ShapeDtypeStruct(self_a.shape, jnp.bfloat16),
+        jax.ShapeDtypeStruct((count, rows, cols + 2 * EXPERTS), jnp.bfloat16),
         jax.ShapeDtypeStruct(self_b.shape, jnp.bfloat16),
-        jax.ShapeDtypeStruct(share.shape, jnp.float32),
     )
     return pl.pallas_call(
         middle_kernel,
         out_shape=outs,
-        in_specs=[pl.BlockSpec(memory_space=pltpu.VMEM)] * 8,
-        out_specs=[pl.BlockSpec(memory_space=pltpu.VMEM)] * 3,
+        in_specs=[pl.BlockSpec(memory_space=pltpu.SMEM)]
+        + [pl.BlockSpec(memory_space=pltpu.VMEM)] * 8,
+        out_specs=[pl.BlockSpec(memory_space=pltpu.VMEM)] * 2,
         compiler_params=pltpu.CompilerParams(vmem_limit_bytes=VMEM_BYTES),
         cost_estimate=pl.CostEstimate(
             flops=40 * self_a.size, bytes_accessed=14 * self_a.size, transcendentals=self_a.size
         ),
-    )(self_a, self_b, first_a, first_b, last_a, last_b, slots, share)
+    )(first, self_a, self_b, first_a, first_b, last_a, last_b, slots, share)
 
 
 def combine_kernel(count, me, *refs):
@@ -184,15 +189,16 @@
     slots, w_gate, w_up, w_down, same, other, rows_in, hots, outs = refs[8:]
     step = pl.program_id(0)
     part, half = step // count, step % count
-    rows, cols = rows_in.shape[0], lefts[0].shape[2]
+    rows, cols = rows_in.shape[0], rights[0].shape[2]
     hidden = w_gate.shape[2]
     features = w_gate.shape[1]
+    at = pl.ds(pl.multiple_of(step * rows, 16), rows)
     for v in range(4):
         @pl.when(part == v)
         def _():
-            rows_in[:, pl.ds(0, cols)] = lefts[v][half]
+            rows_in[:, pl.ds(0, cols)] = lefts[v][half, :, pl.ds(0, cols)]
             rows_in[:, pl.ds(cols, cols)] = rights[v][half]
-    at = pl.ds(pl.multiple_of(step * rows, 16), rows)
+            outs[at, pl.ds(2 * features, 2 * EXPERTS)] = lefts[v][half, :, pl.ds(cols, 2 * EXPERTS)]
     outs[at, pl.ds(0, features)] = dot_nn(rows_in[:, pl.ds(0, hidden)], w_down[0]).astype(jnp.bfloat16)
     outs[at, pl.ds(features, features)] = (
         dot_nt(rows_in[:, pl.ds(hidden, hidden)], w_gate[0])
@@ -213,7 +219,8 @@
     rows = 2 * CAP
     tokens = slots.shape[2] // 2
     steps = 4 * count
-    out = jax.ShapeDtypeStruct((tokens, 2 * features), jnp.bfloat16)
+    width = 2 * features + 2 * EXPERTS
+    out = jax.ShapeDtypeStruct((tokens, width), jnp.bfloat16)
     return pl.pallas_call(
         functools.partial(combine_kernel, count),
         grid_spec=pltpu.PrefetchScalarGridSpec(
@@ -230,7 +237,7 @@
             scratch_shapes=[
                 pltpu.VMEM((rows, 3 * hidden), jnp.bfloat16),
                 pltpu.VMEM((steps * rows, 2 * tokens), jnp.bfloat16),
-                pltpu.VMEM((steps * rows, 2 * features), jnp.bfloat16),
+                pltpu.VMEM((steps * rows, width), jnp.bfloat16),
             ],
         ),
         out_shape=(out, out),
@@ -263,28 +270,36 @@
     sames = [payload] + [swap(payload, "expert", 2 * o) for o in range(1, chips)]
     others = [swap(p, "expert", 1) for p in sames]
 
-    picks = lax.all_gather(jnp.stack([routes, gate_levels]), "expert")
-    order = jnp.arange(peers, dtype=jnp.int32) ^ mine
-    picks = picks[order]
-    levels = picks[:, 1].astype(jnp.float32)
-    fractions = levels / jnp.sum(levels, axis=2, keepdims=True)
     local = mine * per_device + jnp.arange(per_device, dtype=jnp.int32)
-    named = picks[:, 0][None] == local[:, None, None, None]
-    share = jnp.sum(jnp.where(named, fractions[None], 0.0), axis=3)
-    chosen = jnp.any(named, axis=3)
     tri = (jnp.arange(block)[:, None] < jnp.arange(block)[None, :]).astype(jnp.bfloat16)
-    place = jnp.einsum(
-        "jst,tu->jsu", chosen.astype(jnp.bfloat16), tri, preferred_element_type=jnp.float32
-    ).astype(jnp.int32)
-    place = place + (jnp.arange(peers, dtype=jnp.int32) % 2 * CAP)[None, :, None]
-    slots = jnp.where(chosen, place, -1).reshape(per_device, chips, 1, 2 * block)
-    share = share.reshape(per_device, chips, 1, 2 * block)
+
+    def placed(picks):
+        levels = picks[:, 1].astype(jnp.float32)
+        fractions = levels / jnp.sum(levels, axis=1, keepdims=True)
+        named = picks[:, 0][None] == local[:, None, None, None]
+        share = jnp.sum(jnp.where(named, fractions[None], 0.0), axis=2)
+        chosen = jnp.any(named, axis=2)
+        place = jnp.einsum(
+            "jst,tu->jsu", chosen.astype(jnp.bfloat16), tri, preferred_element_type=jnp.float32
+        ).astype(jnp.int32)
+        place = place + (jnp.arange(picks.shape[0], dtype=jnp.int32) % 2 * CAP)[None, :, None]
+        slots = jnp.where(chosen, place, -1)
+        pairs = (per_device, picks.shape[0] // 2, 1, 2 * block)
+        return slots.reshape(pairs), share.reshape(pairs)
+
+    picks = jnp.stack([routes.T, gate_levels.T])
+    near = jnp.stack([picks, swap(picks, "expert", 1)])
+    away = jnp.stack([swap(picks, "expert", 2 * o) for o in range(1, chips)])
+    far = jnp.stack([away, swap(away, "expert", 1)], axis=1).reshape(-1, *picks.shape)
+    near_slots, near_share = placed(near)
+    far_slots, far_share = placed(far)
 
     weights = (gate_weight, up_weight, down_weight)
     chunks = [(0, (0,))] + [(o, (0, 1)) for o in range(1, chips)] + [(0, (1,))]
-    partials, grads, totals = [], {}, []
+    totals = []
     for o, halves in chunks:
-        slot = slots[:, o]
+        slot = far_slots[:, o - 1] if o else near_slots[:, 0]
+        part = far_share[:, o - 1] if o else near_share[:, 0]
         self_a, self_b, send_a, keep_a, send_b, keep_b = partial_sums(
             me, sames[o], others[o], slot, *weights, halves
         )
@@ -293,12 +308,11 @@
         last_b = swap(keep_b + first_b[1], "dp", 1)
         first = 2 * member + halves[0]
         own_slot = lax.dynamic_slice_in_dim(slot, first, len(halves), 0)
-        own_share = lax.dynamic_slice_in_dim(share[:, o], first, len(halves), 0)
-        a, b, grad = middle(
-            self_a, self_b, first_a, first_b, last_a, last_b, own_slot, own_share
+        own_share = lax.dynamic_slice_in_dim(part, first, len(halves), 0)
+        expert = (mine * per_device + first).astype(jnp.int32).reshape(1)
+        a, b = middle(
+            expert, self_a, self_b, first_a, first_b, last_a, last_b, own_slot, own_share
         )
-        for n, h in enumerate(halves):
-            grads[o, h] = grad[n]
         a_x, a_y, b_x, b_y = swap(a, "dp", 1), swap(a, "dp", 2), swap(b, "dp", 1), swap(b, "dp", 2)
         a_d, b_d = swap(a_y, "dp", 1), swap(b_x, "dp", 2)
         same, other = combine(
@@ -308,16 +322,11 @@
         if o:
             both = swap(both.astype(jnp.bfloat16), "expert", 2 * o)
         totals.append(both)
-    total = sum(t.astype(jnp.float32) for t in totals).astype(jnp.bfloat16)
-
-    grad_all = jnp.stack([jnp.stack([grads[o, h] for o in range(chips)]) for h in range(2)])
-    grad_all = lax.all_gather(grad_all.reshape(2, peers, block), ("expert", "dp"))
-    grad_all = grad_all.reshape(peers, per_device, peers, block)
-    place_of = (jnp.arange(peers)[:, None] ^ mine) == jnp.arange(peers)[None, :]
-    to_me = jnp.sum(jnp.where(place_of[:, None, :, None], grad_all, 0.0), axis=2)
-    to_me = to_me.reshape(peers * per_device, block)
+    total = sum(t.astype(jnp.float32) for t in totals)
+    grads = total[:, 2 * features : 2 * features + EXPERTS] + total[:, 2 * features + EXPERTS :]
     hit = routes[:, :, None] == jnp.arange(EXPERTS, dtype=jnp.int32)
-    gate_grad = jnp.sum(jnp.where(hit, to_me.T[:, None, :], 0.0), axis=2)
+    gate_grad = jnp.sum(jnp.where(hit, grads[:, None, :], 0.0), axis=2)
+    total = total[:, : 2 * features].astype(jnp.bfloat16)
     return total[:, :features], total[:, features:], gate_grad
 
 

time: 560 us -> 504 us (0.900)
  blocking collectives: 225 us -> 0 us
  waiting for transfers between devices: 74.6 us -> 255 us
  local copies, waits for them, and re-layouts: 15.5 us -> 3.54 us
  starting transfers between devices: 62.2 us -> 73.9 us
    all_gather x2 -> x0, blocking collectives: 225 us -> none  [the longest x1 130 us: grouped(): lax.all_gather(grad_all.reshape(2, peers, block), ('expert', 'dp'))]
    ppermute x65 -> x70, waiting for transfers between devices: 74.6 us -> 255 us  [swap(): return lax.ppermute(value, axis, [(n, n ^ bits) for n in range(count)])]
    ppermute x65 -> x70, starting transfers between devices: 62.2 us -> 73.9 us  [swap(): return lax.ppermute(value, axis, [(n, n ^ bits) for n in range(count)])]
    unnamed x74 -> x40, local copies, waits for them, and re-layouts: 7.69 us -> 2.09 us
  transfers between devices with their start and end apart: 65 -> 70, of which waited for: 15 -> 22; matrix products, arithmetic and copies ran while one was open for 2% -> 1% of each run, Pallas kernels for 29% -> 32%
where the time goes in v2:
time: 504 us; the launch traced here: 503 us
  waiting for transfers between devices  255 us (51%)
  Pallas kernels  160 us (32%)
  starting transfers between devices  73.9 us (15%)
  other arithmetic  8.72 us (2%)
    ppermute x70, waiting for transfers between devices, swap(): return lax.ppermute(value, axis, [(n, n ^ bits) for n in range(count)])  255 us
    pallas_call x5, Pallas kernels, combine(): pl.pallas_call(functools.partial(combine_kernel, count), grid_spec=pltpu....  82.2 us
    pallas_call x5, Pallas kernels, partial_sums(): pl.pallas_call(functools.partial(partial_kernel, count), grid_spec=pltpu....  75.6 us
    ppermute x70, starting transfers between devices, swap(): return lax.ppermute(value, axis, [(n, n ^ bits) for n in range(count)])  73.9 us
  transfers between devices with their start and end apart: 70, of which 22 were waited for; matrix products, arithmetic and copies ran while one was open for 1% of the time, Pallas kernels for 32%

profile of v2, /device:TPU:8, one launch (start us, length us, event | category | flops | bytes accessed | tf_op | source)
XLA Modules:
  0.0 503.3 jit_solution(3036851586854719131)
XLA Ops:
  16.1 9.6 %shard_map.115 = (bf16[1,80,1152]{2,1,0:T(8,128)(2,1)S(1)}, bf16[1,80,1152]{2,1,0:T(8,128)(2,1)S(1)}, bf16[2,1,80,1152]{3,2,1,0:T(8,128)(2,1)S(1)}, bf16[1,80,11...) custom-call(s32[1]{0:T(128)} %bitcast.me, ...), custom_call_target="tpu_custom_call" | custom-call | flops 2516582400 | bytes 18874368 | tf_op jit(solution)/shard_map/pallas_call | solution.py:98
  29.0 9.6 %shard_map.103 = (bf16[1,80,1152]{2,1,0:T(8,128)(2,1)S(1)}, bf16[1,80,1152]{2,1,0:T(8,128)(2,1)S(1)}, bf16[2,1,80,1152]{3,2,1,0:T(8,128)(2,1)S(1)}, bf16[1,80,11...) custom-call(s32[1]{0:T(128)} %bitcast.me, ...), custom_call_target="tpu_custom_call" | custom-call | flops 2516582400 | bytes 18874368 | tf_op jit(solution)/shard_map/pallas_call | solution.py:98
  39.2 38.7 %collective-permute-done.45.same = bf16[256,2048]{1,0:T(8,128)(2,1)S(1)} collective-permute-done((bf16[256,2048]{1,0:T(8,128)(2,1)S(1)}, bf16[256,2048]{1,0:T(8,128)(2,1)S(1)}, u32[]{:S(2)}, u32[]{:S(2)}) %collective-permute-start.45) | collective-permute-done | bytes 1048608 | tf_op jit(solution)/shard_map/ppermute | solution.py:255
  79.4 19.3 %collective-permute-done.31.same = bf16[256,2048]{1,0:T(8,128)(2,1)} collective-permute-done((bf16[256,2048]{1,0:T(8,128)(2,1)S(1)}, bf16[256,2048]{1,0:T(8,128)(2,1)}, u32[]{:S(2)}, u32[]{:S(2)}) %collective-permute-start.31) | collective-permute-done | bytes 1048608 | tf_op jit(solution)/shard_map/ppermute | solution.py:255
  103.1 3.8 collective-permute-done.61.last_a
  115.9 18.5 %shard_map.112 = (bf16[2,80,1152]{2,1,0:T(8,128)(2,1)S(1)}, bf16[2,80,1152]{2,1,0:T(8,128)(2,1)S(1)}, bf16[2,2,80,1152]{3,2,1,0:T(8,128)(2,1)S(1)}, bf16[2,80,11...) custom-call(s32[1]{0:T(128)} %bitcast.me, ...), custom_call_target="tpu_custom_call" | custom-call | flops 5033164800 | bytes 37748736 | tf_op jit(solution)/shard_map/pallas_call | solution.py:98
  135.9 18.8 %shard_map.109 = (bf16[2,80,1152]{2,1,0:T(8,128)(2,1)S(1)}, bf16[2,80,1152]{2,1,0:T(8,128)(2,1)S(1)}, bf16[2,2,80,1152]{3,2,1,0:T(8,128)(2,1)S(1)}, bf16[2,80,11...) custom-call(s32[1]{0:T(128)} %bitcast.me, ...), custom_call_target="tpu_custom_call" | custom-call | flops 5033164800 | bytes 37748736 | tf_op jit(solution)/shard_map/pallas_call | solution.py:98
  155.7 19.0 %shard_map.106 = (bf16[2,80,1152]{2,1,0:T(8,128)(2,1)S(1)}, bf16[2,80,1152]{2,1,0:T(8,128)(2,1)S(1)}, bf16[2,2,80,1152]{3,2,1,0:T(8,128)(2,1)S(1)}, bf16[2,80,11...) custom-call(s32[1]{0:T(128)} %bitcast.me, ...), custom_call_target="tpu_custom_call" | custom-call | flops 5033164800 | bytes 37748736 | tf_op jit(solution)/shard_map/pallas_call | solution.py:98
  177.1 17.2 %collective-permute-done.33.first_a = bf16[2,2,80,1152]{3,2,1,0:T(8,128)(2,1)S(1)} collective-permute-done((bf16[2,2,80,1152]{3,2,1,0:T(8,128)(2,1)S(1)}, bf16[2,2,80,1152]{3,2,1,0:T(8,128)(2,1)S(1)}, u32[]{:S(2)}, u32[]{:S(2)}) %collective-permute-start.33) | collective-permute-done | bytes 737312 | tf_op jit(solution)/shard_map/ppermute | solution.py:255
  196.2 10.7 %collective-permute-done.19.first_a = bf16[2,2,80,1152]{3,2,1,0:T(8,128)(2,1)S(1)} collective-permute-done((bf16[2,2,80,1152]{3,2,1,0:T(8,128)(2,1)S(1)}, bf16[2,2,80,1152]{3,2,1,0:T(8,128)(2,1)S(1)}, u32[]{:S(2)}, u32[]{:S(2)}) %collective-permute-start.19) | collective-permute-done | bytes 737312 | tf_op jit(solution)/shard_map/ppermute | solution.py:255
  211.1 16.2 %collective-permute-done.10.refs_6_ = bf16[1,80,1152]{2,1,0:T(8,128)(2,1)S(1)} collective-permute-done((bf16[1,80,1152]{2,1,0:T(8,128)(2,1)S(1)}, bf16[1,80,1152]{2,1,0:T(8,128)(2,1)S(1)}, u32[]{:S(2)}, u32[]{:S(2)}) %collective-permute-start.10) | collective-permute-done | bytes 184352 | tf_op jit(solution)/shard_map/ppermute | solution.py:255
  231.9 3.4 collective-permute-done.7.refs_2_
  235.8 7.4 %collective-permute-done.49.last_a = bf16[2,80,1152]{2,1,0:T(8,128)(2,1)S(1)} collective-permute-done((bf16[2,80,1152]{2,1,0:T(8,128)(2,1)S(1)}, bf16[2,80,1152]{2,1,0:T(8,128)(2,1)S(1)}, u32[]{:S(2)}, u32[]{:S(2)}) %collective-permute-start.49) | collective-permute-done | bytes 368672 | tf_op jit(solution)/shard_map/ppermute | solution.py:255
  245.3 5.9 %collective-permute-done.21.last_a = bf16[2,80,1152]{2,1,0:T(8,128)(2,1)S(1)} collective-permute-done((bf16[2,80,1152]{2,1,0:T(8,128)(2,1)S(1)}, bf16[2,80,1152]{2,1,0:T(8,128)(2,1)S(1)}, u32[]{:S(2)}, u32[]{:S(2)}) %collective-permute-start.21) | collective-permute-done | bytes 368672 | tf_op jit(solution)/shard_map/ppermute | solution.py:255
  267.9 20.3 %collective-permute-done.8.refs_3_ = bf16[1,80,1280]{2,1,0:T(8,128)(2,1)S(1)} collective-permute-done((bf16[1,80,1280]{2,1,0:T(8,128)(2,1)S(1)}, bf16[1,80,1280]{2,1,0:T(8,128)(2,1)S(1)}, u32[]{:S(2)}, u32[]{:S(2)}) %collective-permute-start.8) | collective-permute-done | bytes 204832 | tf_op jit(solution)/shard_map/ppermute | solution.py:255
  295.2 10.5 %shard_map.105 = (bf16[256,2176]{1,0:T(8,128)(2,1)S(1)}, bf16[256,2176]{1,0:T(8,128)(2,1)S(1)}) custom-call(s32[1]{0:T(128)} %bitcast.me, bf16[1,80,1280]{2,1,0:T(8,128)(2,1)S(1)} %get-tuple-element.59.refs_0_, bf16[1,80,1280]{2,1,0:T(8,128)(2,1)S(1)} %collective-permute-done.6.refs_1_, bf16[1,80,1280]{2,1,0:T(8,128)(2,1)S(1)} %collective-permute-done.7.refs_2_, ...), custom_call_target="tpu_custom_call" | custom-call | flops 2516582400 | bytes 18874368 | tf_op jit(solution)/shard_map/pallas_call | solution.py:224
  312.0 4.4 collective-permute-done.28.refs_7_
  319.7 20.3 %shard_map.108 = (bf16[256,2176]{1,0:T(8,128)(2,1)}, bf16[256,2176]{1,0:T(8,128)(2,1)}) custom-call(s32[1]{0:T(128)} %bitcast.me, bf16[2,80,1280]{2,1,0:T(8,128)(2,1)S(1)} %get-tuple-element.69.refs_0_, bf16[2,80,1280]{2,1,0:T(8,128)(2,1)S(1)} %collective-permute-done.23.refs_1_, bf16[2,80,1280]{2,1,0:T(8,128)(2,1)S(1)} %collective-permute-done.24.refs_2_, ...), custom_call_target="tpu_custom_call" | custom-call | flops 5033164800 | bytes 37748736 | tf_op jit(solution)/shard_map/pallas_call | solution.py:224
  340.1 10.6 %shard_map.117 = (bf16[256,2176]{1,0:T(8,128)(2,1)S(1)}, bf16[256,2176]{1,0:T(8,128)(2,1)S(1)}) custom-call(s32[1]{0:T(128)} %bitcast.me, bf16[1,80,1280]{2,1,0:T(8,128)(2,1)S(1)} %get-tuple-element.99.refs_0_, bf16[1,80,1280]{2,1,0:T(8,128)(2,1)S(1)} %collective-permute-done.63.refs_1_, bf16[1,80,1280]{2,1,0:T(8,128)(2,1)S(1)} %collective-permute-done.64.refs_2_, ...), custom_call_target="tpu_custom_call" | custom-call | flops 2516582400 | bytes 18874368 | tf_op jit(solution)/shard_map/pallas_call | solution.py:224
  355.8 20.3 %shard_map.111 = (bf16[256,2176]{1,0:T(8,128)(2,1)}, bf16[256,2176]{1,0:T(8,128)(2,1)}) custom-call(s32[1]{0:T(128)} %bitcast.me, bf16[2,80,1280]{2,1,0:T(8,128)(2,1)S(1)} %get-tuple-element.79.refs_0_, bf16[2,80,1280]{2,1,0:T(8,128)(2,1)S(1)} %collective-permute-done.37.refs_1_, bf16[2,80,1280]{2,1,0:T(8,128)(2,1)S(1)} %collective-permute-done.38.refs_2_, ...), custom_call_target="tpu_custom_call" | custom-call | flops 5033164800 | bytes 37748736 | tf_op jit(solution)/shard_map/pallas_call | solution.py:224
  376.8 20.5 %shard_map.114 = (bf16[256,2176]{1,0:T(8,128)(2,1)}, bf16[256,2176]{1,0:T(8,128)(2,1)}) custom-call(s32[1]{0:T(128)} %bitcast.me, bf16[2,80,1280]{2,1,0:T(8,128)(2,1)S(1)} %get-tuple-element.89.refs_0_, bf16[2,80,1280]{2,1,0:T(8,128)(2,1)S(1)} %collective-permute-done.51.refs_1_, bf16[2,80,1280]{2,1,0:T(8,128)(2,1)S(1)} %collective-permute-done.52.refs_2_, ...), custom_call_target="tpu_custom_call" | custom-call | flops 5033164800 | bytes 37748736 | tf_op jit(solution)/shard_map/pallas_call | solution.py:224
  405.1 44.3 %collective-permute-done.30 = bf16[256,2176]{1,0:T(8,128)(2,1)S(1)} collective-permute-done((bf16[256,2176]{1,0:T(8,128)(2,1)S(1)}, bf16[256,2176]{1,0:T(8,128)(2,1)S(1)}, u32[]{:S(2)}, u32[]{:S(2)}) %collective-permute-start.30) | collective-permute-done | bytes 1114144 | tf_op jit(solution)/shard_map/ppermute | solution.py:255
  449.4 26.7 %collective-permute-done.44 = bf16[256,2176]{1,0:T(8,128)(2,1)S(1)} collective-permute-done((bf16[256,2176]{1,0:T(8,128)(2,1)S(1)}, bf16[256,2176]{1,0:T(8,128)(2,1)S(1)}, u32[]{:S(2)}, u32[]{:S(2)}) %collective-permute-start.44) | collective-permute-done | bytes 1114144 | tf_op jit(solution)/shard_map/ppermute | solution.py:255
  476.1 24.2 %collective-permute-done.58 = bf16[256,2176]{1,0:T(8,128)(2,1)S(1)} collective-permute-done((bf16[256,2176]{1,0:T(8,128)(2,1)S(1)}, bf16[256,2176]{1,0:T(8,128)(2,1)S(1)}, u32[]{:S(2)}, u32[]{:S(2)}) %collective-permute-start.58) | collective-permute-done | bytes 1114144 | tf_op jit(solution)/shard_map/ppermute | solution.py:255
  (226 shorter events, 101.7 us)
Async XLA Ops:
  6.9 71.0 %collective-permute-start.45 = (bf16[256,2048]{1,0:T(8,128)(2,1)S(1)}, bf16[256,2048]{1,0:T(8,128)(2,1)S(1)}, u32[]{:S(2)}, u32[]{:S(2)}) collective-permute-start(bf16[256,2048]{1,0:T(8,128)(2,1)S(1)} %pad_maximum_fusion.same), channel_id=1, source_target_pairs={{0,6},{1,7},{2,4},{3,5},{4,2},{5,3},{6,0},{7,1},{8,14},{9,15},{10,... | collective-permute-start | bytes 3145736 | tf_op jit(solution)/shard_map/ppermute | solution.py:255
  8.6 90.2 %collective-permute-start.31 = (bf16[256,2048]{1,0:T(8,128)(2,1)S(1)}, bf16[256,2048]{1,0:T(8,128)(2,1)}, u32[]{:S(2)}, u32[]{:S(2)}) collective-permute-start(bf16[256,2048]{1,0:T(8,128)(2,1)S(1)} %pad_maximum_fusion.same), channel_id=1, source_target_pairs={{0,4},{1,5},{2,6},{3,7},{4,0},{5,1},{6,2},{7,3},{8,12},{9,13},{10,... | collective-permute-start | bytes 3145736 | tf_op jit(solution)/shard_map/ppermute | solution.py:255
  11.1 91.4 %collective-permute-start.13 = (bf16[256,2048]{1,0:T(8,128)(2,1)S(1)}, bf16[256,2048]{1,0:T(8,128)(2,1)}, u32[]{:S(2)}, u32[]{:S(2)}) collective-permute-start(bf16[256,2048]{1,0:T(8,128)(2,1)S(1)} %pad_maximum_fusion.same), channel_id=1, source_target_pairs={{0,2},{1,3},{2,0},{3,1},{4,6},{5,7},{6,4},{7,5},{8,10},{9,11},{10,... | collective-permute-start | bytes 3145736 | tf_op jit(solution)/shard_map/ppermute | solution.py:255
  27.4 71.4 %collective-permute-start.60 = (bf16[2,1,80,1152]{3,2,1,0:T(8,128)(2,1)S(1)}, bf16[2,1,80,1152]{3,2,1,0:T(8,128)(2,1)S(1)}, u32[]{:S(2)}, u32[]{:S(2)}) collective-permute-start(bf16[2,1,80,1152]{3,2,1,0:T(8,128)(2,1)S(1)} %get-tuple-element.96), channel_id=1, source_target_pairs={{0,16},{8,24},{16,0},{24,8},{1,17},{9,25},{17,1},{25,9},{2,18},{10... | collective-permute-start | bytes 1105928 | tf_op jit(solution)/shard_map/ppermute | solution.py:255
  38.6 60.7 %collective-permute-start.2 = (bf16[2,1,80,1152]{3,2,1,0:T(8,128)(2,1)S(1)}, bf16[2,1,80,1152]{3,2,1,0:T(8,128)(2,1)S(1)}, u32[]{:S(2)}, u32[]{:S(2)}) collective-permute-start(bf16[2,1,80,1152]{3,2,1,0:T(8,128)(2,1)S(1)} %get-tuple-element.55), channel_id=1, source_target_pairs={{0,8},{8,0},{16,24},{24,16},{1,9},{9,1},{17,25},{25,17},{2,10},{10... | collective-permute-start | bytes 1105928 | tf_op jit(solution)/shard_map/ppermute | solution.py:255
  98.8 35.6 %collective-permute-start.32 = (bf16[256,2048]{1,0:T(8,128)(2,1)}, bf16[256,2048]{1,0:T(8,128)(2,1)S(1)}, u32[]{:S(2)}, u32[]{:S(2)}) collective-permute-start(bf16[256,2048]{1,0:T(8,128)(2,1)} %collective-permute-done.31.same), channel_id=1, source_target_pairs={{0,1},{1,0},{2,3},{3,2},{4,5},{5,4},{6,7},{7,6},{8,9},{9,8},{10,11... | collective-permute-start | bytes 3145736 | tf_op jit(solution)/shard_map/ppermute | solution.py:255
  108.5 46.3 %collective-permute-start.14 = (bf16[256,2048]{1,0:T(8,128)(2,1)}, bf16[256,2048]{1,0:T(8,128)(2,1)S(1)}, u32[]{:S(2)}, u32[]{:S(2)}) collective-permute-start(bf16[256,2048]{1,0:T(8,128)(2,1)} %collective-permute-done.13.same), channel_id=1, source_target_pairs={{0,1},{1,0},{2,3},{3,2},{4,5},{5,4},{6,7},{7,6},{8,9},{9,8},{10,11... | collective-permute-start | bytes 3145736 | tf_op jit(solution)/shard_map/ppermute | solution.py:255
  109.9 97.3 %collective-permute-start.67 = (bf16[1,80,1152]{2,1,0:T(8,128)(2,1)S(1)}, bf16[1,80,1152]{2,1,0:T(8,128)(2,1)S(1)}, u32[]{:S(2)}, u32[]{:S(2)}) collective-permute-start(bf16[1,80,1152]{2,1,0:T(8,128)(2,1)S(1)} %get-tuple-element.100.refs_4_), channel_id=1, source_target_pairs={{0,16},{8,24},{16,0},{24,8},{1,17},{9,25},{17,1},{25,9},{2,18},{10... | collective-permute-start | bytes 552968 | tf_op jit(solution)/shard_map/ppermute | solution.py:255
  112.4 96.7 %collective-permute-start.66 = (bf16[1,80,1152]{2,1,0:T(8,128)(2,1)S(1)}, bf16[1,80,1152]{2,1,0:T(8,128)(2,1)S(1)}, u32[]{:S(2)}, u32[]{:S(2)}) collective-permute-start(bf16[1,80,1152]{2,1,0:T(8,128)(2,1)S(1)} %get-tuple-element.100.refs_4_), channel_id=1, source_target_pairs={{0,8},{8,0},{16,24},{24,16},{1,9},{9,1},{17,25},{25,17},{2,10},{10... | collective-permute-start | bytes 552968 | tf_op jit(solution)/shard_map/ppermute | solution.py:255
  114.3 115.1 %collective-permute-start.64 = (bf16[1,80,1280]{2,1,0:T(8,128)(2,1)S(1)}, bf16[1,80,1280]{2,1,0:T(8,128)(2,1)S(1)}, u32[]{:S(2)}, u32[]{:S(2)}) collective-permute-start(bf16[1,80,1280]{2,1,0:T(8,128)(2,1)S(1)} %get-tuple-element.99.refs_0_), channel_id=1, source_target_pairs={{0,16},{8,24},{16,0},{24,8},{1,17},{9,25},{17,1},{25,9},{2,18},{10... | collective-permute-start | bytes 614408 | tf_op jit(solution)/shard_map/ppermute | solution.py:255
  135.4 39.4 %collective-permute-start.47 = (bf16[2,2,80,1152]{3,2,1,0:T(8,128)(2,1)S(1)}, bf16[2,2,80,1152]{3,2,1,0:T(8,128)(2,1)S(1)}, u32[]{:S(2)}, u32[]{:S(2)}) collective-permute-start(bf16[2,2,80,1152]{3,2,1,0:T(8,128)(2,1)S(1)} %get-tuple-element.85), channel_id=1, source_target_pairs={{0,8},{8,0},{16,24},{24,16},{1,9},{9,1},{17,25},{25,17},{2,10},{10... | collective-permute-start | bytes 2211848 | tf_op jit(solution)/shard_map/ppermute | solution.py:255
  176.4 30.4 %collective-permute-start.19 = (bf16[2,2,80,1152]{3,2,1,0:T(8,128)(2,1)S(1)}, bf16[2,2,80,1152]{3,2,1,0:T(8,128)(2,1)S(1)}, u32[]{:S(2)}, u32[]{:S(2)}) collective-permute-start(bf16[2,2,80,1152]{3,2,1,0:T(8,128)(2,1)S(1)} %get-tuple-element.65), channel_id=1, source_target_pairs={{0,8},{8,0},{16,24},{24,16},{1,9},{9,1},{17,25},{25,17},{2,10},{10... | collective-permute-start | bytes 2211848 | tf_op jit(solution)/shard_map/ppermute | solution.py:255
  259.0 32.2 %collective-permute-start.54 = (bf16[2,80,1152]{2,1,0:T(8,128)(2,1)S(1)}, bf16[2,80,1152]{2,1,0:T(8,128)(2,1)S(1)}, u32[]{:S(2)}, u32[]{:S(2)}) collective-permute-start(bf16[2,80,1152]{2,1,0:T(8,128)(2,1)S(1)} %get-tuple-element.90.refs_4_), channel_id=1, source_target_pairs={{0,8},{8,0},{16,24},{24,16},{1,9},{9,1},{17,25},{25,17},{2,10},{10... | collective-permute-start | bytes 1105928 | tf_op jit(solution)/shard_map/ppermute | solution.py:255
  260.4 31.6 %collective-permute-start.24 = (bf16[2,80,1280]{2,1,0:T(8,128)(2,1)S(1)}, bf16[2,80,1280]{2,1,0:T(8,128)(2,1)S(1)}, u32[]{:S(2)}, u32[]{:S(2)}) collective-permute-start(bf16[2,80,1280]{2,1,0:T(8,128)(2,1)S(1)} %get-tuple-element.69.refs_0_), channel_id=1, source_target_pairs={{0,16},{8,24},{16,0},{24,8},{1,17},{9,25},{17,1},{25,9},{2,18},{10... | collective-permute-start | bytes 1228808 | tf_op jit(solution)/shard_map/ppermute | solution.py:255
  263.0 30.2 %collective-permute-start.40 = (bf16[2,80,1152]{2,1,0:T(8,128)(2,1)S(1)}, bf16[2,80,1152]{2,1,0:T(8,128)(2,1)S(1)}, u32[]{:S(2)}, u32[]{:S(2)}) collective-permute-start(bf16[2,80,1152]{2,1,0:T(8,128)(2,1)S(1)} %get-tuple-element.80.refs_4_), channel_id=1, source_target_pairs={{0,8},{8,0},{16,24},{24,16},{1,9},{9,1},{17,25},{25,17},{2,10},{10... | collective-permute-start | bytes 1105928 | tf_op jit(solution)/shard_map/ppermute | solution.py:255
  308.5 31.5 %collective-permute-start.41 = (bf16[2,80,1152]{2,1,0:T(8,128)(2,1)S(1)}, bf16[2,80,1152]{2,1,0:T(8,128)(2,1)S(1)}, u32[]{:S(2)}, u32[]{:S(2)}) collective-permute-start(bf16[2,80,1152]{2,1,0:T(8,128)(2,1)S(1)} %get-tuple-element.80.refs_4_), channel_id=1, source_target_pairs={{0,16},{8,24},{16,0},{24,8},{1,17},{9,25},{17,1},{25,9},{2,18},{10... | collective-permute-start | bytes 1105928 | tf_op jit(solution)/shard_map/ppermute | solution.py:255
  311.0 40.9 %collective-permute-start.37 = (bf16[2,80,1280]{2,1,0:T(8,128)(2,1)S(1)}, bf16[2,80,1280]{2,1,0:T(8,128)(2,1)S(1)}, u32[]{:S(2)}, u32[]{:S(2)}) collective-permute-start(bf16[2,80,1280]{2,1,0:T(8,128)(2,1)S(1)} %get-tuple-element.79.refs_0_), channel_id=1, source_target_pairs={{0,8},{8,0},{16,24},{24,16},{1,9},{9,1},{17,25},{25,17},{2,10},{10... | collective-permute-start | bytes 1228808 | tf_op jit(solution)/shard_map/ppermute | solution.py:255
  311.8 40.0 %collective-permute-start.52 = (bf16[2,80,1280]{2,1,0:T(8,128)(2,1)S(1)}, bf16[2,80,1280]{2,1,0:T(8,128)(2,1)S(1)}, u32[]{:S(2)}, u32[]{:S(2)}) collective-permute-start(bf16[2,80,1280]{2,1,0:T(8,128)(2,1)S(1)} %get-tuple-element.89.refs_0_), channel_id=1, source_target_pairs={{0,16},{8,24},{16,0},{24,8},{1,17},{9,25},{17,1},{25,9},{2,18},{10... | collective-permute-start | bytes 1228808 | tf_op jit(solution)/shard_map/ppermute | solution.py:255
  316.4 36.7 %collective-permute-start.42 = (bf16[2,80,1152]{2,1,0:T(8,128)(2,1)S(1)}, bf16[2,80,1152]{2,1,0:T(8,128)(2,1)S(1)}, u32[]{:S(2)}, u32[]{:S(2)}) collective-permute-start(bf16[2,80,1152]{2,1,0:T(8,128)(2,1)S(1)} %collective-permute-done.40.refs_5_), channel_id=1, source_target_pairs={{0,16},{8,24},{16,0},{24,8},{1,17},{9,25},{17,1},{25,9},{2,18},{10... | collective-permute-start | bytes 1105928 | tf_op jit(solution)/shard_map/ppermute | solution.py:255
  318.9 36.1 %collective-permute-start.39 = (bf16[2,80,1280]{2,1,0:T(8,128)(2,1)S(1)}, bf16[2,80,1280]{2,1,0:T(8,128)(2,1)S(1)}, u32[]{:S(2)}, u32[]{:S(2)}) collective-permute-start(bf16[2,80,1280]{2,1,0:T(8,128)(2,1)S(1)} %collective-permute-done.38.refs_2_), channel_id=1, source_target_pairs={{0,8},{8,0},{16,24},{24,16},{1,9},{9,1},{17,25},{25,17},{2,10},{10... | collective-permute-start | bytes 1228808 | tf_op jit(solution)/shard_map/ppermute | solution.py:255
  340.0 57.7 %collective-permute-start.29 = (bf16[256,2176]{1,0:T(8,128)(2,1)}, bf16[256,2176]{1,0:T(8,128)(2,1)}, u32[]{:S(2)}, u32[]{:S(2)}) collective-permute-start(bf16[256,2176]{1,0:T(8,128)(2,1)} %get-tuple-element.72), channel_id=1, source_target_pairs={{0,1},{1,0},{2,3},{3,2},{4,5},{5,4},{6,7},{7,6},{8,9},{9,8},{10,11... | collective-permute-start | bytes 3342344 | tf_op jit(solution)/shard_map/ppermute | solution.py:255
  399.3 50.1 %collective-permute-start.30 = (bf16[256,2176]{1,0:T(8,128)(2,1)S(1)}, bf16[256,2176]{1,0:T(8,128)(2,1)S(1)}, u32[]{:S(2)}, u32[]{:S(2)}) collective-permute-start(bf16[256,2176]{1,0:T(8,128)(2,1)S(1)} %add_convert_fusion.2), channel_id=1, source_target_pairs={{0,2},{1,3},{2,0},{3,1},{4,6},{5,7},{6,4},{7,5},{8,10},{9,11},{10,... | collective-permute-start | bytes 3342344 | tf_op jit(solution)/shard_map/ppermute | solution.py:255
  402.4 73.7 %collective-permute-start.44 = (bf16[256,2176]{1,0:T(8,128)(2,1)S(1)}, bf16[256,2176]{1,0:T(8,128)(2,1)S(1)}, u32[]{:S(2)}, u32[]{:S(2)}) collective-permute-start(bf16[256,2176]{1,0:T(8,128)(2,1)S(1)} %add_convert_fusion.1), channel_id=1, source_target_pairs={{0,4},{1,5},{2,6},{3,7},{4,0},{5,1},{6,2},{7,3},{8,12},{9,13},{10,... | collective-permute-start | bytes 3342344 | tf_op jit(solution)/shard_map/ppermute | solution.py:255
  403.7 96.6 %collective-permute-start.58 = (bf16[256,2176]{1,0:T(8,128)(2,1)S(1)}, bf16[256,2176]{1,0:T(8,128)(2,1)S(1)}, u32[]{:S(2)}, u32[]{:S(2)}) collective-permute-start(bf16[256,2176]{1,0:T(8,128)(2,1)S(1)} %add_convert_fusion), channel_id=1, source_target_pairs={{0,6},{1,7},{2,4},{3,5},{4,2},{5,3},{6,0},{7,1},{8,14},{9,15},{10,... | collective-permute-start | bytes 3342344 | tf_op jit(solution)/shard_map/ppermute | solution.py:255
  (66 other events, 1210.8 us)

commit v3 on v2

--- a/solution.py
+++ b/solution.py
@@ -43,7 +43,7 @@
     )
 
 
-def partial_kernel(count, me, same, other, slots, w_gate, w_up, w_down,
+def partial_kernel(count, me, same, other, slots, w_gate, w_up, w_down, after,
                    self_a, self_b, send_a, keep_a, send_b, keep_b):
     step = pl.program_id(0)
     part, half = step // count, step % count
@@ -87,7 +87,7 @@
         put_b(send_b, 1, half)
 
 
-def partial_sums(me, same, other, slots, w_gate, w_up, w_down, halves):
+def partial_sums(me, same, other, slots, w_gate, w_up, w_down, after, halves):
     count = len(halves)
     features, hidden = w_gate.shape[1:]
     rows, cols = 2 * CAP, 3 * hidden // 2
@@ -107,6 +107,7 @@
                 expert_block((features, hidden), halves),
                 expert_block((features, hidden), halves),
                 expert_block((hidden, features), halves),
+                pl.BlockSpec(memory_space=pl.ANY),
             ],
             out_specs=[whole(o.shape) for o in outs],
         ),
@@ -114,17 +115,17 @@
         compiler_params=pltpu.CompilerParams(vmem_limit_bytes=VMEM_BYTES),
         cost_estimate=pl.CostEstimate(
             flops=steps * rows * 10 * features * hidden,
-            bytes_accessed=steps * features * hidden * 6,
+            bytes_accessed=steps * features * hidden * 11,
             transcendentals=0,
         ),
-    )(me, same, other, slots, w_gate, w_up, w_down)
-
-
-def middle_kernel(me, self_a, self_b, first_a, first_b, last_a, last_b, slots, share,
-                  out_a, out_b):
+    )(me, same, other, slots, w_gate, w_up, w_down, after)
+
+
+def middle_kernel(me, self_a, self_b, first_a, first_b, last_a, last_b, slots, share, after, out):
     count, rows, cols = self_a.shape
     hidden = 2 * cols // 3
     half = hidden // 2
+    extra = 2 * EXPERTS
     for h in range(count):
         def total(own, first, last, lo, size):
             cut = pl.ds(lo, size)
@@ -152,53 +153,112 @@
             act_out = (act * fraction).astype(jnp.bfloat16)
             gate_out = (hidden_grad * up * sig * (1.0 + gate * (1.0 - sig))).astype(jnp.bfloat16)
             up_out = (hidden_grad * silu).astype(jnp.bfloat16)
-            out_a[h, :, pl.ds(lo, half)] = act_out
-            if side == 0:
-                out_a[h, :, pl.ds(hidden, half)] = gate_out
-            else:
-                out_b[h, :, pl.ds(0, half)] = gate_out
-            out_b[h, :, pl.ds(half + lo, half)] = up_out
-        lane = lax.broadcasted_iota(jnp.int32, (rows, 2 * EXPERTS), 1)
+            out[h, :, pl.ds(lo, half)] = act_out
+            out[h, :, pl.ds(hidden + side * (half + extra), half)] = gate_out
+            out[h, :, pl.ds(2 * hidden + extra + lo, half)] = up_out
+        lane = lax.broadcasted_iota(jnp.int32, (rows, extra), 1)
         high = grads.astype(jnp.bfloat16).astype(jnp.float32)
         spread = jnp.where(lane == me[0] + h, high, 0.0)
         spread = jnp.where(lane == me[0] + h + EXPERTS, grads - high, spread)
-        out_a[h, :, pl.ds(cols, 2 * EXPERTS)] = spread.astype(jnp.bfloat16)
-
-
-def middle(first, self_a, self_b, first_a, first_b, last_a, last_b, slots, share):
+        out[h, :, pl.ds(cols, extra)] = spread.astype(jnp.bfloat16)
+
+
+def first_of(shape, at):
+    return pl.BlockSpec((1,) + shape[1:], lambda g: (at,) + (0,) * (len(shape) - 1))
+
+
+def at_once(shape):
+    return pl.BlockSpec(shape, lambda g: (0,) * len(shape))
+
+
+def middle(first, self_a, self_b, first_a, first_b, last_a, last_b, slots, share, after):
     count, rows, cols = self_a.shape
-    outs = (
-        jax.ShapeDtypeStruct((count, rows, cols + 2 * EXPERTS), jnp.bfloat16),
-        jax.ShapeDtypeStruct(self_b.shape, jnp.bfloat16),
-    )
+    out = jax.ShapeDtypeStruct((count, rows, 2 * cols + 2 * EXPERTS), jnp.bfloat16)
     return pl.pallas_call(
         middle_kernel,
-        out_shape=outs,
-        in_specs=[pl.BlockSpec(memory_space=pltpu.SMEM)]
-        + [pl.BlockSpec(memory_space=pltpu.VMEM)] * 8,
-        out_specs=[pl.BlockSpec(memory_space=pltpu.VMEM)] * 2,
+        grid=(1,),
+        out_shape=out,
+        in_specs=[
+            pl.BlockSpec(memory_space=pltpu.SMEM),
+            at_once(self_a.shape),
+            at_once(self_b.shape),
+            first_of(first_a.shape, 0),
+            first_of(first_b.shape, 0),
+            at_once(last_a.shape),
+            at_once(last_b.shape),
+            at_once(slots.shape),
+            at_once(share.shape),
+            pl.BlockSpec(memory_space=pl.ANY),
+        ],
+        out_specs=at_once(out.shape),
         compiler_params=pltpu.CompilerParams(vmem_limit_bytes=VMEM_BYTES),
         cost_estimate=pl.CostEstimate(
-            flops=40 * self_a.size, bytes_accessed=14 * self_a.size, transcendentals=self_a.size
+            flops=40 * self_a.size, bytes_accessed=20 * self_a.size, transcendentals=self_a.size
         ),
-    )(first, self_a, self_b, first_a, first_b, last_a, last_b, slots, share)
+    )(first, self_a, self_b, first_a, first_b, last_a, last_b, slots, share, after)
+
+
+def between_kernel(adds, relays, *refs):
+    ins, outs = refs[: 4 * adds + 2 * relays], refs[4 * adds + 2 * relays + 1 :]
+    if adds:
+        for n in range(2):
+            outs[n][...] = (
+                ins[n][...].astype(jnp.float32) + ins[2 + n][0].astype(jnp.float32)
+            ).astype(jnp.bfloat16)
+    if relays:
+        rows_x, rows_y = ins[4 * adds :]
+        out_a, out_b = outs[2 * adds :]
+        cut = out_a.shape[2]
+        out_a[...] = rows_y[:, :, pl.ds(0, cut)]
+        out_b[...] = rows_x[:, :, pl.ds(cut, out_b.shape[2])]
+
+
+def between(add, relay, after):
+    ins, specs, outs = [], [], []
+    if add is not None:
+        keep_a, keep_b, first_a, first_b = add
+        ins += [keep_a, keep_b, first_a, first_b]
+        specs += [at_once(keep_a.shape), at_once(keep_b.shape)]
+        specs += [first_of(first_a.shape, 1), first_of(first_b.shape, 1)]
+        outs += [keep_a.shape, keep_b.shape]
+    if relay is not None:
+        ins += list(relay)
+        specs += [at_once(r.shape) for r in relay]
+        count, rows, width = relay[0].shape
+        cols = (width - 2 * EXPERTS) // 2
+        outs += [(count, rows, cols + 2 * EXPERTS), (count, rows, cols)]
+    size = sum(i.size for i in ins)
+    return pl.pallas_call(
+        functools.partial(between_kernel, int(add is not None), int(relay is not None)),
+        grid=(1,),
+        out_shape=[jax.ShapeDtypeStruct(o, jnp.bfloat16) for o in outs],
+        in_specs=specs + [pl.BlockSpec(memory_space=pl.ANY)],
+        out_specs=[at_once(o) for o in outs],
+        compiler_params=pltpu.CompilerParams(vmem_limit_bytes=VMEM_BYTES),
+        cost_estimate=pl.CostEstimate(flops=size, bytes_accessed=4 * size, transcendentals=0),
+    )(*ins, after)
 
 
 def combine_kernel(count, me, *refs):
-    lefts, rights = refs[0:4], refs[4:8]
-    slots, w_gate, w_up, w_down, same, other, rows_in, hots, outs = refs[8:]
+    across_a, across_b = refs[3:5]
+    slots, w_gate, w_up, w_down, _, same, other, rows_in, hots, outs = refs[5:]
     step = pl.program_id(0)
     part, half = step // count, step % count
-    rows, cols = rows_in.shape[0], rights[0].shape[2]
+    rows, cols = rows_in.shape[0], across_b.shape[2]
+    extra = pl.ds(cols, 2 * EXPERTS)
     hidden = w_gate.shape[2]
     features = w_gate.shape[1]
     at = pl.ds(pl.multiple_of(step * rows, 16), rows)
     for v in range(4):
         @pl.when(part == v)
         def _():
-            rows_in[:, pl.ds(0, cols)] = lefts[v][half, :, pl.ds(0, cols)]
-            rows_in[:, pl.ds(cols, cols)] = rights[v][half]
-            outs[at, pl.ds(2 * features, 2 * EXPERTS)] = lefts[v][half, :, pl.ds(cols, 2 * EXPERTS)]
+            left = refs[v] if v < 3 else across_a
+            rows_in[:, pl.ds(0, cols)] = left[half, :, pl.ds(0, cols)]
+            outs[at, pl.ds(2 * features, 2 * EXPERTS)] = left[half, :, extra]
+            if v < 3:
+                rows_in[:, pl.ds(cols, cols)] = left[half, :, pl.ds(cols + 2 * EXPERTS, cols)]
+            else:
+                rows_in[:, pl.ds(cols, cols)] = across_b[half]
     outs[at, pl.ds(0, features)] = dot_nn(rows_in[:, pl.ds(0, hidden)], w_down[0]).astype(jnp.bfloat16)
     outs[at, pl.ds(features, features)] = (
         dot_nt(rows_in[:, pl.ds(hidden, hidden)], w_gate[0])
@@ -213,7 +273,7 @@
             ref[...] = dot_tn(hots[:, pl.ds(lo, tokens)], outs[...]).astype(jnp.bfloat16)
 
 
-def combine(me, lefts, rights, slots, w_gate, w_up, w_down, halves):
+def combine(me, given, slots, w_gate, w_up, w_down, after, halves):
     count = len(halves)
     features, hidden = w_gate.shape[1:]
     rows = 2 * CAP
@@ -226,12 +286,13 @@
         grid_spec=pltpu.PrefetchScalarGridSpec(
             num_scalar_prefetch=1,
             grid=(steps,),
-            in_specs=[whole(a.shape) for a in (*lefts, *rights)]
+            in_specs=[whole(a.shape) for a in given]
             + [
                 expert_block(slots.shape[1:], halves),
                 expert_block((features, hidden), halves),
                 expert_block((features, hidden), halves),
                 expert_block((hidden, features), halves),
+                pl.BlockSpec(memory_space=pl.ANY),
             ],
             out_specs=[whole(out.shape)] * 2,
             scratch_shapes=[
@@ -244,10 +305,10 @@
         compiler_params=pltpu.CompilerParams(vmem_limit_bytes=VMEM_BYTES),
         cost_estimate=pl.CostEstimate(
             flops=steps * rows * 10 * features * hidden,
-            bytes_accessed=steps * features * hidden * 6,
+            bytes_accessed=steps * features * hidden * 11,
             transcendentals=0,
         ),
-    )(me, *lefts, *rights, slots, w_gate, w_up, w_down)
+    )(me, *given, slots, w_gate, w_up, w_down, after)
 
 
 def swap(value, axis, bits):
@@ -267,7 +328,8 @@
     ratio_weight = jnp.minimum(jnp.exp(log_ratio), clip_ratio)
     weighted = (ratio_weight[:, None] * cotangent.astype(jnp.float32)).astype(jnp.bfloat16)
     payload = jnp.concatenate([tokens, weighted], axis=1)
-    sames = [payload] + [swap(payload, "expert", 2 * o) for o in range(1, chips)]
+    across = swap(payload, "expert", 4)
+    sames = [payload, swap(payload, "expert", 2), across, swap(across, "expert", 2)]
     others = [swap(p, "expert", 1) for p in sames]
 
     local = mine * per_device + jnp.arange(per_device, dtype=jnp.int32)
@@ -295,33 +357,74 @@
     far_slots, far_share = placed(far)
 
     weights = (gate_weight, up_weight, down_weight)
-    chunks = [(0, (0,))] + [(o, (0, 1)) for o in range(1, chips)] + [(0, (1,))]
-    totals = []
-    for o, halves in chunks:
-        slot = far_slots[:, o - 1] if o else near_slots[:, 0]
-        part = far_share[:, o - 1] if o else near_share[:, 0]
-        self_a, self_b, send_a, keep_a, send_b, keep_b = partial_sums(
-            me, sames[o], others[o], slot, *weights, halves
-        )
-        first_a, first_b = swap(send_a, "dp", 1), swap(send_b, "dp", 2)
-        last_a = swap(keep_a + first_a[1], "dp", 2)
-        last_b = swap(keep_b + first_b[1], "dp", 1)
+    chunks = [(0, (0,)), (2, (0, 1)), (3, (0, 1)), (1, (0, 1)), (0, (1,))]
+    count = len(chunks)
+    sums, adds, sent, got, relayed, totals = {}, {}, {}, {}, {}, []
+    after = near_slots
+
+    def slots_of(k):
+        o = chunks[k][0]
+        return far_slots[:, o - 1] if o else near_slots[:, 0]
+
+    def share_of(k):
+        o = chunks[k][0]
+        return far_share[:, o - 1] if o else near_share[:, 0]
+
+    def start_rows(k, after):
+        o, halves = chunks[k]
+        out = partial_sums(me, sames[o], others[o], slots_of(k), *weights, after, halves)
+        self_a, self_b, send_a, keep_a, send_b, keep_b = out
+        firsts = swap(send_a, "dp", 1), swap(send_b, "dp", 2)
+        sums[k] = self_a, self_b, *firsts
+        adds[k] = keep_a, keep_b, *firsts
+        return self_a
+
+    def move(k, r, after):
+        outs = between(adds.get(k), got.get(r), after)
+        if k in adds:
+            last_a, last_b = swap(outs[0], "dp", 2), swap(outs[1], "dp", 1)
+            sums[k] = (*sums[k], last_a, last_b)
+        if r in got:
+            relayed[r] = swap(outs[-2], "dp", 1), swap(outs[-1], "dp", 2)
+        return outs[0]
+
+    def turn_rows(k, after):
+        halves = chunks[k][1]
         first = 2 * member + halves[0]
-        own_slot = lax.dynamic_slice_in_dim(slot, first, len(halves), 0)
-        own_share = lax.dynamic_slice_in_dim(part, first, len(halves), 0)
+        own_slot = lax.dynamic_slice_in_dim(slots_of(k), first, len(halves), 0)
+        own_share = lax.dynamic_slice_in_dim(share_of(k), first, len(halves), 0)
         expert = (mine * per_device + first).astype(jnp.int32).reshape(1)
-        a, b = middle(
-            expert, self_a, self_b, first_a, first_b, last_a, last_b, own_slot, own_share
-        )
-        a_x, a_y, b_x, b_y = swap(a, "dp", 1), swap(a, "dp", 2), swap(b, "dp", 1), swap(b, "dp", 2)
-        a_d, b_d = swap(a_y, "dp", 1), swap(b_x, "dp", 2)
-        same, other = combine(
-            me, (a, a_x, a_y, a_d), (b, b_x, b_y, b_d), slot, *weights, halves
-        )
+        sent[k] = middle(expert, *sums[k], own_slot, own_share, after)
+        got[k] = swap(sent[k], "dp", 1), swap(sent[k], "dp", 2)
+        return sent[k]
+
+    def finish_rows(k, after):
+        o, halves = chunks[k]
+        given = (sent[k], *got[k], *relayed[k])
+        same, other = combine(me, given, slots_of(k), *weights, after, halves)
         both = same.astype(jnp.float32) + swap(other, "expert", 1).astype(jnp.float32)
         if o:
             both = swap(both.astype(jnp.bfloat16), "expert", 2 * o)
         totals.append(both)
+        return same
+
+    after = start_rows(0, after)
+    after = move(0, None, after)
+    after = turn_rows(0, after)
+    after = move(None, 0, after)
+    for k in range(1, count):
+        after = start_rows(k, after)
+        if k == 1:
+            after = finish_rows(0, after)
+        else:
+            after = turn_rows(k - 1, after)
+            if k > 2:
+                after = finish_rows(k - 2, after)
+        after = move(k, k - 1 if k > 1 else None, after)
+    after = turn_rows(count - 1, after)
+    after = finish_rows(count - 2, after)
+    after = move(None, count - 1, after)
+    after = finish_rows(count - 1, after)
     total = sum(t.astype(jnp.float32) for t in totals)
     grads = total[:, 2 * features : 2 * features + EXPERTS] + total[:, 2 * features + EXPERTS :]
     hit = routes[:, :, None] == jnp.arange(EXPERTS, dtype=jnp.int32)

time: 504 us -> 458 us (0.909)
  waiting for transfers between devices: 255 us -> 195 us
  local copies, waits for them, and re-layouts: 3.54 us -> 20.3 us
  starting transfers between devices: 73.9 us -> 57.8 us
  Pallas kernels: 160 us -> 174 us
    ppermute x70 -> x60, waiting for transfers between devices: 255 us -> 195 us  [swap(): return lax.ppermute(value, axis, [(n, n ^ bits) for n in range(count)])]
    ppermute x70 -> x60, starting transfers between devices: 73.9 us -> 57.8 us  [swap(): return lax.ppermute(value, axis, [(n, n ^ bits) for n in range(count)])]
    unnamed x40 -> x92, local copies, waits for them, and re-layouts: 2.09 us -> 15.5 us
    pallas_call x5 -> x12, Pallas kernels: 2.56 us -> 12.6 us  [the longest x7 7 us: between(): pl.pallas_call(functools.partial(between_kernel, int(add is not None), in...]
  transfers between devices with their start and end apart: 70 -> 60, of which waited for: 22 -> 17; matrix products, arithmetic and copies ran while one was open for 1% -> 2% of each run, Pallas kernels for 32% -> 38%
where the time goes in v3:
time: 458 us; the launch traced here: 457 us
  waiting for transfers between devices  195 us (43%)
  Pallas kernels  174 us (38%)
  starting transfers between devices  57.8 us (13%)
  local copies, waits for them, and re-layouts  20.3 us (4%)
  other arithmetic  8.71 us (2%)
    ppermute x60, waiting for transfers between devices, swap(): return lax.ppermute(value, axis, [(n, n ^ bits) for n in range(count)])  195 us
    pallas_call x5, Pallas kernels, combine(): pl.pallas_call(functools.partial(combine_kernel, count), grid_spec=pltpu....  84 us
    pallas_call x5, Pallas kernels, partial_sums(): pl.pallas_call(functools.partial(partial_kernel, count), grid_spec=pltpu....  77 us
    ppermute x60, starting transfers between devices, swap(): return lax.ppermute(value, axis, [(n, n ^ bits) for n in range(count)])  57.8 us
    unnamed x92, local copies, waits for them, and re-layouts  15.5 us
  transfers between devices with their start and end apart: 60, of which 17 were waited for; matrix products, arithmetic and copies ran while one was open for 2% of the time, Pallas kernels for 38%

profile of v3, /device:TPU:8, one launch (start us, length us, event | category | flops | bytes accessed | tf_op | source)
XLA Modules:
  0.0 457.2 jit_solution(5162272465970528904)
XLA Ops:
  7.6 3.0 collective-permute-start.10
  11.6 9.7 %shard_map.103 = (bf16[1,80,1152]{2,1,0:T(8,128)(2,1)S(1)}, bf16[1,80,1152]{2,1,0:T(8,128)(2,1)S(1)}, bf16[2,1,80,1152]{3,2,1,0:T(8,128)(2,1)S(1)}, bf16[1,80,11...) custom-call(s32[1]{0:T(128)} %bitcast.me, ...), custom_call_target="tpu_custom_call" | custom-call | flops 2516582400 | bytes 34603008 | tf_op jit(solution)/shard_map/pallas_call | solution.py:98
  24.3 31.3 %collective-permute-done.10.same = bf16[256,2048]{1,0:T(8,128)(2,1)} collective-permute-done((bf16[256,2048]{1,0:T(8,128)(2,1)S(1)}, bf16[256,2048]{1,0:T(8,128)(2,1)}, u32[]{:S(2)}, u32[]{:S(2)}) %collective-permute-start.10) | collective-permute-done | bytes 1048608 | tf_op jit(solution)/shard_map/ppermute | solution.py:316
  63.1 3.1 collective-permute-done.4.last_a
  74.9 7.5 %collective-permute-done.6.refs_0_.refs_1_ = bf16[1,80,2432]{2,1,0:T(8,128)(2,1)S(1)} collective-permute-done((bf16[1,80,2432]{2,1,0:T(8,128)(2,1)S(1)}, bf16[1,80,2432]{2,1,0:T(8,128)(2,1)S(1)}, u32[]{:S(2)}, u32[]{:S(2)}) %collective-permute-start.6) | collective-permute-done | bytes 389152 | tf_op jit(solution)/shard_map/ppermute | solution.py:316
  85.1 20.0 %shard_map.107 = (bf16[2,80,1152]{2,1,0:T(8,128)(2,1)S(1)}, bf16[2,80,1152]{2,1,0:T(8,128)(2,1)S(1)}, bf16[2,2,80,1152]{3,2,1,0:T(8,128)(2,1)}, bf16[2,80,1152]{...) custom-call(s32[1]{0:T(128)} %bitcast.me, ...), custom_call_target="tpu_custom_call" | custom-call | flops 5033164800 | bytes 69206016 | tf_op jit(solution)/shard_map/pallas_call | solution.py:98
  112.5 18.2 %collective-permute-done.9.refs_4_ = bf16[1,80,1152]{2,1,0:T(8,128)(2,1)S(1)} collective-permute-done((bf16[1,80,1152]{2,1,0:T(8,128)(2,1)}, bf16[1,80,1152]{2,1,0:T(8,128)(2,1)S(1)}, u32[]{:S(2)}, u32[]{:S(2)}) %collective-permute-start.9) | collective-permute-done | bytes 184352 | tf_op jit(solution)/shard_map/ppermute | solution.py:316
  134.8 11.6 %shard_map.108 = (bf16[256,2176]{1,0:T(8,128)(2,1)S(1)}, bf16[256,2176]{1,0:T(8,128)(2,1)}) custom-call(s32[1]{0:T(128)} %bitcast.me, bf16[1,80,2432]{2,1,0:T(8,128)(2,1)S(1)} %copy-done.4, bf16[1,80,2432]{2,1,0:T(8,128)(2,1)S(1)} %copy-done.16, bf16[1,80,2432]{2,1,0:T(8,128)(2,1)S(1)} %copy-done.18, ...), custom_call_target="tpu_custom_call" | custom-call | flops 2516582400 | bytes 34603008 | tf_op jit(solution)/shard_map/pallas_call | solution.py:284
  150.2 18.9 %shard_map.110 = (bf16[2,80,1152]{2,1,0:T(8,128)(2,1)S(1)}, bf16[2,80,1152]{2,1,0:T(8,128)(2,1)S(1)}, bf16[2,2,80,1152]{3,2,1,0:T(8,128)(2,1)S(1)}, bf16[2,80,11...) custom-call(s32[1]{0:T(128)} %bitcast.me, ...), custom_call_target="tpu_custom_call" | custom-call | flops 5033164800 | bytes 69206016 | tf_op jit(solution)/shard_map/pallas_call | solution.py:98
  175.7 30.3 %collective-permute-done.25.refs_2_.first_a = bf16[2,2,80,1152]{3,2,1,0:T(8,128)(2,1)S(1)} collective-permute-done((bf16[2,2,80,1152]{3,2,1,0:T(8,128)(2,1)S(1)}, bf16[2,2,80,1152]{3,2,1,0:T(8,128)(2,1)S(1)}, u32[]{:S(2)}, u32[]{:S(2)}) %collective-permute-start.25) | collective-permute-done | bytes 737312 | tf_op jit(solution)/shard_map/ppermute | solution.py:316
  207.3 2.2 shard_map.112
  213.6 18.8 %shard_map.113 = (bf16[2,80,1152]{2,1,0:T(8,128)(2,1)S(1)}, bf16[2,80,1152]{2,1,0:T(8,128)(2,1)S(1)}, bf16[2,2,80,1152]{3,2,1,0:T(8,128)(2,1)S(1)}, bf16[2,80,11...) custom-call(s32[1]{0:T(128)} %bitcast.me, ...), custom_call_target="tpu_custom_call" | custom-call | flops 5033164800 | bytes 69206016 | tf_op jit(solution)/shard_map/pallas_call | solution.py:98
  237.3 20.6 %shard_map.115 = (bf16[256,2176]{1,0:T(8,128)(2,1)}, bf16[256,2176]{1,0:T(8,128)(2,1)}) custom-call(s32[1]{0:T(128)} %bitcast.me, bf16[2,80,2432]{2,1,0:T(8,128)(2,1)S(1)} %copy-done.1, bf16[2,80,2432]{2,1,0:T(8,128)(2,1)S(1)} %copy-done.12, bf16[2,80,2432]{2,1,0:T(8,128)(2,1)S(1)} %copy-done.14, bf16[2,80,1280]{2,1,0:T(8,128)(2,1)S(1)} %collective-permute-done.27.refs_3_, ...), custom_call_target="tpu_custom_call" | custom-call | flops 5033164800 | bytes 69206016 | tf_op jit(solution)/shard_map/pallas_call | solution.py:284
  257.9 8.1 %collective-permute-done.37.refs_2_.first_a = bf16[2,2,80,1152]{3,2,1,0:T(8,128)(2,1)S(1)} collective-permute-done((bf16[2,2,80,1152]{3,2,1,0:T(8,128)(2,1)S(1)}, bf16[2,2,80,1152]{3,2,1,0:T(8,128)(2,1)S(1)}, u32[]{:S(2)}, u32[]{:S(2)}) %collective-permute-start.37) | collective-permute-done | bytes 737312 | tf_op jit(solution)/shard_map/ppermute | solution.py:316
  274.7 9.6 %shard_map.117 = (bf16[1,80,1152]{2,1,0:T(8,128)(2,1)S(1)}, bf16[1,80,1152]{2,1,0:T(8,128)(2,1)S(1)}, bf16[2,1,80,1152]{3,2,1,0:T(8,128)(2,1)S(1)}, bf16[1,80,11...) custom-call(s32[1]{0:T(128)} %bitcast.me, ...), custom_call_target="tpu_custom_call" | custom-call | flops 2516582400 | bytes 34603008 | tf_op jit(solution)/shard_map/pallas_call | solution.py:98
  290.8 20.4 %shard_map.119 = (bf16[256,2176]{1,0:T(8,128)(2,1)}, bf16[256,2176]{1,0:T(8,128)(2,1)}) custom-call(s32[1]{0:T(128)} %bitcast.me, bf16[2,80,2432]{2,1,0:T(8,128)(2,1)S(1)} %shard_map.114.refs_9_.refs_0_, bf16[2,80,2432]{2,1,0:T(8,128)(2,1)S(1)} %copy-done.6, bf16[2,80,2432]{2,1,0:T(8,128)(2,1)S(1)} %copy-done.8, ...), custom_call_target="tpu_custom_call" | custom-call | flops 5033164800 | bytes 69206016 | tf_op jit(solution)/shard_map/pallas_call | solution.py:284
  316.6 9.3 %collective-permute-done.51.last_a = bf16[1,80,1152]{2,1,0:T(8,128)(2,1)} collective-permute-done((bf16[1,80,1152]{2,1,0:T(8,128)(2,1)}, bf16[1,80,1152]{2,1,0:T(8,128)(2,1)}, u32[]{:S(2)}, u32[]{:S(2)}) %collective-permute-start.51) | collective-permute-done | bytes 184352 | tf_op jit(solution)/shard_map/ppermute | solution.py:316
  331.2 20.9 %shard_map.122 = (bf16[256,2176]{1,0:T(8,128)(2,1)}, bf16[256,2176]{1,0:T(8,128)(2,1)}) custom-call(s32[1]{0:T(128)} %bitcast.me, bf16[2,80,2432]{2,1,0:T(8,128)(2,1)S(1)} %shard_map.118.refs_9_.refs_0_, bf16[2,80,2432]{2,1,0:T(8,128)(2,1)S(1)} %collective-permute-done.45.refs_4_.refs_1_, bf16[2,80,2432]{2,1,0:T(8,128)(2,1)S(1)} %copy-done.10, ...), custom_call_target="tpu_custom_call" | custom-call | flops 5033164800 | bytes 69206016 | tf_op jit(solution)/shard_map/pallas_call | solution.py:284
  357.7 5.0 %collective-permute-done.58.refs_4_ = bf16[1,80,1152]{2,1,0:T(8,128)(2,1)S(1)} collective-permute-done((bf16[1,80,1152]{2,1,0:T(8,128)(2,1)S(1)}, bf16[1,80,1152]{2,1,0:T(8,128)(2,1)S(1)}, u32[]{:S(2)}, u32[]{:S(2)}) %collective-permute-start.58) | collective-permute-done | bytes 184352 | tf_op jit(solution)/shard_map/ppermute | solution.py:316
  363.6 10.5 %shard_map.124 = (bf16[256,2176]{1,0:T(8,128)(2,1)S(1)}, bf16[256,2176]{1,0:T(8,128)(2,1)S(1)}) custom-call(s32[1]{0:T(128)} %bitcast.me, bf16[1,80,2432]{2,1,0:T(8,128)(2,1)S(1)} %shard_map.121.refs_9_.refs_0_, bf16[1,80,2432]{2,1,0:T(8,128)(2,1)S(1)} %collective-permute-done.55.refs_0_.refs_1_, ...), custom_call_target="tpu_custom_call" | custom-call | flops 2516582400 | bytes 34603008 | tf_op jit(solution)/shard_map/pallas_call | solution.py:284
  374.5 2.0 collective-permute-start.54
  376.5 51.7 %collective-permute-done.34 = bf16[256,2176]{1,0:T(8,128)(2,1)S(1)} collective-permute-done((bf16[256,2176]{1,0:T(8,128)(2,1)S(1)}, bf16[256,2176]{1,0:T(8,128)(2,1)S(1)}, u32[]{:S(2)}, u32[]{:S(2)}) %collective-permute-start.34) | collective-permute-done | bytes 1114144 | tf_op jit(solution)/shard_map/ppermute | solution.py:316
  428.2 24.7 %collective-permute-done.44 = bf16[256,2176]{1,0:T(8,128)(2,1)S(1)} collective-permute-done((bf16[256,2176]{1,0:T(8,128)(2,1)S(1)}, bf16[256,2176]{1,0:T(8,128)(2,1)S(1)}, u32[]{:S(2)}, u32[]{:S(2)}) %collective-permute-start.44) | collective-permute-done | bytes 1114144 | tf_op jit(solution)/shard_map/ppermute | solution.py:316
  452.9 2.3 fusion.20
  (256 shorter events, 96.2 us)
Async XLA Ops:
  7.6 48.0 %collective-permute-start.10 = (bf16[256,2048]{1,0:T(8,128)(2,1)S(1)}, bf16[256,2048]{1,0:T(8,128)(2,1)}, u32[]{:S(2)}, u32[]{:S(2)}) collective-permute-start(bf16[256,2048]{1,0:T(8,128)(2,1)S(1)} %pad_maximum_fusion.same), channel_id=1, source_target_pairs={{0,4},{1,5},{2,6},{3,7},{4,0},{5,1},{6,2},{7,3},{8,12},{9,13},{10,... | collective-permute-start | bytes 3145736 | tf_op jit(solution)/shard_map/ppermute | solution.py:316
  11.0 99.8 %collective-permute-start.31 = (bf16[256,2048]{1,0:T(8,128)(2,1)S(1)}, bf16[256,2048]{1,0:T(8,128)(2,1)}, u32[]{:S(2)}, u32[]{:S(2)}) collective-permute-start(bf16[256,2048]{1,0:T(8,128)(2,1)S(1)} %pad_maximum_fusion.same), channel_id=1, source_target_pairs={{0,2},{1,3},{2,0},{3,1},{4,6},{5,7},{6,4},{7,5},{8,10},{9,11},{10,... | collective-permute-start | bytes 3145736 | tf_op jit(solution)/shard_map/ppermute | solution.py:316
  21.3 36.4 %collective-permute-start.2 = (bf16[2,1,80,1152]{3,2,1,0:T(8,128)(2,1)S(1)}, bf16[2,1,80,1152]{3,2,1,0:T(8,128)(2,1)S(1)}, u32[]{:S(2)}, u32[]{:S(2)}) collective-permute-start(bf16[2,1,80,1152]{3,2,1,0:T(8,128)(2,1)S(1)} %get-tuple-element.65), channel_id=1, source_target_pairs={{0,8},{8,0},{16,24},{24,16},{1,9},{9,1},{17,25},{25,17},{2,10},{10... | collective-permute-start | bytes 1105928 | tf_op jit(solution)/shard_map/ppermute | solution.py:316
  22.8 34.8 %collective-permute-start.3 = (bf16[2,1,80,1152]{3,2,1,0:T(8,128)(2,1)S(1)}, bf16[2,1,80,1152]{3,2,1,0:T(8,128)(2,1)S(1)}, u32[]{:S(2)}, u32[]{:S(2)}) collective-permute-start(bf16[2,1,80,1152]{3,2,1,0:T(8,128)(2,1)S(1)} %get-tuple-element.66), channel_id=1, source_target_pairs={{0,16},{8,24},{16,0},{24,8},{1,17},{9,25},{17,1},{25,9},{2,18},{10... | collective-permute-start | bytes 1105928 | tf_op jit(solution)/shard_map/ppermute | solution.py:316
  55.6 29.5 %collective-permute-start.21 = (bf16[256,2048]{1,0:T(8,128)(2,1)}, bf16[256,2048]{1,0:T(8,128)(2,1)}, u32[]{:S(2)}, u32[]{:S(2)}) collective-permute-start(bf16[256,2048]{1,0:T(8,128)(2,1)} %collective-permute-done.10.same), channel_id=1, source_target_pairs={{0,2},{1,3},{2,0},{3,1},{4,6},{5,7},{6,4},{7,5},{8,10},{9,11},{10,... | collective-permute-start | bytes 3145736 | tf_op jit(solution)/shard_map/ppermute | solution.py:316
  85.1 65.1 %collective-permute-start.22 = (bf16[256,2048]{1,0:T(8,128)(2,1)}, bf16[256,2048]{1,0:T(8,128)(2,1)}, u32[]{:S(2)}, u32[]{:S(2)}) collective-permute-start(bf16[256,2048]{1,0:T(8,128)(2,1)} %collective-permute-done.21.same), channel_id=1, source_target_pairs={{0,1},{1,0},{2,3},{3,2},{4,5},{5,4},{6,7},{7,6},{8,9},{9,8},{10,11... | collective-permute-start | bytes 3145736 | tf_op jit(solution)/shard_map/ppermute | solution.py:316
  107.4 39.0 %collective-permute-start.17 = (bf16[2,2,80,1152]{3,2,1,0:T(8,128)(2,1)}, bf16[2,2,80,1152]{3,2,1,0:T(8,128)(2,1)}, u32[]{:S(2)}, u32[]{:S(2)}) collective-permute-start(bf16[2,2,80,1152]{3,2,1,0:T(8,128)(2,1)} %get-tuple-element.77), channel_id=1, source_target_pairs={{0,8},{8,0},{16,24},{24,16},{1,9},{9,1},{17,25},{25,17},{2,10},{10... | collective-permute-start | bytes 2211848 | tf_op jit(solution)/shard_map/ppermute | solution.py:316
  107.9 38.5 %collective-permute-start.18 = (bf16[2,2,80,1152]{3,2,1,0:T(8,128)(2,1)}, bf16[2,2,80,1152]{3,2,1,0:T(8,128)(2,1)}, u32[]{:S(2)}, u32[]{:S(2)}) collective-permute-start(bf16[2,2,80,1152]{3,2,1,0:T(8,128)(2,1)} %get-tuple-element.78), channel_id=1, source_target_pairs={{0,16},{8,24},{16,0},{24,8},{1,17},{9,25},{17,1},{25,9},{2,18},{10... | collective-permute-start | bytes 2211848 | tf_op jit(solution)/shard_map/ppermute | solution.py:316
  130.6 83.0 %collective-permute-start.32 = (bf16[256,2048]{1,0:T(8,128)(2,1)}, bf16[256,2048]{1,0:T(8,128)(2,1)}, u32[]{:S(2)}, u32[]{:S(2)}) collective-permute-start(bf16[256,2048]{1,0:T(8,128)(2,1)} %collective-permute-done.31.same), channel_id=1, source_target_pairs={{0,1},{1,0},{2,3},{3,2},{4,5},{5,4},{6,7},{7,6},{8,9},{9,8},{10,11... | collective-permute-start | bytes 3145736 | tf_op jit(solution)/shard_map/ppermute | solution.py:316
  170.9 35.3 %collective-permute-start.23 = (bf16[2,80,2432]{2,1,0:T(8,128)(2,1)S(1)}, bf16[2,80,2432]{2,1,0:T(8,128)(2,1)S(1)}, u32[]{:S(2)}, u32[]{:S(2)}) collective-permute-start(bf16[2,80,2432]{2,1,0:T(8,128)(2,1)S(1)} %shard_map.111.refs_6_.refs_0_), channel_id=1, source_target_pairs={{0,8},{8,0},{16,24},{24,16},{1,9},{9,1},{17,25},{25,17},{2,10},{10... | collective-permute-start | bytes 2334728 | tf_op jit(solution)/shard_map/ppermute | solution.py:316
  171.6 34.6 %collective-permute-start.24 = (bf16[2,80,2432]{2,1,0:T(8,128)(2,1)S(1)}, bf16[2,80,2432]{2,1,0:T(8,128)(2,1)S(1)}, u32[]{:S(2)}, u32[]{:S(2)}) collective-permute-start(bf16[2,80,2432]{2,1,0:T(8,128)(2,1)S(1)} %shard_map.111.refs_6_.refs_0_), channel_id=1, source_target_pairs={{0,16},{8,24},{16,0},{24,8},{1,17},{9,25},{17,1},{25,9},{2,18},{10... | collective-permute-start | bytes 2334728 | tf_op jit(solution)/shard_map/ppermute | solution.py:316
  172.6 33.4 %collective-permute-start.25 = (bf16[2,2,80,1152]{3,2,1,0:T(8,128)(2,1)S(1)}, bf16[2,2,80,1152]{3,2,1,0:T(8,128)(2,1)S(1)}, u32[]{:S(2)}, u32[]{:S(2)}) collective-permute-start(bf16[2,2,80,1152]{3,2,1,0:T(8,128)(2,1)S(1)} %get-tuple-element.86), channel_id=1, source_target_pairs={{0,8},{8,0},{16,24},{24,16},{1,9},{9,1},{17,25},{25,17},{2,10},{10... | collective-permute-start | bytes 2211848 | tf_op jit(solution)/shard_map/ppermute | solution.py:316
  173.9 32.3 %collective-permute-start.26 = (bf16[2,2,80,1152]{3,2,1,0:T(8,128)(2,1)S(1)}, bf16[2,2,80,1152]{3,2,1,0:T(8,128)(2,1)S(1)}, u32[]{:S(2)}, u32[]{:S(2)}) collective-permute-start(bf16[2,2,80,1152]{3,2,1,0:T(8,128)(2,1)S(1)} %get-tuple-element.87), channel_id=1, source_target_pairs={{0,16},{8,24},{16,0},{24,8},{1,17},{9,25},{17,1},{25,9},{2,18},{10... | collective-permute-start | bytes 2211848 | tf_op jit(solution)/shard_map/ppermute | solution.py:316
  233.2 34.0 %collective-permute-start.35 = (bf16[2,80,2432]{2,1,0:T(8,128)(2,1)S(1)}, bf16[2,80,2432]{2,1,0:T(8,128)(2,1)S(1)}, u32[]{:S(2)}, u32[]{:S(2)}) collective-permute-start(bf16[2,80,2432]{2,1,0:T(8,128)(2,1)S(1)} %shard_map.114.refs_9_.refs_0_), channel_id=1, source_target_pairs={{0,8},{8,0},{16,24},{24,16},{1,9},{9,1},{17,25},{25,17},{2,10},{10... | collective-permute-start | bytes 2334728 | tf_op jit(solution)/shard_map/ppermute | solution.py:316
  234.7 32.4 %collective-permute-start.36 = (bf16[2,80,2432]{2,1,0:T(8,128)(2,1)S(1)}, bf16[2,80,2432]{2,1,0:T(8,128)(2,1)S(1)}, u32[]{:S(2)}, u32[]{:S(2)}) collective-permute-start(bf16[2,80,2432]{2,1,0:T(8,128)(2,1)S(1)} %shard_map.114.refs_9_.refs_0_), channel_id=1, source_target_pairs={{0,16},{8,24},{16,0},{24,8},{1,17},{9,25},{17,1},{25,9},{2,18},{10... | collective-permute-start | bytes 2334728 | tf_op jit(solution)/shard_map/ppermute | solution.py:316
  235.6 30.3 %collective-permute-start.37 = (bf16[2,2,80,1152]{3,2,1,0:T(8,128)(2,1)S(1)}, bf16[2,2,80,1152]{3,2,1,0:T(8,128)(2,1)S(1)}, u32[]{:S(2)}, u32[]{:S(2)}) collective-permute-start(bf16[2,2,80,1152]{3,2,1,0:T(8,128)(2,1)S(1)} %get-tuple-element.98), channel_id=1, source_target_pairs={{0,8},{8,0},{16,24},{24,16},{1,9},{9,1},{17,25},{25,17},{2,10},{10... | collective-permute-start | bytes 2211848 | tf_op jit(solution)/shard_map/ppermute | solution.py:316
  236.2 30.9 %collective-permute-start.38 = (bf16[2,2,80,1152]{3,2,1,0:T(8,128)(2,1)S(1)}, bf16[2,2,80,1152]{3,2,1,0:T(8,128)(2,1)S(1)}, u32[]{:S(2)}, u32[]{:S(2)}) collective-permute-start(bf16[2,2,80,1152]{3,2,1,0:T(8,128)(2,1)S(1)} %get-tuple-element.99), channel_id=1, source_target_pairs={{0,16},{8,24},{16,0},{24,8},{1,17},{9,25},{17,1},{25,9},{2,18},{10... | collective-permute-start | bytes 2211848 | tf_op jit(solution)/shard_map/ppermute | solution.py:316
  286.6 65.5 %collective-permute-start.33 = (bf16[256,2176]{1,0:T(8,128)(2,1)}, bf16[256,2176]{1,0:T(8,128)(2,1)}, u32[]{:S(2)}, u32[]{:S(2)}) collective-permute-start(bf16[256,2176]{1,0:T(8,128)(2,1)} %get-tuple-element.95), channel_id=1, source_target_pairs={{0,1},{1,0},{2,3},{3,2},{4,5},{5,4},{6,7},{7,6},{8,9},{9,8},{10,11... | collective-permute-start | bytes 3342344 | tf_op jit(solution)/shard_map/ppermute | solution.py:316
  325.9 50.6 %collective-permute-start.16 = (bf16[256,2176]{1,0:T(8,128)(2,1)}, bf16[256,2176]{1,0:T(8,128)(2,1)}, u32[]{:S(2)}, u32[]{:S(2)}) collective-permute-start(bf16[256,2176]{1,0:T(8,128)(2,1)} %get-tuple-element.75), channel_id=1, source_target_pairs={{0,1},{1,0},{2,3},{3,2},{4,5},{5,4},{6,7},{7,6},{8,9},{9,8},{10,11... | collective-permute-start | bytes 3342344 | tf_op jit(solution)/shard_map/ppermute | solution.py:316
  326.5 29.8 %collective-permute-start.43 = (bf16[256,2176]{1,0:T(8,128)(2,1)}, bf16[256,2176]{1,0:T(8,128)(2,1)S(1)}, u32[]{:S(2)}, u32[]{:S(2)}) collective-permute-start(bf16[256,2176]{1,0:T(8,128)(2,1)} %get-tuple-element.107), channel_id=1, source_target_pairs={{0,1},{1,0},{2,3},{3,2},{4,5},{5,4},{6,7},{7,6},{8,9},{9,8},{10,11... | collective-permute-start | bytes 3342344 | tf_op jit(solution)/shard_map/ppermute | solution.py:316
  353.9 74.3 %collective-permute-start.34 = (bf16[256,2176]{1,0:T(8,128)(2,1)S(1)}, bf16[256,2176]{1,0:T(8,128)(2,1)S(1)}, u32[]{:S(2)}, u32[]{:S(2)}) collective-permute-start(bf16[256,2176]{1,0:T(8,128)(2,1)S(1)} %add_convert_fusion.2), channel_id=1, source_target_pairs={{0,4},{1,5},{2,6},{3,7},{4,0},{5,1},{6,2},{7,3},{8,12},{9,13},{10,... | collective-permute-start | bytes 3342344 | tf_op jit(solution)/shard_map/ppermute | solution.py:316
  362.7 90.2 %collective-permute-start.44 = (bf16[256,2176]{1,0:T(8,128)(2,1)S(1)}, bf16[256,2176]{1,0:T(8,128)(2,1)S(1)}, u32[]{:S(2)}, u32[]{:S(2)}) collective-permute-start(bf16[256,2176]{1,0:T(8,128)(2,1)S(1)} %add_convert_fusion.1), channel_id=1, source_target_pairs={{0,6},{1,7},{2,4},{3,5},{4,2},{5,3},{6,0},{7,1},{8,14},{9,15},{10,... | collective-permute-start | bytes 3342344 | tf_op jit(solution)/shard_map/ppermute | solution.py:316
  374.2 78.8 %collective-permute-start.59 = (bf16[256,2176]{1,0:T(8,128)(2,1)S(1)}, bf16[256,2176]{1,0:T(8,128)(2,1)S(1)}, u32[]{:S(2)}, u32[]{:S(2)}) collective-permute-start(bf16[256,2176]{1,0:T(8,128)(2,1)S(1)} %get-tuple-element.122), channel_id=1, source_target_pairs={{0,1},{1,0},{2,3},{3,2},{4,5},{5,4},{6,7},{7,6},{8,9},{9,8},{10,11... | collective-permute-start | bytes 3342344 | tf_op jit(solution)/shard_map/ppermute | solution.py:316
  374.5 78.4 %collective-permute-start.54 = (bf16[256,2176]{1,0:T(8,128)(2,1)S(1)}, bf16[256,2176]{1,0:T(8,128)(2,1)S(1)}, u32[]{:S(2)}, u32[]{:S(2)}) collective-permute-start(bf16[256,2176]{1,0:T(8,128)(2,1)S(1)} %add_convert_fusion), channel_id=1, source_target_pairs={{0,2},{1,3},{2,0},{3,1},{4,6},{5,7},{6,4},{7,5},{8,10},{9,11},{10,... | collective-permute-start | bytes 3342344 | tf_op jit(solution)/shard_map/ppermute | solution.py:316
  (82 other events, 920.6 us)

commit v4 on v3

--- a/solution.py
+++ b/solution.py
@@ -11,6 +11,12 @@
 CAP = 40
 VMEM_BYTES = 50 * 1024 * 1024
 
+
+def moves(ample):
+    count = 400_000_000 if ample else 1000
+    return pl.CostEstimate(flops=count, bytes_accessed=count, transcendentals=0)
+
+
 clip_ratio = 2.0
 
 
@@ -44,12 +50,13 @@
 
 
 def partial_kernel(count, me, same, other, slots, w_gate, w_up, w_down, after,
-                   self_a, self_b, send_a, keep_a, send_b, keep_b):
+                   own, part_x, part_y, across_a, across_b):
     step = pl.program_id(0)
     part, half = step // count, step % count
     tokens, width = same.shape
-    rows = self_a.shape[1]
+    rows = own.shape[1]
     hidden = w_gate.shape[2]
+    cut = across_a.shape[2]
     pick = jnp.where(one_hot(slots, rows), 1.0, 0.0).astype(jnp.bfloat16)
     taken = dot_nn(pick[:, :tokens], same[...]) + dot_nn(pick[:, tokens:], other[...])
     taken = taken.astype(jnp.bfloat16)
@@ -57,43 +64,28 @@
     gate = dot_nn(taken[:, :features], w_gate[0]).astype(jnp.bfloat16)
     up = dot_nn(taken[:, :features], w_up[0]).astype(jnp.bfloat16)
     back = dot_nt(taken[:, features:], w_down[0]).astype(jnp.bfloat16)
-
-    def put_a(ref, *where):
-        ref[(*where, slice(None), pl.ds(0, hidden))] = gate
-        ref[(*where, slice(None), pl.ds(hidden, hidden // 2))] = up[:, : hidden // 2]
-
-    def put_b(ref, *where):
-        ref[(*where, slice(None), pl.ds(0, hidden // 2))] = up[:, hidden // 2 :]
-        ref[(*where, slice(None), pl.ds(hidden // 2, hidden))] = back
-
-    @pl.when(part == 0)
-    def _():
-        put_a(self_a, half)
-        put_b(self_b, half)
-
-    @pl.when(part == 1)
-    def _():
-        put_a(send_a, 0, half)
-        put_b(keep_b, half)
-
-    @pl.when(part == 2)
-    def _():
-        put_a(keep_a, half)
-        put_b(send_b, 0, half)
+    for v, ref in enumerate((own, part_x, part_y)):
+        @pl.when(part == v)
+        def _():
+            ref[half, :, pl.ds(0, hidden)] = gate
+            ref[half, :, pl.ds(hidden, hidden)] = up
+            ref[half, :, pl.ds(2 * hidden, hidden)] = back
 
     @pl.when(part == 3)
     def _():
-        put_a(send_a, 1, half)
-        put_b(send_b, 1, half)
-
-
-def partial_sums(me, same, other, slots, w_gate, w_up, w_down, after, halves):
+        across_a[half, :, pl.ds(0, hidden)] = gate
+        across_a[half, :, pl.ds(hidden, cut - hidden)] = up[:, : cut - hidden]
+        across_b[half, :, pl.ds(0, cut - hidden)] = up[:, cut - hidden :]
+        across_b[half, :, pl.ds(cut - hidden, hidden)] = back
+
+
+def partial_sums(me, same, other, slots, w_gate, w_up, w_down, after, halves, ample):
     count = len(halves)
     features, hidden = w_gate.shape[1:]
-    rows, cols = 2 * CAP, 3 * hidden // 2
-    one = jax.ShapeDtypeStruct((count, rows, cols), jnp.bfloat16)
-    two = jax.ShapeDtypeStruct((2, count, rows, cols), jnp.bfloat16)
-    outs = (one, one, two, one, two, one)
+    rows, cols = 2 * CAP, 3 * hidden
+    full = jax.ShapeDtypeStruct((count, rows, cols), jnp.bfloat16)
+    cut = jax.ShapeDtypeStruct((count, rows, cols // 2), jnp.bfloat16)
+    outs = (full, full, full, cut, cut)
     steps = 4 * count
     return pl.pallas_call(
         functools.partial(partial_kernel, count),
@@ -113,38 +105,30 @@
         ),
         out_shape=outs,
         compiler_params=pltpu.CompilerParams(vmem_limit_bytes=VMEM_BYTES),
-        cost_estimate=pl.CostEstimate(
-            flops=steps * rows * 10 * features * hidden,
-            bytes_accessed=steps * features * hidden * 11,
-            transcendentals=0,
-        ),
+        cost_estimate=moves(ample),
     )(me, same, other, slots, w_gate, w_up, w_down, after)
 
 
-def middle_kernel(me, self_a, self_b, first_a, first_b, last_a, last_b, slots, share, after, out):
-    count, rows, cols = self_a.shape
-    hidden = 2 * cols // 3
+def middle_kernel(me, own, from_x, from_y, slots, share, *rest):
+    out = rest[-1]
+    count, rows, cols = own.shape
+    hidden = cols // 3
     half = hidden // 2
     extra = 2 * EXPERTS
     for h in range(count):
-        def total(own, first, last, lo, size):
-            cut = pl.ds(lo, size)
+        def total(lo):
+            cut = pl.ds(lo, half)
             return (
                 own[h, :, cut].astype(jnp.float32)
-                + first[0, h, :, cut].astype(jnp.float32)
-                + last[h, :, cut].astype(jnp.float32)
+                + from_x[h, :, cut].astype(jnp.float32)
+                + from_y[h, :, cut].astype(jnp.float32)
             )
         hot = one_hot(slots.at[pl.ds(h, 1)], rows)
         fraction = jnp.sum(jnp.where(hot, share[h], 0.0), axis=1, keepdims=True)
         grads = jnp.zeros((rows, 1), jnp.float32)
         for side in range(2):
             lo = side * half
-            gate = total(self_a, first_a, last_a, lo, half)
-            if side == 0:
-                up = total(self_a, first_a, last_a, hidden, half)
-            else:
-                up = total(self_b, first_b, last_b, 0, half)
-            back = total(self_b, first_b, last_b, half + lo, half)
+            gate, up, back = total(lo), total(hidden + lo), total(2 * hidden + lo)
             sig = 1.0 / (1.0 + jnp.exp(-gate))
             silu = gate * sig
             act = silu * up
@@ -160,88 +144,111 @@
         high = grads.astype(jnp.bfloat16).astype(jnp.float32)
         spread = jnp.where(lane == me[0] + h, high, 0.0)
         spread = jnp.where(lane == me[0] + h + EXPERTS, grads - high, spread)
-        out[h, :, pl.ds(cols, extra)] = spread.astype(jnp.bfloat16)
-
-
-def first_of(shape, at):
-    return pl.BlockSpec((1,) + shape[1:], lambda g: (at,) + (0,) * (len(shape) - 1))
+        out[h, :, pl.ds(cols // 2, extra)] = spread.astype(jnp.bfloat16)
 
 
 def at_once(shape):
     return pl.BlockSpec(shape, lambda g: (0,) * len(shape))
 
 
-def middle(first, self_a, self_b, first_a, first_b, last_a, last_b, slots, share, after):
-    count, rows, cols = self_a.shape
-    out = jax.ShapeDtypeStruct((count, rows, 2 * cols + 2 * EXPERTS), jnp.bfloat16)
+def middle(first, own, from_x, from_y, slots, share, after, ample):
+    count, rows, cols = own.shape
+    out = jax.ShapeDtypeStruct((count, rows, cols + 2 * EXPERTS), jnp.bfloat16)
     return pl.pallas_call(
         middle_kernel,
         grid=(1,),
         out_shape=out,
-        in_specs=[
-            pl.BlockSpec(memory_space=pltpu.SMEM),
-            at_once(self_a.shape),
-            at_once(self_b.shape),
-            first_of(first_a.shape, 0),
-            first_of(first_b.shape, 0),
-            at_once(last_a.shape),
-            at_once(last_b.shape),
-            at_once(slots.shape),
-            at_once(share.shape),
-            pl.BlockSpec(memory_space=pl.ANY),
-        ],
+        in_specs=[pl.BlockSpec(memory_space=pltpu.SMEM)]
+        + [at_once(a.shape) for a in (own, from_x, from_y, slots, share)]
+        + [pl.BlockSpec(memory_space=pl.ANY)] * len(after),
         out_specs=at_once(out.shape),
         compiler_params=pltpu.CompilerParams(vmem_limit_bytes=VMEM_BYTES),
-        cost_estimate=pl.CostEstimate(
-            flops=40 * self_a.size, bytes_accessed=20 * self_a.size, transcendentals=self_a.size
-        ),
-    )(first, self_a, self_b, first_a, first_b, last_a, last_b, slots, share, after)
-
-
-def between_kernel(adds, relays, *refs):
-    ins, outs = refs[: 4 * adds + 2 * relays], refs[4 * adds + 2 * relays + 1 :]
+        cost_estimate=moves(ample),
+    )(first, own, from_x, from_y, slots, share, *after)
+
+
+def between_kernel(waits, adds, relays, passes, *refs):
+    count = 4 * adds + 2 * relays + passes
+    ins, outs = list(refs[:count]), list(refs[count + waits :])
     if adds:
-        for n in range(2):
-            outs[n][...] = (
-                ins[n][...].astype(jnp.float32) + ins[2 + n][0].astype(jnp.float32)
-            ).astype(jnp.bfloat16)
+        part_x, part_y, given_a, given_b = ins[:4]
+        to_x, to_y = outs[:2]
+        cut = given_a.shape[2]
+        low, high = pl.ds(0, cut), pl.ds(cut, cut)
+        to_x[:, :, low] = part_x[:, :, low]
+        to_x[:, :, high] = (
+            part_x[:, :, high].astype(jnp.float32) + given_b[...].astype(jnp.float32)
+        ).astype(jnp.bfloat16)
+        to_y[:, :, low] = (
+            part_y[:, :, low].astype(jnp.float32) + given_a[...].astype(jnp.float32)
+        ).astype(jnp.bfloat16)
+        to_y[:, :, high] = part_y[:, :, high]
+        ins, outs = ins[4:], outs[2:]
     if relays:
-        rows_x, rows_y = ins[4 * adds :]
-        out_a, out_b = outs[2 * adds :]
+        rows_x, rows_y = ins[:2]
+        out_a, out_b = outs[:2]
         cut = out_a.shape[2]
         out_a[...] = rows_y[:, :, pl.ds(0, cut)]
         out_b[...] = rows_x[:, :, pl.ds(cut, out_b.shape[2])]
-
-
-def between(add, relay, after):
-    ins, specs, outs = [], [], []
+        ins, outs = ins[2:], outs[2:]
+    if passes:
+        outs[0][...] = ins[0][...]
+
+
+def between(add, relay, block, after, ample):
+    ins, outs = [], []
     if add is not None:
-        keep_a, keep_b, first_a, first_b = add
-        ins += [keep_a, keep_b, first_a, first_b]
-        specs += [at_once(keep_a.shape), at_once(keep_b.shape)]
-        specs += [first_of(first_a.shape, 1), first_of(first_b.shape, 1)]
-        outs += [keep_a.shape, keep_b.shape]
+        ins += add
+        outs += [add[0].shape, add[1].shape]
     if relay is not None:
-        ins += list(relay)
-        specs += [at_once(r.shape) for r in relay]
+        ins += relay
         count, rows, width = relay[0].shape
         cols = (width - 2 * EXPERTS) // 2
         outs += [(count, rows, cols + 2 * EXPERTS), (count, rows, cols)]
-    size = sum(i.size for i in ins)
+    if block is not None:
+        ins += [block]
+        outs += [block.shape]
+    given = [int(a is not None) for a in (add, relay, block)]
     return pl.pallas_call(
-        functools.partial(between_kernel, int(add is not None), int(relay is not None)),
+        functools.partial(between_kernel, len(after), *given),
         grid=(1,),
         out_shape=[jax.ShapeDtypeStruct(o, jnp.bfloat16) for o in outs],
-        in_specs=specs + [pl.BlockSpec(memory_space=pl.ANY)],
+        in_specs=[at_once(i.shape) for i in ins]
+        + [pl.BlockSpec(memory_space=pl.ANY)] * len(after),
         out_specs=[at_once(o) for o in outs],
         compiler_params=pltpu.CompilerParams(vmem_limit_bytes=VMEM_BYTES),
-        cost_estimate=pl.CostEstimate(flops=size, bytes_accessed=4 * size, transcendentals=0),
-    )(*ins, after)
-
-
-def combine_kernel(count, me, *refs):
+        cost_estimate=moves(ample),
+    )(*ins, *after)
+
+
+def add_up_kernel(count, *refs):
+    ins, outs = refs[:count], refs[count + 1 :]
+    for n, out in enumerate(outs):
+        cut = pl.ds(n * out.shape[0], out.shape[0])
+        total = ins[0][cut, :].astype(jnp.float32)
+        for ref in ins[1:]:
+            total = total + ref[cut, :].astype(jnp.float32)
+        out[...] = total.astype(jnp.bfloat16)
+
+
+def add_up(blocks, splits, after):
+    rows, width = blocks[0].shape
+    out = jax.ShapeDtypeStruct((rows // splits, width), jnp.bfloat16)
+    return pl.pallas_call(
+        functools.partial(add_up_kernel, len(blocks)),
+        grid=(1,),
+        out_shape=[out] * splits,
+        in_specs=[at_once((rows, width))] * len(blocks) + [pl.BlockSpec(memory_space=pl.ANY)],
+        out_specs=[at_once(out.shape)] * splits,
+        compiler_params=pltpu.CompilerParams(vmem_limit_bytes=VMEM_BYTES),
+        cost_estimate=moves(True),
+    )(*blocks, after)
+
+
+def combine_kernel(count, waits, me, *refs):
     across_a, across_b = refs[3:5]
-    slots, w_gate, w_up, w_down, _, same, other, rows_in, hots, outs = refs[5:]
+    slots, w_gate, w_up, w_down = refs[5:9]
+    same, other, rows_in, hots, outs = refs[9 + waits :]
     step = pl.program_id(0)
     part, half = step // count, step % count
     rows, cols = rows_in.shape[0], across_b.shape[2]
@@ -273,7 +280,7 @@
             ref[...] = dot_tn(hots[:, pl.ds(lo, tokens)], outs[...]).astype(jnp.bfloat16)
 
 
-def combine(me, given, slots, w_gate, w_up, w_down, after, halves):
+def combine(me, given, slots, w_gate, w_up, w_down, after, halves, ample=True):
     count = len(halves)
     features, hidden = w_gate.shape[1:]
     rows = 2 * CAP
@@ -282,7 +289,7 @@
     width = 2 * features + 2 * EXPERTS
     out = jax.ShapeDtypeStruct((tokens, width), jnp.bfloat16)
     return pl.pallas_call(
-        functools.partial(combine_kernel, count),
+        functools.partial(combine_kernel, count, len(after)),
         grid_spec=pltpu.PrefetchScalarGridSpec(
             num_scalar_prefetch=1,
             grid=(steps,),
@@ -292,7 +299,7 @@
                 expert_block((features, hidden), halves),
                 expert_block((features, hidden), halves),
                 expert_block((hidden, features), halves),
-                pl.BlockSpec(memory_space=pl.ANY),
+                *[pl.BlockSpec(memory_space=pl.ANY)] * len(after),
             ],
             out_specs=[whole(out.shape)] * 2,
             scratch_shapes=[
@@ -303,12 +310,8 @@
         ),
         out_shape=(out, out),
         compiler_params=pltpu.CompilerParams(vmem_limit_bytes=VMEM_BYTES),
-        cost_estimate=pl.CostEstimate(
-            flops=steps * rows * 10 * features * hidden,
-            bytes_accessed=steps * features * hidden * 11,
-            transcendentals=0,
-        ),
-    )(me, *given, slots, w_gate, w_up, w_down, after)
+        cost_estimate=moves(ample),
+    )(me, *given, slots, w_gate, w_up, w_down, *after)
 
 
 def swap(value, axis, bits):
@@ -328,9 +331,9 @@
     ratio_weight = jnp.minimum(jnp.exp(log_ratio), clip_ratio)
     weighted = (ratio_weight[:, None] * cotangent.astype(jnp.float32)).astype(jnp.bfloat16)
     payload = jnp.concatenate([tokens, weighted], axis=1)
-    across = swap(payload, "expert", 4)
-    sames = [payload, swap(payload, "expert", 2), across, swap(across, "expert", 2)]
-    others = [swap(p, "expert", 1) for p in sames]
+    arriving = swap(payload, "expert", 6)
+    sames = {0: payload, 1: swap(payload, "expert", 2)}
+    others = {0: swap(payload, "expert", 1)}
 
     local = mine * per_device + jnp.arange(per_device, dtype=jnp.int32)
     tri = (jnp.arange(block)[:, None] < jnp.arange(block)[None, :]).astype(jnp.bfloat16)
@@ -357,9 +360,8 @@
     far_slots, far_share = placed(far)
 
     weights = (gate_weight, up_weight, down_weight)
-    chunks = [(0, (0,)), (2, (0, 1)), (3, (0, 1)), (1, (0, 1)), (0, (1,))]
-    count = len(chunks)
-    sums, adds, sent, got, relayed, totals = {}, {}, {}, {}, {}, []
+    chunks = [(0, (0,)), (3, (0, 1)), (2, (0, 1)), (1, (0, 1)), (0, (1,))]
+    sums, adds, sent, got, relayed, blocks = {}, {}, {}, {}, {}, {}
     after = near_slots
 
     def slots_of(k):
@@ -372,60 +374,74 @@
 
     def start_rows(k, after):
         o, halves = chunks[k]
-        out = partial_sums(me, sames[o], others[o], slots_of(k), *weights, after, halves)
-        self_a, self_b, send_a, keep_a, send_b, keep_b = out
-        firsts = swap(send_a, "dp", 1), swap(send_b, "dp", 2)
-        sums[k] = self_a, self_b, *firsts
-        adds[k] = keep_a, keep_b, *firsts
-        return self_a
-
-    def move(k, r, after):
-        outs = between(adds.get(k), got.get(r), after)
+        own, part_x, part_y, across_a, across_b = partial_sums(
+            me, sames[o], others[o], slots_of(k), *weights, after, halves, k > 0
+        )
+        sums[k] = own
+        adds[k] = [part_x, part_y, swap(across_a, "dp", 1), swap(across_b, "dp", 2)]
+        return own
+
+    def move(k, r, *after, block=None):
+        outs = between(adds.get(k), got.get(r), block, after, k != 0 and r != 0)
         if k in adds:
-            last_a, last_b = swap(outs[0], "dp", 2), swap(outs[1], "dp", 1)
-            sums[k] = (*sums[k], last_a, last_b)
+            sums[k] = sums[k], swap(outs[0], "dp", 1), swap(outs[1], "dp", 2)
         if r in got:
-            relayed[r] = swap(outs[-2], "dp", 1), swap(outs[-1], "dp", 2)
+            at = 2 if k in adds else 0
+            relayed[r] = swap(outs[at], "dp", 1), swap(outs[at + 1], "dp", 2)
+        if block is not None:
+            return outs[0], outs[-1], swap(outs[-1], "expert", 1)
         return outs[0]
 
-    def turn_rows(k, after):
+    def turn_rows(k, *after):
         halves = chunks[k][1]
         first = 2 * member + halves[0]
         own_slot = lax.dynamic_slice_in_dim(slots_of(k), first, len(halves), 0)
         own_share = lax.dynamic_slice_in_dim(share_of(k), first, len(halves), 0)
         expert = (mine * per_device + first).astype(jnp.int32).reshape(1)
-        sent[k] = middle(expert, *sums[k], own_slot, own_share, after)
-        got[k] = swap(sent[k], "dp", 1), swap(sent[k], "dp", 2)
+        sent[k] = middle(expert, *sums[k], own_slot, own_share, after, k > 0)
+        got[k] = [swap(sent[k], "dp", 1), swap(sent[k], "dp", 2)]
         return sent[k]
 
-    def finish_rows(k, after):
+    def finish_rows(k, *after):
         o, halves = chunks[k]
         given = (sent[k], *got[k], *relayed[k])
         same, other = combine(me, given, slots_of(k), *weights, after, halves)
-        both = same.astype(jnp.float32) + swap(other, "expert", 1).astype(jnp.float32)
-        if o:
-            both = swap(both.astype(jnp.bfloat16), "expert", 2 * o)
-        totals.append(both)
+        blocks[k] = [same, other]
         return same
 
     after = start_rows(0, after)
     after = move(0, None, after)
     after = turn_rows(0, after)
-    after = move(None, 0, after)
-    for k in range(1, count):
-        after = start_rows(k, after)
-        if k == 1:
-            after = finish_rows(0, after)
-        else:
-            after = turn_rows(k - 1, after)
-            if k > 2:
-                after = finish_rows(k - 2, after)
-        after = move(k, k - 1 if k > 1 else None, after)
-    after = turn_rows(count - 1, after)
-    after = finish_rows(count - 2, after)
-    after = move(None, count - 1, after)
-    after = finish_rows(count - 1, after)
-    total = sum(t.astype(jnp.float32) for t in totals)
+    after, sames[3], others[3] = move(None, 0, after, block=arriving)
+    sames[2] = swap(sames[3], "expert", 2)
+    after = start_rows(1, after)
+    after, sames[2], others[2] = move(1, None, after, *relayed[0], block=sames[2])
+    after = start_rows(2, after)
+    after = turn_rows(1, after)
+    after = finish_rows(0, after)
+    after, sames[1], others[1] = move(2, 1, after, block=sames[1])
+    after = start_rows(3, after)
+    after = turn_rows(2, after, *relayed[1])
+    after = finish_rows(1, after)
+    after, _, other = move(3, 2, after, block=blocks[1][1])
+    after = start_rows(4, after)
+    (after,) = add_up([blocks[1][0], other], 1, after)
+    hop = swap(after, "expert", 2)
+    after = turn_rows(3, after, *relayed[2], *adds[4][2:])
+    after = finish_rows(2, after)
+    after, _, other = move(4, 3, after, hop, block=blocks[2][1])
+    after, second = add_up([blocks[2][0], other, hop], 2, after)
+    far_low, far_high = swap(after, "expert", 4), swap(second, "expert", 4)
+    after = turn_rows(4, second, *relayed[3])
+    after = finish_rows(3, after)
+    after, _, other = move(None, 4, after, far_low, block=blocks[3][1])
+    (after,) = add_up([blocks[3][0], other], 1, after)
+    near_back = swap(after, "expert", 2)
+    after = finish_rows(4, after)
+    for k in (0, 4):
+        blocks[k][1] = swap(blocks[k][1], "expert", 1)
+    far_back = jnp.concatenate([far_low, far_high], axis=0)
+    total = sum(t.astype(jnp.float32) for t in (*blocks[0], *blocks[4], near_back, far_back))
     grads = total[:, 2 * features : 2 * features + EXPERTS] + total[:, 2 * features + EXPERTS :]
     hit = routes[:, :, None] == jnp.arange(EXPERTS, dtype=jnp.int32)
     gate_grad = jnp.sum(jnp.where(hit, grads[:, None, :], 0.0), axis=2)

time: 458 us -> 412 us (0.90)
  waiting for transfers between devices: 195 us -> 133 us
  local copies, waits for them, and re-layouts: 20.3 us -> 31.2 us
  Pallas kernels: 174 us -> 184 us
    ppermute x60 -> x61, waiting for transfers between devices: 195 us -> 133 us  [swap(): return lax.ppermute(value, axis, [(n, n ^ bits) for n in range(count)])]
    unnamed x92 -> x110, local copies, waits for them, and re-layouts: 15.5 us -> 24 us
    pallas_call x12 -> x15, Pallas kernels: 91 us -> 98.8 us  [the longest x5 83.5 us: combine(): pl.pallas_call(functools.partial(combine_kernel, count, len(after)), grid...]
    ppermute x60 -> x61, starting transfers between devices: 57.8 us -> 54.8 us  [swap(): return lax.ppermute(value, axis, [(n, n ^ bits) for n in range(count)])]
  transfers between devices with their start and end apart: 60 -> 61, of which waited for: 17 -> 23; matrix products, arithmetic and copies ran while one was open for 2% -> 2% of each run, Pallas kernels for 38% -> 39%
where the time goes in v4:
time: 412 us; the launch traced here: 409 us
  Pallas kernels  184 us (45%)
  waiting for transfers between devices  133 us (32%)
  starting transfers between devices  54.8 us (13%)
  local copies, waits for them, and re-layouts  31.2 us (8%)
  other arithmetic  4.37 us (1%)
    ppermute x61, waiting for transfers between devices, swap(): return lax.ppermute(value, axis, [(n, n ^ bits) for n in range(count)])  133 us
    pallas_call x5, Pallas kernels, combine(): pl.pallas_call(functools.partial(combine_kernel, count, len(after)), grid...  83.5 us
    pallas_call x5, Pallas kernels, partial_sums(): pl.pallas_call(functools.partial(partial_kernel, count), grid_spec=pltpu....  77.8 us
    ppermute x61, starting transfers between devices, swap(): return lax.ppermute(value, axis, [(n, n ^ bits) for n in range(count)])  54.8 us
    unnamed x110, local copies, waits for them, and re-layouts  24 us
    pallas_call x7, Pallas kernels, between(): pl.pallas_call(functools.partial(between_kernel, len(after), *given), gri...  13.1 us
  transfers between devices with their start and end apart: 61, of which 23 were waited for; matrix products, arithmetic and copies ran while one was open for 2% of the time, Pallas kernels for 39%

profile of v4, /device:TPU:8, one launch (start us, length us, event | category | flops | bytes accessed | tf_op | source)
XLA Modules:
  0.0 408.8 jit_solution(8859708406178309556)
XLA Ops:
  5.9 10.6 %shard_map.103 = (bf16[1,80,2304]{2,1,0:T(8,128)(2,1)S(1)}, bf16[1,80,2304]{2,1,0:T(8,128)(2,1)S(1)}, bf16[1,80,2304]{2,1,0:T(8,128)(2,1)S(1)}, bf16[1,80,1152]{2,1,0:T(8,128)(2,1)}, bf16[1,80,1152]{2,1,0:T(8,128)(2,1)S(1)}) custom-call(s32[1]{0:T(128)} %bitcast.me, bf16[256,2048]{1,0:T(8,128)(2,1)S(1)} %pad_maximum_fusion.same, ...), custom_call_target="tpu_custom_call" | custom-call | flops 1000 | bytes 1000 | tf_op jit(solution)/shard_map/pallas_call | solution.py:90
  30.9 7.2 %collective-permute-done.4.from_x = bf16[1,80,2304]{2,1,0:T(8,128)(2,1)S(1)} collective-permute-done((bf16[1,80,2304]{2,1,0:T(8,128)(2,1)S(1)}, bf16[1,80,2304]{2,1,0:T(8,128)(2,1)S(1)}, u32[]{:S(2)}, u32[]{:S(2)}) %collective-permute-start.4) | collective-permute-done | bytes 368672 | tf_op jit(solution)/shard_map/ppermute | solution.py:319
  44.5 2.6 collective-permute-start.13
  47.1 21.9 %collective-permute-done.8.refs_2_ = bf16[256,2048]{1,0:T(8,128)(2,1)S(1)} collective-permute-done((bf16[256,2048]{1,0:T(8,128)(2,1)S(1)}, bf16[256,2048]{1,0:T(8,128)(2,1)S(1)}, u32[]{:S(2)}, u32[]{:S(2)}) %collective-permute-start.8) | collective-permute-done | bytes 1048608 | tf_op jit(solution)/shard_map/ppermute | solution.py:319
  81.1 18.9 %shard_map.107 = (bf16[2,80,2304]{2,1,0:T(8,128)(2,1)S(1)}, bf16[2,80,2304]{2,1,0:T(8,128)(2,1)S(1)}, bf16[2,80,2304]{2,1,0:T(8,128)(2,1)S(1)}, bf16[2,80,1152]{2,1,0:T(8,128)(2,1)S(1)}, bf16[2,80,1152]{2,1,0:T(8,128)(2,1)S(1)}) custom-call(s32[1]{0:T(128)} %bitcast.me, bf16[256,2048]{1,0:T(8,128)(2,1)} %copy-done.26, ...), custom_call_target="tpu_custom_call" | custom-call | flops 400000000 | bytes 400000000 | tf_op jit(solution)/shard_map/pallas_call | solution.py:90
  104.9 10.8 %collective-permute-done.10.refs_7_.refs_4_ = bf16[1,80,1152]{2,1,0:T(8,128)(2,1)S(1)} collective-permute-done((bf16[1,80,1152]{2,1,0:T(8,128)(2,1)S(1)}, bf16[1,80,1152]{2,1,0:T(8,128)(2,1)S(1)}, u32[]{:S(2)}, u32[]{:S(2)}) %collective-permute-start.10) | collective-permute-done | bytes 184352 | tf_op jit(solution)/shard_map/ppermute | solution.py:319
  115.9 2.6 shard_map.108
  122.8 18.9 %shard_map.109 = (bf16[2,80,2304]{2,1,0:T(8,128)(2,1)S(1)}, bf16[2,80,2304]{2,1,0:T(8,128)(2,1)S(1)}, bf16[2,80,2304]{2,1,0:T(8,128)(2,1)S(1)}, bf16[2,80,1152]{2,1,0:T(8,128)(2,1)S(1)}, bf16[2,80,1152]{2,1,0:T(8,128)(2,1)S(1)}) custom-call(s32[1]{0:T(128)} %bitcast.me, bf16[256,2048]{1,0:T(8,128)(2,1)} %get-tuple-element.83.same, ...), custom_call_target="tpu_custom_call" | custom-call | flops 400000000 | bytes 400000000 | tf_op jit(solution)/shard_map/pallas_call | solution.py:90
  148.8 11.5 %shard_map.111 = (bf16[256,2176]{1,0:T(8,128)(2,1)S(1)}, bf16[256,2176]{1,0:T(8,128)(2,1)}) custom-call(s32[1]{0:T(128)} %bitcast.me, bf16[1,80,2432]{2,1,0:T(8,128)(2,1)S(1)} %shard_map.105.refs_3_.refs_0_, bf16[1,80,2432]{2,1,0:T(8,128)(2,1)S(1)} %collective-permute-done.6.refs_0_.refs_1_, bf16[1,80,2432]{2,1,0:T(8,128)(2,1)S(1)} %collective-permute-done.7.refs_1_.refs_2_, ...), custom_call_target="tpu_custom_call" | custom-call | flops 400000000 | bytes 400000000 | tf_op jit(solution)/shard_map/pallas_call | solution.py:291
  161.3 10.2 %collective-permute-done.23.refs_2_ = bf16[2,80,1152]{2,1,0:T(8,128)(2,1)S(1)} collective-permute-done((bf16[2,80,1152]{2,1,0:T(8,128)(2,1)S(1)}, bf16[2,80,1152]{2,1,0:T(8,128)(2,1)S(1)}, u32[]{:S(2)}, u32[]{:S(2)}) %collective-permute-start.23) | collective-permute-done | bytes 368672 | tf_op jit(solution)/shard_map/ppermute | solution.py:319
  173.0 3.1 shard_map.112
  181.9 19.0 %shard_map.113 = (bf16[2,80,2304]{2,1,0:T(8,128)(2,1)S(1)}, bf16[2,80,2304]{2,1,0:T(8,128)(2,1)S(1)}, bf16[2,80,2304]{2,1,0:T(8,128)(2,1)S(1)}, bf16[2,80,1152]{2,1,0:T(8,128)(2,1)S(1)}, bf16[2,80,1152]{2,1,0:T(8,128)(2,1)S(1)}) custom-call(s32[1]{0:T(128)} %bitcast.me, bf16[256,2048]{1,0:T(8,128)(2,1)} %get-tuple-element.91.same, ...), custom_call_target="tpu_custom_call" | custom-call | flops 400000000 | bytes 400000000 | tf_op jit(solution)/shard_map/pallas_call | solution.py:90
  210.8 20.4 %shard_map.115 = (bf16[256,2176]{1,0:T(8,128)(2,1)}, bf16[256,2176]{1,0:T(8,128)(2,1)}) custom-call(s32[1]{0:T(128)} %bitcast.me, bf16[2,80,2432]{2,1,0:T(8,128)(2,1)S(1)} %shard_map.110.refs_9_.refs_0_, bf16[2,80,2432]{2,1,0:T(8,128)(2,1)S(1)} %copy-done.18, bf16[2,80,2432]{2,1,0:T(8,128)(2,1)S(1)} %copy-done.20, ...), custom_call_target="tpu_custom_call" | custom-call | flops 400000000 | bytes 400000000 | tf_op jit(solution)/shard_map/pallas_call | solution.py:291
  234.8 3.1 shard_map.116
  240.1 10.4 %shard_map.117 = (bf16[1,80,2304]{2,1,0:T(8,128)(2,1)S(1)}, bf16[1,80,2304]{2,1,0:T(8,128)(2,1)S(1)}, bf16[1,80,2304]{2,1,0:T(8,128)(2,1)S(1)}, bf16[1,80,1152]{2,1,0:T(8,128)(2,1)S(1)}, bf16[1,80,1152]{2,1,0:T(8,128)(2,1)S(1)}) custom-call(s32[1]{0:T(128)} %bitcast.me, bf16[256,2048]{1,0:T(8,128)(2,1)S(1)} %pad_maximum_fusion.same, ...), custom_call_target="tpu_custom_call" | custom-call | flops 400000000 | bytes 400000000 | tf_op jit(solution)/shard_map/pallas_call | solution.py:90
  252.4 8.4 %collective-permute-done.37.rest_3_.refs_2_ = bf16[1,80,1152]{2,1,0:T(8,128)(2,1)S(1)} collective-permute-done((bf16[1,80,1152]{2,1,0:T(8,128)(2,1)S(1)}, bf16[1,80,1152]{2,1,0:T(8,128)(2,1)S(1)}, u32[]{:S(2)}, u32[]{:S(2)}) %collective-permute-start.37) | collective-permute-done | bytes 184352 | tf_op jit(solution)/shard_map/ppermute | solution.py:319
  264.8 6.6 %collective-permute-done.43.rest_2_.refs_4_ = bf16[2,80,1152]{2,1,0:T(8,128)(2,1)S(1)} collective-permute-done((bf16[2,80,1152]{2,1,0:T(8,128)(2,1)S(1)}, bf16[2,80,1152]{2,1,0:T(8,128)(2,1)S(1)}, u32[]{:S(2)}, u32[]{:S(2)}) %collective-permute-start.43) | collective-permute-done | bytes 368672 | tf_op jit(solution)/shard_map/ppermute | solution.py:319
  276.9 20.3 %shard_map.120 = (bf16[256,2176]{1,0:T(8,128)(2,1)}, bf16[256,2176]{1,0:T(8,128)(2,1)}) custom-call(s32[1]{0:T(128)} %bitcast.me, bf16[2,80,2432]{2,1,0:T(8,128)(2,1)S(1)} %copy-done.1, bf16[2,80,2432]{2,1,0:T(8,128)(2,1)S(1)} %copy-done.14, bf16[2,80,2432]{2,1,0:T(8,128)(2,1)S(1)} %copy-done.16, ...), custom_call_target="tpu_custom_call" | custom-call | flops 400000000 | bytes 400000000 | tf_op jit(solution)/shard_map/pallas_call | solution.py:291
  298.6 3.2 shard_map.121
  309.0 12.9 %collective-permute-done.47.from_x = bf16[1,80,2304]{2,1,0:T(8,128)(2,1)} collective-permute-done((bf16[1,80,2304]{2,1,0:T(8,128)(2,1)}, bf16[1,80,2304]{2,1,0:T(8,128)(2,1)}, u32[]{:S(2)}, u32[]{:S(2)}) %collective-permute-start.47) | collective-permute-done | bytes 368672 | tf_op jit(solution)/shard_map/ppermute | solution.py:319
  326.7 20.7 %shard_map.124 = (bf16[256,2176]{1,0:T(8,128)(2,1)}, bf16[256,2176]{1,0:T(8,128)(2,1)}) custom-call(s32[1]{0:T(128)} %bitcast.me, bf16[2,80,2432]{2,1,0:T(8,128)(2,1)S(1)} %copy-done.3, bf16[2,80,2432]{2,1,0:T(8,128)(2,1)S(1)} %collective-permute-done.44.refs_4_.refs_1_, bf16[2,80,2432]{2,1,0:T(8,128)(2,1)S(1)} %copy-done.22, ...), custom_call_target="tpu_custom_call" | custom-call | flops 400000000 | bytes 400000000 | tf_op jit(solution)/shard_map/pallas_call | solution.py:291
  352.8 3.6 collective-permute-done.56.refs_4_
  356.5 10.6 %shard_map.127 = (bf16[256,2176]{1,0:T(8,128)(2,1)S(1)}, bf16[256,2176]{1,0:T(8,128)(2,1)S(1)}) custom-call(s32[1]{0:T(128)} %bitcast.me, bf16[1,80,2432]{2,1,0:T(8,128)(2,1)S(1)} %shard_map.123.refs_9_.refs_0_, bf16[1,80,2432]{2,1,0:T(8,128)(2,1)S(1)} %collective-permute-done.52.refs_0_.refs_1_, ...), custom_call_target="tpu_custom_call" | custom-call | flops 400000000 | bytes 400000000 | tf_op jit(solution)/shard_map/pallas_call | solution.py:291
  369.2 36.8 %collective-permute-done.60 = bf16[128,2176]{1,0:T(8,128)(2,1)S(1)} collective-permute-done((bf16[128,2176]{1,0:T(8,128)(2,1)S(1)}, bf16[128,2176]{1,0:T(8,128)(2,1)S(1)}, u32[]{:S(2)}, u32[]{:S(2)}) %collective-permute-start.60) | collective-permute-done | bytes 557088 | tf_op jit(solution)/shard_map/ppermute | solution.py:319
  (276 shorter events, 113.3 us)
Async XLA Ops:
  21.0 48.0 %collective-permute-start.8 = (bf16[256,2048]{1,0:T(8,128)(2,1)S(1)}, bf16[256,2048]{1,0:T(8,128)(2,1)S(1)}, u32[]{:S(2)}, u32[]{:S(2)}) collective-permute-start(bf16[256,2048]{1,0:T(8,128)(2,1)S(1)} %pad_maximum_fusion.same), channel_id=1, source_target_pairs={{0,6},{1,7},{2,4},{3,5},{4,2},{5,3},{6,0},{7,1},{8,14},{9,15},{10,... | collective-permute-start | bytes 3145736 | tf_op jit(solution)/shard_map/ppermute | solution.py:319
  41.3 30.2 %collective-permute-start.6 = (bf16[1,80,2432]{2,1,0:T(8,128)(2,1)S(1)}, bf16[1,80,2432]{2,1,0:T(8,128)(2,1)S(1)}, u32[]{:S(2)}, u32[]{:S(2)}) collective-permute-start(bf16[1,80,2432]{2,1,0:T(8,128)(2,1)S(1)} %shard_map.105.refs_3_.refs_0_), channel_id=1, source_target_pairs={{0,8},{8,0},{16,24},{24,16},{1,9},{9,1},{17,25},{25,17},{2,10},{10... | collective-permute-start | bytes 1167368 | tf_op jit(solution)/shard_map/ppermute | solution.py:319
  42.6 29.0 %collective-permute-start.7 = (bf16[1,80,2432]{2,1,0:T(8,128)(2,1)S(1)}, bf16[1,80,2432]{2,1,0:T(8,128)(2,1)S(1)}, u32[]{:S(2)}, u32[]{:S(2)}) collective-permute-start(bf16[1,80,2432]{2,1,0:T(8,128)(2,1)S(1)} %shard_map.105.refs_3_.refs_0_), channel_id=1, source_target_pairs={{0,16},{8,24},{16,0},{24,8},{1,17},{9,25},{17,1},{25,9},{2,18},{10... | collective-permute-start | bytes 1167368 | tf_op jit(solution)/shard_map/ppermute | solution.py:319
  44.1 29.5 %collective-permute-start.12 = (s32[2,8,256]{2,1,0:T(8,128)S(1)}, s32[2,8,256]{2,1,0:T(8,128)S(1)}, u32[]{:S(2)}, u32[]{:S(2)}) collective-permute-start(s32[2,8,256]{2,1,0:T(8,128)S(1)} %get-tuple-element.148), channel_id=1, source_target_pairs={{0,2},{1,3},{2,0},{3,1},{4,6},{5,7},{6,4},{7,5},{8,10},{9,11},{10,... | collective-permute-start | bytes 49160 | tf_op jit(solution)/shard_map/ppermute | solution.py:319
  44.5 29.0 %collective-permute-start.13 = (s32[2,8,256]{2,1,0:T(8,128)S(1)}, s32[2,8,256]{2,1,0:T(8,128)S(1)}, u32[]{:S(2)}, u32[]{:S(2)}) collective-permute-start(s32[2,8,256]{2,1,0:T(8,128)S(1)} %get-tuple-element.148), channel_id=1, source_target_pairs={{0,4},{1,5},{2,6},{3,7},{4,0},{5,1},{6,2},{7,3},{8,12},{9,13},{10,... | collective-permute-start | bytes 49160 | tf_op jit(solution)/shard_map/ppermute | solution.py:319
  76.3 39.6 %collective-permute-start.18 = (bf16[256,2048]{1,0:T(8,128)(2,1)S(1)}, bf16[256,2048]{1,0:T(8,128)(2,1)}, u32[]{:S(2)}, u32[]{:S(2)}) collective-permute-start(bf16[256,2048]{1,0:T(8,128)(2,1)S(1)} %get-tuple-element.75.same), channel_id=1, source_target_pairs={{0,2},{1,3},{2,0},{3,1},{4,6},{5,7},{6,4},{7,5},{8,10},{9,11},{10,... | collective-permute-start | bytes 3145736 | tf_op jit(solution)/shard_map/ppermute | solution.py:319
  118.5 42.7 %collective-permute-start.27 = (bf16[256,2048]{1,0:T(8,128)(2,1)S(1)}, bf16[256,2048]{1,0:T(8,128)(2,1)}, u32[]{:S(2)}, u32[]{:S(2)}) collective-permute-start(bf16[256,2048]{1,0:T(8,128)(2,1)S(1)} %pad_maximum_fusion.same), channel_id=1, source_target_pairs={{0,2},{1,3},{2,0},{3,1},{4,6},{5,7},{6,4},{7,5},{8,10},{9,11},{10,... | collective-permute-start | bytes 3145736 | tf_op jit(solution)/shard_map/ppermute | solution.py:319
  144.6 27.2 %collective-permute-start.25 = (bf16[2,80,2432]{2,1,0:T(8,128)(2,1)S(1)}, bf16[2,80,2432]{2,1,0:T(8,128)(2,1)S(1)}, u32[]{:S(2)}, u32[]{:S(2)}) collective-permute-start(bf16[2,80,2432]{2,1,0:T(8,128)(2,1)S(1)} %shard_map.110.refs_9_.refs_0_), channel_id=1, source_target_pairs={{0,8},{8,0},{16,24},{24,16},{1,9},{9,1},{17,25},{25,17},{2,10},{10... | collective-permute-start | bytes 2334728 | tf_op jit(solution)/shard_map/ppermute | solution.py:319
  145.4 26.5 %collective-permute-start.26 = (bf16[2,80,2432]{2,1,0:T(8,128)(2,1)S(1)}, bf16[2,80,2432]{2,1,0:T(8,128)(2,1)S(1)}, u32[]{:S(2)}, u32[]{:S(2)}) collective-permute-start(bf16[2,80,2432]{2,1,0:T(8,128)(2,1)S(1)} %shard_map.110.refs_9_.refs_0_), channel_id=1, source_target_pairs={{0,16},{8,24},{16,0},{24,8},{1,17},{9,25},{17,1},{25,9},{2,18},{10... | collective-permute-start | bytes 2334728 | tf_op jit(solution)/shard_map/ppermute | solution.py:319
  146.9 24.6 %collective-permute-start.23 = (bf16[2,80,1152]{2,1,0:T(8,128)(2,1)S(1)}, bf16[2,80,1152]{2,1,0:T(8,128)(2,1)S(1)}, u32[]{:S(2)}, u32[]{:S(2)}) collective-permute-start(bf16[2,80,1152]{2,1,0:T(8,128)(2,1)S(1)} %get-tuple-element.89), channel_id=1, source_target_pairs={{0,8},{8,0},{16,24},{24,16},{1,9},{9,1},{17,25},{25,17},{2,10},{10... | collective-permute-start | bytes 1105928 | tf_op jit(solution)/shard_map/ppermute | solution.py:319
  176.2 27.9 %collective-permute-start.31 = (bf16[2,80,2304]{2,1,0:T(8,128)(2,1)S(1)}, bf16[2,80,2304]{2,1,0:T(8,128)(2,1)S(1)}, u32[]{:S(2)}, u32[]{:S(2)}) collective-permute-start(bf16[2,80,2304]{2,1,0:T(8,128)(2,1)S(1)} %get-tuple-element.92.after), channel_id=1, source_target_pairs={{0,8},{8,0},{16,24},{24,16},{1,9},{9,1},{17,25},{25,17},{2,10},{10... | collective-permute-start | bytes 2211848 | tf_op jit(solution)/shard_map/ppermute | solution.py:319
  177.5 26.5 %collective-permute-start.32 = (bf16[2,80,2304]{2,1,0:T(8,128)(2,1)S(1)}, bf16[2,80,2304]{2,1,0:T(8,128)(2,1)S(1)}, u32[]{:S(2)}, u32[]{:S(2)}) collective-permute-start(bf16[2,80,2304]{2,1,0:T(8,128)(2,1)S(1)} %get-tuple-element.97), channel_id=1, source_target_pairs={{0,16},{8,24},{16,0},{24,8},{1,17},{9,25},{17,1},{25,9},{2,18},{10... | collective-permute-start | bytes 2211848 | tf_op jit(solution)/shard_map/ppermute | solution.py:319
  179.0 25.0 %collective-permute-start.33 = (bf16[2,80,1280]{2,1,0:T(8,128)(2,1)S(1)}, bf16[2,80,1280]{2,1,0:T(8,128)(2,1)S(1)}, u32[]{:S(2)}, u32[]{:S(2)}) collective-permute-start(bf16[2,80,1280]{2,1,0:T(8,128)(2,1)S(1)} %get-tuple-element.99), channel_id=1, source_target_pairs={{0,8},{8,0},{16,24},{24,16},{1,9},{9,1},{17,25},{25,17},{2,10},{10... | collective-permute-start | bytes 1228808 | tf_op jit(solution)/shard_map/ppermute | solution.py:319
  179.7 24.4 %collective-permute-start.34 = (bf16[2,80,1152]{2,1,0:T(8,128)(2,1)S(1)}, bf16[2,80,1152]{2,1,0:T(8,128)(2,1)S(1)}, u32[]{:S(2)}, u32[]{:S(2)}) collective-permute-start(bf16[2,80,1152]{2,1,0:T(8,128)(2,1)S(1)} %get-tuple-element.100), channel_id=1, source_target_pairs={{0,16},{8,24},{16,0},{24,8},{1,17},{9,25},{17,1},{25,9},{2,18},{10... | collective-permute-start | bytes 1105928 | tf_op jit(solution)/shard_map/ppermute | solution.py:319
  205.6 28.0 %collective-permute-start.35 = (bf16[2,80,2432]{2,1,0:T(8,128)(2,1)}, bf16[2,80,2432]{2,1,0:T(8,128)(2,1)S(1)}, u32[]{:S(2)}, u32[]{:S(2)}) collective-permute-start(bf16[2,80,2432]{2,1,0:T(8,128)(2,1)} %shard_map.114.refs_9_.refs_0_), channel_id=1, source_target_pairs={{0,8},{8,0},{16,24},{24,16},{1,9},{9,1},{17,25},{25,17},{2,10},{10... | collective-permute-start | bytes 2334728 | tf_op jit(solution)/shard_map/ppermute | solution.py:319
  206.8 26.8 %collective-permute-start.36 = (bf16[2,80,2432]{2,1,0:T(8,128)(2,1)}, bf16[2,80,2432]{2,1,0:T(8,128)(2,1)S(1)}, u32[]{:S(2)}, u32[]{:S(2)}) collective-permute-start(bf16[2,80,2432]{2,1,0:T(8,128)(2,1)} %shard_map.114.refs_9_.refs_0_), channel_id=1, source_target_pairs={{0,16},{8,24},{16,0},{24,8},{1,17},{9,25},{17,1},{25,9},{2,18},{10... | collective-permute-start | bytes 2334728 | tf_op jit(solution)/shard_map/ppermute | solution.py:319
  209.2 24.4 %collective-permute-start.30 = (bf16[2,80,1152]{2,1,0:T(8,128)(2,1)S(1)}, bf16[2,80,1152]{2,1,0:T(8,128)(2,1)S(1)}, u32[]{:S(2)}, u32[]{:S(2)}) collective-permute-start(bf16[2,80,1152]{2,1,0:T(8,128)(2,1)S(1)} %get-tuple-element.96), channel_id=1, source_target_pairs={{0,16},{8,24},{16,0},{24,8},{1,17},{9,25},{17,1},{25,9},{2,18},{10... | collective-permute-start | bytes 1105928 | tf_op jit(solution)/shard_map/ppermute | solution.py:319
  237.9 34.0 %collective-permute-start.39 = (bf16[2,80,2304]{2,1,0:T(8,128)(2,1)S(1)}, bf16[2,80,2304]{2,1,0:T(8,128)(2,1)S(1)}, u32[]{:S(2)}, u32[]{:S(2)}) collective-permute-start(bf16[2,80,2304]{2,1,0:T(8,128)(2,1)S(1)} %get-tuple-element.103.after), channel_id=1, source_target_pairs={{0,8},{8,0},{16,24},{24,16},{1,9},{9,1},{17,25},{25,17},{2,10},{10... | collective-permute-start | bytes 2211848 | tf_op jit(solution)/shard_map/ppermute | solution.py:319
  238.6 33.3 %collective-permute-start.40 = (bf16[2,80,2304]{2,1,0:T(8,128)(2,1)S(1)}, bf16[2,80,2304]{2,1,0:T(8,128)(2,1)S(1)}, u32[]{:S(2)}, u32[]{:S(2)}) collective-permute-start(bf16[2,80,2304]{2,1,0:T(8,128)(2,1)S(1)} %get-tuple-element.109), channel_id=1, source_target_pairs={{0,16},{8,24},{16,0},{24,8},{1,17},{9,25},{17,1},{25,9},{2,18},{10... | collective-permute-start | bytes 2211848 | tf_op jit(solution)/shard_map/ppermute | solution.py:319
  263.2 34.1 %collective-permute-start.46 = (bf16[256,2176]{1,0:T(8,128)(2,1)S(1)}, bf16[256,2176]{1,0:T(8,128)(2,1)S(1)}, u32[]{:S(2)}, u32[]{:S(2)}) collective-permute-start(bf16[256,2176]{1,0:T(8,128)(2,1)S(1)} %shard_map.118.rest_0_), channel_id=1, source_target_pairs={{0,2},{1,3},{2,0},{3,1},{4,6},{5,7},{6,4},{7,5},{8,10},{9,11},{10,... | collective-permute-start | bytes 3342344 | tf_op jit(solution)/shard_map/ppermute | solution.py:319
  308.3 39.1 %collective-permute-start.54 = (bf16[128,2176]{1,0:T(8,128)(2,1)S(1)}, bf16[128,2176]{1,0:T(8,128)(2,1)S(1)}, u32[]{:S(2)}, u32[]{:S(2)}) collective-permute-start(bf16[128,2176]{1,0:T(8,128)(2,1)S(1)} %get-tuple-element.123), channel_id=1, source_target_pairs={{0,4},{1,5},{2,6},{3,7},{4,0},{5,1},{6,2},{7,3},{8,12},{9,13},{10,... | collective-permute-start | bytes 1671176 | tf_op jit(solution)/shard_map/ppermute | solution.py:319
  367.1 38.9 %collective-permute-start.58 = (bf16[256,2176]{1,0:T(8,128)(2,1)S(1)}, bf16[256,2176]{1,0:T(8,128)(2,1)S(1)}, u32[]{:S(2)}, u32[]{:S(2)}) collective-permute-start(bf16[256,2176]{1,0:T(8,128)(2,1)S(1)} %get-tuple-element.128), channel_id=1, source_target_pairs={{0,1},{1,0},{2,3},{3,2},{4,5},{5,4},{6,7},{7,6},{8,9},{9,8},{10,11... | collective-permute-start | bytes 3342344 | tf_op jit(solution)/shard_map/ppermute | solution.py:319
  367.2 38.8 %collective-permute-start.59 = (bf16[256,2176]{1,0:T(8,128)(2,1)S(1)}, bf16[256,2176]{1,0:T(8,128)(2,1)S(1)}, u32[]{:S(2)}, u32[]{:S(2)}) collective-permute-start(bf16[256,2176]{1,0:T(8,128)(2,1)S(1)} %copy-done.7), channel_id=1, source_target_pairs={{0,2},{1,3},{2,0},{3,1},{4,6},{5,7},{6,4},{7,5},{8,10},{9,11},{10,... | collective-permute-start | bytes 3342344 | tf_op jit(solution)/shard_map/ppermute | solution.py:319
  368.2 37.8 %collective-permute-start.60 = (bf16[128,2176]{1,0:T(8,128)(2,1)S(1)}, bf16[128,2176]{1,0:T(8,128)(2,1)S(1)}, u32[]{:S(2)}, u32[]{:S(2)}) collective-permute-start(bf16[128,2176]{1,0:T(8,128)(2,1)S(1)} %copy-done.35), channel_id=1, source_target_pairs={{0,4},{1,5},{2,6},{3,7},{4,0},{5,1},{6,2},{7,3},{8,12},{9,13},{10,... | collective-permute-start | bytes 1671176 | tf_op jit(solution)/shard_map/ppermute | solution.py:319
  (92 other events, 793.3 us)

commit v5 on v4

--- a/solution.py
+++ b/solution.py
@@ -49,8 +49,8 @@
     )
 
 
-def partial_kernel(count, me, same, other, slots, w_gate, w_up, w_down, after,
-                   own, part_x, part_y, across_a, across_b):
+def partial_kernel(count, me, same, other, slots, w_gate, w_up, w_down, *rest):
+    own, part_x, part_y, across_a, across_b = rest[-5:]
     step = pl.program_id(0)
     part, half = step // count, step % count
     tokens, width = same.shape
@@ -99,14 +99,14 @@
                 expert_block((features, hidden), halves),
                 expert_block((features, hidden), halves),
                 expert_block((hidden, features), halves),
-                pl.BlockSpec(memory_space=pl.ANY),
+                *[pl.BlockSpec(memory_space=pl.ANY)] * len(after),
             ],
             out_specs=[whole(o.shape) for o in outs],
         ),
         out_shape=outs,
         compiler_params=pltpu.CompilerParams(vmem_limit_bytes=VMEM_BYTES),
         cost_estimate=moves(ample),
-    )(me, same, other, slots, w_gate, w_up, w_down, after)
+    )(me, same, other, slots, w_gate, w_up, w_down, *after)
 
 
 def middle_kernel(me, own, from_x, from_y, slots, share, *rest):
@@ -221,8 +221,8 @@
     )(*ins, *after)
 
 
-def add_up_kernel(count, *refs):
-    ins, outs = refs[:count], refs[count + 1 :]
+def add_up_kernel(count, waits, *refs):
+    ins, outs = refs[:count], refs[count + waits :]
     for n, out in enumerate(outs):
         cut = pl.ds(n * out.shape[0], out.shape[0])
         total = ins[0][cut, :].astype(jnp.float32)
@@ -231,18 +231,19 @@
         out[...] = total.astype(jnp.bfloat16)
 
 
-def add_up(blocks, splits, after):
+def add_up(blocks, splits, *after):
     rows, width = blocks[0].shape
     out = jax.ShapeDtypeStruct((rows // splits, width), jnp.bfloat16)
     return pl.pallas_call(
-        functools.partial(add_up_kernel, len(blocks)),
+        functools.partial(add_up_kernel, len(blocks), len(after)),
         grid=(1,),
         out_shape=[out] * splits,
-        in_specs=[at_once((rows, width))] * len(blocks) + [pl.BlockSpec(memory_space=pl.ANY)],
+        in_specs=[at_once((rows, width))] * len(blocks)
+        + [pl.BlockSpec(memory_space=pl.ANY)] * len(after),
         out_specs=[at_once(out.shape)] * splits,
         compiler_params=pltpu.CompilerParams(vmem_limit_bytes=VMEM_BYTES),
         cost_estimate=moves(True),
-    )(*blocks, after)
+    )(*blocks, *after)
 
 
 def combine_kernel(count, waits, me, *refs):
@@ -372,7 +373,7 @@
         o = chunks[k][0]
         return far_share[:, o - 1] if o else near_share[:, 0]
 
-    def start_rows(k, after):
+    def start_rows(k, *after):
         o, halves = chunks[k]
         own, part_x, part_y, across_a, across_b = partial_sums(
             me, sames[o], others[o], slots_of(k), *weights, after, halves, k > 0
@@ -411,11 +412,11 @@
 
     after = start_rows(0, after)
     after = move(0, None, after)
-    after = turn_rows(0, after)
+    after = turn_rows(0, after, far_slots, far_share)
     after, sames[3], others[3] = move(None, 0, after, block=arriving)
     sames[2] = swap(sames[3], "expert", 2)
-    after = start_rows(1, after)
-    after, sames[2], others[2] = move(1, None, after, *relayed[0], block=sames[2])
+    after = start_rows(1, after, *relayed[0])
+    after, sames[2], others[2] = move(1, None, after, block=sames[2])
     after = start_rows(2, after)
     after = turn_rows(1, after)
     after = finish_rows(0, after)
@@ -425,21 +426,24 @@
     after = finish_rows(1, after)
     after, _, other = move(3, 2, after, block=blocks[1][1])
     after = start_rows(4, after)
-    (after,) = add_up([blocks[1][0], other], 1, after)
+    (after,) = add_up([blocks[1][0], other], 1, after, *relayed[2])
     hop = swap(after, "expert", 2)
-    after = turn_rows(3, after, *relayed[2], *adds[4][2:])
+    after = turn_rows(3, after, *adds[4][2:])
     after = finish_rows(2, after)
     after, _, other = move(4, 3, after, hop, block=blocks[2][1])
     after, second = add_up([blocks[2][0], other, hop], 2, after)
     far_low, far_high = swap(after, "expert", 4), swap(second, "expert", 4)
-    after = turn_rows(4, second, *relayed[3])
-    after = finish_rows(3, after)
-    after, _, other = move(None, 4, after, far_low, block=blocks[3][1])
+    after = finish_rows(3, second)
+    after = turn_rows(4, after, far_low)
+    after, _, other = move(None, None, after, block=blocks[3][1])
     (after,) = add_up([blocks[3][0], other], 1, after)
     near_back = swap(after, "expert", 2)
+    after = move(None, 4, after)
     after = finish_rows(4, after)
-    for k in (0, 4):
-        blocks[k][1] = swap(blocks[k][1], "expert", 1)
+    blocks[0][1] = swap(blocks[0][1], "expert", 1)
+    _, _, blocks[4][1] = move(
+        None, None, after, far_high, near_back, blocks[0][1], block=blocks[4][1]
+    )
     far_back = jnp.concatenate([far_low, far_high], axis=0)
     total = sum(t.astype(jnp.float32) for t in (*blocks[0], *blocks[4], near_back, far_back))
     grads = total[:, 2 * features : 2 * features + EXPERTS] + total[:, 2 * features + EXPERTS :]

time: 412 us -> 381 us (0.925)
  waiting for transfers between devices: 133 us -> 109 us
  local copies, waits for them, and re-layouts: 31.2 us -> 19.8 us
    ppermute x61, waiting for transfers between devices: 133 us -> 109 us  [swap(): return lax.ppermute(value, axis, [(n, n ^ bits) for n in range(count)])]
    unnamed x110 -> x102, local copies, waits for them, and re-layouts: 24 us -> 17 us
    pallas_call x7 -> x9, Pallas kernels: 13.1 us -> 12.9 us  [between(): pl.pallas_call(functools.partial(between_kernel, len(after), *given), gri...]
  transfers between devices with their start and end apart: 61 -> 61, of which waited for: 23 -> 25; matrix products, arithmetic and copies ran while one was open for 2% -> 1% of each run, Pallas kernels for 39% -> 44%
where the time goes in v5:
time: 381 us; the launch traced here: 378 us
  Pallas kernels  183 us (48%)
  waiting for transfers between devices  109 us (29%)
  starting transfers between devices  56.9 us (15%)
  local copies, waits for them, and re-layouts  19.8 us (5%)
  other arithmetic  7.23 us (2%)
    ppermute x61, waiting for transfers between devices, swap(): return lax.ppermute(value, axis, [(n, n ^ bits) for n in range(count)])  109 us
    pallas_call x5, Pallas kernels, combine(): pl.pallas_call(functools.partial(combine_kernel, count, len(after)), grid...  83.7 us
    pallas_call x5, Pallas kernels, partial_sums(): pl.pallas_call(functools.partial(partial_kernel, count), grid_spec=pltpu....  77 us
    ppermute x61, starting transfers between devices, swap(): return lax.ppermute(value, axis, [(n, n ^ bits) for n in range(count)])  56.9 us
    unnamed x102, local copies, waits for them, and re-layouts  17 us
    pallas_call x9, Pallas kernels, between(): pl.pallas_call(functools.partial(between_kernel, len(after), *given), gri...  12.9 us
  transfers between devices with their start and end apart: 61, of which 25 were waited for; matrix products, arithmetic and copies ran while one was open for 1% of the time, Pallas kernels for 44%

profile of v5, /device:TPU:8, one launch (start us, length us, event | category | flops | bytes accessed | tf_op | source)
XLA Modules:
  0.0 378.0 jit_solution(12255153330334196027)
XLA Ops:
  11.4 10.0 %shard_map.103 = (bf16[1,80,2304]{2,1,0:T(8,128)(2,1)S(1)}, bf16[1,80,2304]{2,1,0:T(8,128)(2,1)S(1)}, bf16[1,80,2304]{2,1,0:T(8,128)(2,1)S(1)}, bf16[1,80,1152]{2,1,0:T(8,128)(2,1)S(1)}, bf16[1,80,1152]{2,1,0:T(8,128)(2,1)S(1)}) custom-call(s32[1]{0:T(128)} %bitcast.me, bf16[256,2048]{1,0:T(8,128)(2,1)S(1)} %pad_maximum_fusion.same, ...), custom_call_target="tpu_custom_call" | custom-call | flops 1000 | bytes 1000 | tf_op jit(solution)/shard_map/pallas_call | solution.py:90
  24.5 3.8 %collective-permute-done.2.refs_2_ = bf16[1,80,1152]{2,1,0:T(8,128)(2,1)S(1)} collective-permute-done((bf16[1,80,1152]{2,1,0:T(8,128)(2,1)S(1)}, bf16[1,80,1152]{2,1,0:T(8,128)(2,1)S(1)}, u32[]{:S(2)}, u32[]{:S(2)}) %collective-permute-start.2) | collective-permute-done | bytes 184352 | tf_op jit(solution)/shard_map/ppermute | solution.py:320
  33.2 6.8 %collective-permute-done.4.from_x = bf16[1,80,2304]{2,1,0:T(8,128)(2,1)S(1)} collective-permute-done((bf16[1,80,2304]{2,1,0:T(8,128)(2,1)S(1)}, bf16[1,80,2304]{2,1,0:T(8,128)(2,1)S(1)}, u32[]{:S(2)}, u32[]{:S(2)}) %collective-permute-start.4) | collective-permute-done | bytes 368672 | tf_op jit(solution)/shard_map/ppermute | solution.py:320
  45.0 10.6 %collective-permute-done.12.refs_2_ = bf16[256,2048]{1,0:T(8,128)(2,1)S(1)} collective-permute-done((bf16[256,2048]{1,0:T(8,128)(2,1)S(1)}, bf16[256,2048]{1,0:T(8,128)(2,1)S(1)}, u32[]{:S(2)}, u32[]{:S(2)}) %collective-permute-start.12) | collective-permute-done | bytes 1048608 | tf_op jit(solution)/shard_map/ppermute | solution.py:320
  59.1 5.0 %collective-permute-done.14.rest_2_.refs_4_ = bf16[1,80,1152]{2,1,0:T(8,128)(2,1)S(1)} collective-permute-done((bf16[1,80,1152]{2,1,0:T(8,128)(2,1)S(1)}, bf16[1,80,1152]{2,1,0:T(8,128)(2,1)S(1)}, u32[]{:S(2)}, u32[]{:S(2)}) %collective-permute-start.14) | collective-permute-done | bytes 184352 | tf_op jit(solution)/shard_map/ppermute | solution.py:320
  65.1 18.8 %shard_map.107 = (bf16[2,80,2304]{2,1,0:T(8,128)(2,1)S(1)}, bf16[2,80,2304]{2,1,0:T(8,128)(2,1)S(1)}, bf16[2,80,2304]{2,1,0:T(8,128)(2,1)S(1)}, bf16[2,80,1152]{2,1,0:T(8,128)(2,1)S(1)}, bf16[2,80,1152]{2,1,0:T(8,128)(2,1)S(1)}) custom-call(s32[1]{0:T(128)} %bitcast.me, bf16[256,2048]{1,0:T(8,128)(2,1)} %copy-done.24, bf16[256,2048]{1,0:T(8,128)(2,1)} %copy-done.42, ...), custom_call_target="tpu_custom_call" | custom-call | flops 400000000 | bytes 400000000 | tf_op jit(solution)/shard_map/pallas_call | solution.py:90
  87.0 7.5 %collective-permute-done.16.refs_2_ = bf16[2,80,1152]{2,1,0:T(8,128)(2,1)S(1)} collective-permute-done((bf16[2,80,1152]{2,1,0:T(8,128)(2,1)S(1)}, bf16[2,80,1152]{2,1,0:T(8,128)(2,1)S(1)}, u32[]{:S(2)}, u32[]{:S(2)}) %collective-permute-start.16) | collective-permute-done | bytes 368672 | tf_op jit(solution)/shard_map/ppermute | solution.py:320
  102.7 18.9 %shard_map.109 = (bf16[2,80,2304]{2,1,0:T(8,128)(2,1)S(1)}, bf16[2,80,2304]{2,1,0:T(8,128)(2,1)S(1)}, bf16[2,80,2304]{2,1,0:T(8,128)(2,1)S(1)}, bf16[2,80,1152]{2,1,0:T(8,128)(2,1)S(1)}, bf16[2,80,1152]{2,1,0:T(8,128)(2,1)S(1)}) custom-call(s32[1]{0:T(128)} %bitcast.me, bf16[256,2048]{1,0:T(8,128)(2,1)} %get-tuple-element.82.same, ...), custom_call_target="tpu_custom_call" | custom-call | flops 400000000 | bytes 400000000 | tf_op jit(solution)/shard_map/pallas_call | solution.py:90
  127.3 11.5 %shard_map.111 = (bf16[256,2176]{1,0:T(8,128)(2,1)S(1)}, bf16[256,2176]{1,0:T(8,128)(2,1)}) custom-call(s32[1]{0:T(128)} %bitcast.me, bf16[1,80,2432]{2,1,0:T(8,128)(2,1)S(1)} %shard_map.105.refs_3_.refs_0_, bf16[1,80,2432]{2,1,0:T(8,128)(2,1)S(1)} %collective-permute-done.10.refs_0_.refs_1_, ...), custom_call_target="tpu_custom_call" | custom-call | flops 400000000 | bytes 400000000 | tf_op jit(solution)/shard_map/pallas_call | solution.py:292
  139.8 10.3 %collective-permute-done.23.refs_2_ = bf16[2,80,1152]{2,1,0:T(8,128)(2,1)S(1)} collective-permute-done((bf16[2,80,1152]{2,1,0:T(8,128)(2,1)S(1)}, bf16[2,80,1152]{2,1,0:T(8,128)(2,1)S(1)}, u32[]{:S(2)}, u32[]{:S(2)}) %collective-permute-start.23) | collective-permute-done | bytes 368672 | tf_op jit(solution)/shard_map/ppermute | solution.py:320
  160.1 19.0 %shard_map.113 = (bf16[2,80,2304]{2,1,0:T(8,128)(2,1)S(1)}, bf16[2,80,2304]{2,1,0:T(8,128)(2,1)S(1)}, bf16[2,80,2304]{2,1,0:T(8,128)(2,1)S(1)}, bf16[2,80,1152]{2,1,0:T(8,128)(2,1)S(1)}, bf16[2,80,1152]{2,1,0:T(8,128)(2,1)S(1)}) custom-call(s32[1]{0:T(128)} %bitcast.me, bf16[256,2048]{1,0:T(8,128)(2,1)} %get-tuple-element.90.same, ...), custom_call_target="tpu_custom_call" | custom-call | flops 400000000 | bytes 400000000 | tf_op jit(solution)/shard_map/pallas_call | solution.py:90
  179.1 3.5 collective-permute-done.34.rest_2_.refs_4_
  189.5 20.3 %shard_map.115 = (bf16[256,2176]{1,0:T(8,128)(2,1)}, bf16[256,2176]{1,0:T(8,128)(2,1)}) custom-call(s32[1]{0:T(128)} %bitcast.me, bf16[2,80,2432]{2,1,0:T(8,128)(2,1)S(1)} %shard_map.110.refs_9_.refs_0_, bf16[2,80,2432]{2,1,0:T(8,128)(2,1)S(1)} %copy-done.18, bf16[2,80,2432]{2,1,0:T(8,128)(2,1)S(1)} %copy-done.20, ...), custom_call_target="tpu_custom_call" | custom-call | flops 400000000 | bytes 400000000 | tf_op jit(solution)/shard_map/pallas_call | solution.py:292
  213.3 3.1 shard_map.116
  220.5 10.4 %shard_map.117 = (bf16[1,80,2304]{2,1,0:T(8,128)(2,1)S(1)}, bf16[1,80,2304]{2,1,0:T(8,128)(2,1)S(1)}, bf16[1,80,2304]{2,1,0:T(8,128)(2,1)S(1)}, bf16[1,80,1152]{2,1,0:T(8,128)(2,1)S(1)}, bf16[1,80,1152]{2,1,0:T(8,128)(2,1)S(1)}) custom-call(s32[1]{0:T(128)} %bitcast.me, bf16[256,2048]{1,0:T(8,128)(2,1)S(1)} %pad_maximum_fusion.same, ...), custom_call_target="tpu_custom_call" | custom-call | flops 400000000 | bytes 400000000 | tf_op jit(solution)/shard_map/pallas_call | solution.py:90
  230.9 13.8 %collective-permute-done.43.refs_4_ = bf16[2,80,1152]{2,1,0:T(8,128)(2,1)S(1)} collective-permute-done((bf16[2,80,1152]{2,1,0:T(8,128)(2,1)S(1)}, bf16[2,80,1152]{2,1,0:T(8,128)(2,1)S(1)}, u32[]{:S(2)}, u32[]{:S(2)}) %collective-permute-start.43) | collective-permute-done | bytes 368672 | tf_op jit(solution)/shard_map/ppermute | solution.py:320
  257.9 20.4 %shard_map.120 = (bf16[256,2176]{1,0:T(8,128)(2,1)}, bf16[256,2176]{1,0:T(8,128)(2,1)}) custom-call(s32[1]{0:T(128)} %bitcast.me, bf16[2,80,2432]{2,1,0:T(8,128)(2,1)S(1)} %copy-done.1, bf16[2,80,2432]{2,1,0:T(8,128)(2,1)S(1)} %copy-done.14, bf16[2,80,2432]{2,1,0:T(8,128)(2,1)S(1)} %copy-done.16, bf16[2,80,1280]{2,1,0:T(8,128)(2,1)S(1)} %collective-permute-done.42.refs_3_, ...), custom_call_target="tpu_custom_call" | custom-call | flops 400000000 | bytes 400000000 | tf_op jit(solution)/shard_map/pallas_call | solution.py:292
  279.5 3.2 shard_map.121
  294.4 8.8 %collective-permute-done.50.refs_4_ = bf16[2,80,1152]{2,1,0:T(8,128)(2,1)} collective-permute-done((bf16[2,80,1152]{2,1,0:T(8,128)(2,1)}, bf16[2,80,1152]{2,1,0:T(8,128)(2,1)}, u32[]{:S(2)}, u32[]{:S(2)}) %collective-permute-start.50) | collective-permute-done | bytes 368672 | tf_op jit(solution)/shard_map/ppermute | solution.py:320
  304.3 21.0 %shard_map.123 = (bf16[256,2176]{1,0:T(8,128)(2,1)}, bf16[256,2176]{1,0:T(8,128)(2,1)}) custom-call(s32[1]{0:T(128)} %bitcast.me, bf16[2,80,2432]{2,1,0:T(8,128)(2,1)S(1)} %shard_map.119.refs_9_.refs_0_, bf16[2,80,2432]{2,1,0:T(8,128)(2,1)S(1)} %collective-permute-done.44.refs_4_.refs_1_, bf16[2,80,2432]{2,1,0:T(8,128)(2,1)S(1)} %copy-done.12, ...), custom_call_target="tpu_custom_call" | custom-call | flops 400000000 | bytes 400000000 | tf_op jit(solution)/shard_map/pallas_call | solution.py:292
  335.5 8.1 %collective-permute-done.53.refs_0_.refs_1_ = bf16[1,80,2432]{2,1,0:T(8,128)(2,1)S(1)} collective-permute-done((bf16[1,80,2432]{2,1,0:T(8,128)(2,1)S(1)}, bf16[1,80,2432]{2,1,0:T(8,128)(2,1)S(1)}, u32[]{:S(2)}, u32[]{:S(2)}) %collective-permute-start.53) | collective-permute-done | bytes 389152 | tf_op jit(solution)/shard_map/ppermute | solution.py:320
  345.9 5.0 %collective-permute-done.57.refs_4_ = bf16[1,80,1152]{2,1,0:T(8,128)(2,1)S(1)} collective-permute-done((bf16[1,80,1152]{2,1,0:T(8,128)(2,1)S(1)}, bf16[1,80,1152]{2,1,0:T(8,128)(2,1)S(1)}, u32[]{:S(2)}, u32[]{:S(2)}) %collective-permute-start.57) | collective-permute-done | bytes 184352 | tf_op jit(solution)/shard_map/ppermute | solution.py:320
  351.0 10.5 %shard_map.128 = (bf16[256,2176]{1,0:T(8,128)(2,1)S(1)}, bf16[256,2176]{1,0:T(8,128)(2,1)S(1)}) custom-call(s32[1]{0:T(128)} %bitcast.me, bf16[1,80,2432]{2,1,0:T(8,128)(2,1)S(1)} %shard_map.124.refs_1_.refs_0_, bf16[1,80,2432]{2,1,0:T(8,128)(2,1)S(1)} %collective-permute-done.53.refs_0_.refs_1_, ...), custom_call_target="tpu_custom_call" | custom-call | flops 400000000 | bytes 400000000 | tf_op jit(solution)/shard_map/pallas_call | solution.py:292
  361.5 8.2 %collective-permute-done.58.refs_2_ = bf16[128,2176]{1,0:T(8,128)(2,1)S(1)} collective-permute-done((bf16[128,2176]{1,0:T(8,128)(2,1)S(1)}, bf16[128,2176]{1,0:T(8,128)(2,1)S(1)}, u32[]{:S(2)}, u32[]{:S(2)}) %collective-permute-start.58) | collective-permute-done | bytes 557088 | tf_op jit(solution)/shard_map/ppermute | solution.py:320
  (272 shorter events, 118.2 us)
Async XLA Ops:
  7.6 48.1 %collective-permute-start.12 = (bf16[256,2048]{1,0:T(8,128)(2,1)S(1)}, bf16[256,2048]{1,0:T(8,128)(2,1)S(1)}, u32[]{:S(2)}, u32[]{:S(2)}) collective-permute-start(bf16[256,2048]{1,0:T(8,128)(2,1)S(1)} %pad_maximum_fusion.same), channel_id=1, source_target_pairs={{0,6},{1,7},{2,4},{3,5},{4,2},{5,3},{6,0},{7,1},{8,14},{9,15},{10,... | collective-permute-start | bytes 3145736 | tf_op jit(solution)/shard_map/ppermute | solution.py:320
  55.9 31.2 %collective-permute-start.18 = (bf16[256,2048]{1,0:T(8,128)(2,1)S(1)}, bf16[256,2048]{1,0:T(8,128)(2,1)S(1)}, u32[]{:S(2)}, u32[]{:S(2)}) collective-permute-start(bf16[256,2048]{1,0:T(8,128)(2,1)S(1)} %get-tuple-element.74.same), channel_id=1, source_target_pairs={{0,2},{1,3},{2,0},{3,1},{4,6},{5,7},{6,4},{7,5},{8,10},{9,11},{10,... | collective-permute-start | bytes 3145736 | tf_op jit(solution)/shard_map/ppermute | solution.py:320
  100.1 39.7 %collective-permute-start.27 = (bf16[256,2048]{1,0:T(8,128)(2,1)S(1)}, bf16[256,2048]{1,0:T(8,128)(2,1)S(1)}, u32[]{:S(2)}, u32[]{:S(2)}) collective-permute-start(bf16[256,2048]{1,0:T(8,128)(2,1)S(1)} %pad_maximum_fusion.same), channel_id=1, source_target_pairs={{0,2},{1,3},{2,0},{3,1},{4,6},{5,7},{6,4},{7,5},{8,10},{9,11},{10,... | collective-permute-start | bytes 3145736 | tf_op jit(solution)/shard_map/ppermute | solution.py:320
  123.2 27.7 %collective-permute-start.25 = (bf16[2,80,2432]{2,1,0:T(8,128)(2,1)S(1)}, bf16[2,80,2432]{2,1,0:T(8,128)(2,1)S(1)}, u32[]{:S(2)}, u32[]{:S(2)}) collective-permute-start(bf16[2,80,2432]{2,1,0:T(8,128)(2,1)S(1)} %shard_map.110.refs_9_.refs_0_), channel_id=1, source_target_pairs={{0,8},{8,0},{16,24},{24,16},{1,9},{9,1},{17,25},{25,17},{2,10},{10... | collective-permute-start | bytes 2334728 | tf_op jit(solution)/shard_map/ppermute | solution.py:320
  124.3 26.6 %collective-permute-start.26 = (bf16[2,80,2432]{2,1,0:T(8,128)(2,1)S(1)}, bf16[2,80,2432]{2,1,0:T(8,128)(2,1)S(1)}, u32[]{:S(2)}, u32[]{:S(2)}) collective-permute-start(bf16[2,80,2432]{2,1,0:T(8,128)(2,1)S(1)} %shard_map.110.refs_9_.refs_0_), channel_id=1, source_target_pairs={{0,16},{8,24},{16,0},{24,8},{1,17},{9,25},{17,1},{25,9},{2,18},{10... | collective-permute-start | bytes 2334728 | tf_op jit(solution)/shard_map/ppermute | solution.py:320
  124.8 25.3 %collective-permute-start.23 = (bf16[2,80,1152]{2,1,0:T(8,128)(2,1)S(1)}, bf16[2,80,1152]{2,1,0:T(8,128)(2,1)S(1)}, u32[]{:S(2)}, u32[]{:S(2)}) collective-permute-start(bf16[2,80,1152]{2,1,0:T(8,128)(2,1)S(1)} %get-tuple-element.88), channel_id=1, source_target_pairs={{0,8},{8,0},{16,24},{24,16},{1,9},{9,1},{17,25},{25,17},{2,10},{10... | collective-permute-start | bytes 1105928 | tf_op jit(solution)/shard_map/ppermute | solution.py:320
  155.1 27.7 %collective-permute-start.31 = (bf16[2,80,2304]{2,1,0:T(8,128)(2,1)S(1)}, bf16[2,80,2304]{2,1,0:T(8,128)(2,1)S(1)}, u32[]{:S(2)}, u32[]{:S(2)}) collective-permute-start(bf16[2,80,2304]{2,1,0:T(8,128)(2,1)S(1)} %get-tuple-element.91.rest_0_), channel_id=1, source_target_pairs={{0,8},{8,0},{16,24},{24,16},{1,9},{9,1},{17,25},{25,17},{2,10},{10... | collective-permute-start | bytes 2211848 | tf_op jit(solution)/shard_map/ppermute | solution.py:320
  156.1 26.7 %collective-permute-start.32 = (bf16[2,80,2304]{2,1,0:T(8,128)(2,1)S(1)}, bf16[2,80,2304]{2,1,0:T(8,128)(2,1)S(1)}, u32[]{:S(2)}, u32[]{:S(2)}) collective-permute-start(bf16[2,80,2304]{2,1,0:T(8,128)(2,1)S(1)} %get-tuple-element.96), channel_id=1, source_target_pairs={{0,16},{8,24},{16,0},{24,8},{1,17},{9,25},{17,1},{25,9},{2,18},{10... | collective-permute-start | bytes 2211848 | tf_op jit(solution)/shard_map/ppermute | solution.py:320
  156.8 26.0 %collective-permute-start.33 = (bf16[2,80,1280]{2,1,0:T(8,128)(2,1)S(1)}, bf16[2,80,1280]{2,1,0:T(8,128)(2,1)S(1)}, u32[]{:S(2)}, u32[]{:S(2)}) collective-permute-start(bf16[2,80,1280]{2,1,0:T(8,128)(2,1)S(1)} %get-tuple-element.98), channel_id=1, source_target_pairs={{0,8},{8,0},{16,24},{24,16},{1,9},{9,1},{17,25},{25,17},{2,10},{10... | collective-permute-start | bytes 1228808 | tf_op jit(solution)/shard_map/ppermute | solution.py:320
  184.3 27.8 %collective-permute-start.35 = (bf16[2,80,2432]{2,1,0:T(8,128)(2,1)}, bf16[2,80,2432]{2,1,0:T(8,128)(2,1)S(1)}, u32[]{:S(2)}, u32[]{:S(2)}) collective-permute-start(bf16[2,80,2432]{2,1,0:T(8,128)(2,1)} %shard_map.114.refs_9_.refs_0_), channel_id=1, source_target_pairs={{0,8},{8,0},{16,24},{24,16},{1,9},{9,1},{17,25},{25,17},{2,10},{10... | collective-permute-start | bytes 2334728 | tf_op jit(solution)/shard_map/ppermute | solution.py:320
  185.3 26.8 %collective-permute-start.36 = (bf16[2,80,2432]{2,1,0:T(8,128)(2,1)}, bf16[2,80,2432]{2,1,0:T(8,128)(2,1)S(1)}, u32[]{:S(2)}, u32[]{:S(2)}) collective-permute-start(bf16[2,80,2432]{2,1,0:T(8,128)(2,1)} %shard_map.114.refs_9_.refs_0_), channel_id=1, source_target_pairs={{0,16},{8,24},{16,0},{24,8},{1,17},{9,25},{17,1},{25,9},{2,18},{10... | collective-permute-start | bytes 2334728 | tf_op jit(solution)/shard_map/ppermute | solution.py:320
  186.0 25.4 %collective-permute-start.29 = (bf16[2,80,1152]{2,1,0:T(8,128)(2,1)S(1)}, bf16[2,80,1152]{2,1,0:T(8,128)(2,1)S(1)}, u32[]{:S(2)}, u32[]{:S(2)}) collective-permute-start(bf16[2,80,1152]{2,1,0:T(8,128)(2,1)S(1)} %get-tuple-element.94), channel_id=1, source_target_pairs={{0,8},{8,0},{16,24},{24,16},{1,9},{9,1},{17,25},{25,17},{2,10},{10... | collective-permute-start | bytes 1105928 | tf_op jit(solution)/shard_map/ppermute | solution.py:320
  216.4 28.3 %collective-permute-start.41 = (bf16[256,2176]{1,0:T(8,128)(2,1)}, bf16[256,2176]{1,0:T(8,128)(2,1)S(1)}, u32[]{:S(2)}, u32[]{:S(2)}) collective-permute-start(bf16[256,2176]{1,0:T(8,128)(2,1)} %get-tuple-element.109), channel_id=1, source_target_pairs={{0,1},{1,0},{2,3},{3,2},{4,5},{5,4},{6,7},{7,6},{8,9},{9,8},{10,11... | collective-permute-start | bytes 3342344 | tf_op jit(solution)/shard_map/ppermute | solution.py:320
  216.4 28.3 %collective-permute-start.42 = (bf16[2,80,1280]{2,1,0:T(8,128)(2,1)S(1)}, bf16[2,80,1280]{2,1,0:T(8,128)(2,1)S(1)}, u32[]{:S(2)}, u32[]{:S(2)}) collective-permute-start(bf16[2,80,1280]{2,1,0:T(8,128)(2,1)S(1)} %get-tuple-element.110), channel_id=1, source_target_pairs={{0,8},{8,0},{16,24},{24,16},{1,9},{9,1},{17,25},{25,17},{2,10},{10... | collective-permute-start | bytes 1228808 | tf_op jit(solution)/shard_map/ppermute | solution.py:320
  217.5 37.1 %collective-permute-start.39 = (bf16[2,80,2304]{2,1,0:T(8,128)(2,1)S(1)}, bf16[2,80,2304]{2,1,0:T(8,128)(2,1)S(1)}, u32[]{:S(2)}, u32[]{:S(2)}) collective-permute-start(bf16[2,80,2304]{2,1,0:T(8,128)(2,1)S(1)} %get-tuple-element.102.rest_0_), channel_id=1, source_target_pairs={{0,8},{8,0},{16,24},{24,16},{1,9},{9,1},{17,25},{25,17},{2,10},{10... | collective-permute-start | bytes 2211848 | tf_op jit(solution)/shard_map/ppermute | solution.py:320
  218.5 36.1 %collective-permute-start.40 = (bf16[2,80,2304]{2,1,0:T(8,128)(2,1)S(1)}, bf16[2,80,2304]{2,1,0:T(8,128)(2,1)S(1)}, u32[]{:S(2)}, u32[]{:S(2)}) collective-permute-start(bf16[2,80,2304]{2,1,0:T(8,128)(2,1)S(1)} %get-tuple-element.108), channel_id=1, source_target_pairs={{0,16},{8,24},{16,0},{24,8},{1,17},{9,25},{17,1},{25,9},{2,18},{10... | collective-permute-start | bytes 2211848 | tf_op jit(solution)/shard_map/ppermute | solution.py:320
  219.2 25.5 %collective-permute-start.43 = (bf16[2,80,1152]{2,1,0:T(8,128)(2,1)S(1)}, bf16[2,80,1152]{2,1,0:T(8,128)(2,1)S(1)}, u32[]{:S(2)}, u32[]{:S(2)}) collective-permute-start(bf16[2,80,1152]{2,1,0:T(8,128)(2,1)S(1)} %get-tuple-element.111), channel_id=1, source_target_pairs={{0,16},{8,24},{16,0},{24,8},{1,17},{9,25},{17,1},{25,9},{2,18},{10... | collective-permute-start | bytes 1105928 | tf_op jit(solution)/shard_map/ppermute | solution.py:320
  247.3 31.0 %collective-permute-start.46 = (bf16[256,2176]{1,0:T(8,128)(2,1)S(1)}, bf16[256,2176]{1,0:T(8,128)(2,1)S(1)}, u32[]{:S(2)}, u32[]{:S(2)}) collective-permute-start(bf16[256,2176]{1,0:T(8,128)(2,1)S(1)} %shard_map.118.rest_0_), channel_id=1, source_target_pairs={{0,2},{1,3},{2,0},{3,1},{4,6},{5,7},{6,4},{7,5},{8,10},{9,11},{10,... | collective-permute-start | bytes 3342344 | tf_op jit(solution)/shard_map/ppermute | solution.py:320
  288.9 36.4 %collective-permute-start.52 = (bf16[128,2176]{1,0:T(8,128)(2,1)}, bf16[128,2176]{1,0:T(8,128)(2,1)S(1)}, u32[]{:S(2)}, u32[]{:S(2)}) collective-permute-start(bf16[128,2176]{1,0:T(8,128)(2,1)} %get-tuple-element.121), channel_id=1, source_target_pairs={{0,4},{1,5},{2,6},{3,7},{4,0},{5,1},{6,2},{7,3},{8,12},{9,13},{10,... | collective-permute-start | bytes 1671176 | tf_op jit(solution)/shard_map/ppermute | solution.py:320
  292.7 32.5 %collective-permute-start.47 = (bf16[1,80,2304]{2,1,0:T(8,128)(2,1)}, bf16[1,80,2304]{2,1,0:T(8,128)(2,1)}, u32[]{:S(2)}, u32[]{:S(2)}) collective-permute-start(bf16[1,80,2304]{2,1,0:T(8,128)(2,1)} %get-tuple-element.114.refs_3_), channel_id=1, source_target_pairs={{0,8},{8,0},{16,24},{24,16},{1,9},{9,1},{17,25},{25,17},{2,10},{10... | collective-permute-start | bytes 1105928 | tf_op jit(solution)/shard_map/ppermute | solution.py:320
  293.7 31.5 %collective-permute-start.48 = (bf16[1,80,2304]{2,1,0:T(8,128)(2,1)}, bf16[1,80,2304]{2,1,0:T(8,128)(2,1)}, u32[]{:S(2)}, u32[]{:S(2)}) collective-permute-start(bf16[1,80,2304]{2,1,0:T(8,128)(2,1)} %get-tuple-element.115), channel_id=1, source_target_pairs={{0,16},{8,24},{16,0},{24,8},{1,17},{9,25},{17,1},{25,9},{2,18},{10... | collective-permute-start | bytes 1105928 | tf_op jit(solution)/shard_map/ppermute | solution.py:320
  329.7 31.9 %collective-permute-start.22 = (bf16[256,2176]{1,0:T(8,128)(2,1)S(1)}, bf16[256,2176]{1,0:T(8,128)(2,1)S(1)}, u32[]{:S(2)}, u32[]{:S(2)}) collective-permute-start(bf16[256,2176]{1,0:T(8,128)(2,1)S(1)} %copy-done.49), channel_id=1, source_target_pairs={{0,1},{1,0},{2,3},{3,2},{4,5},{5,4},{6,7},{7,6},{8,9},{9,8},{10,11... | collective-permute-start | bytes 3342344 | tf_op jit(solution)/shard_map/ppermute | solution.py:320
  331.2 38.5 %collective-permute-start.59 = (bf16[256,2176]{1,0:T(8,128)(2,1)S(1)}, bf16[256,2176]{1,0:T(8,128)(2,1)S(1)}, u32[]{:S(2)}, u32[]{:S(2)}) collective-permute-start(bf16[256,2176]{1,0:T(8,128)(2,1)S(1)} %shard_map.126.refs_2_), channel_id=1, source_target_pairs={{0,2},{1,3},{2,0},{3,1},{4,6},{5,7},{6,4},{7,5},{8,10},{9,11},{10,... | collective-permute-start | bytes 3342344 | tf_op jit(solution)/shard_map/ppermute | solution.py:320
  334.3 35.4 %collective-permute-start.58 = (bf16[128,2176]{1,0:T(8,128)(2,1)S(1)}, bf16[128,2176]{1,0:T(8,128)(2,1)S(1)}, u32[]{:S(2)}, u32[]{:S(2)}) collective-permute-start(bf16[128,2176]{1,0:T(8,128)(2,1)S(1)} %copy-done.29), channel_id=1, source_target_pairs={{0,4},{1,5},{2,6},{3,7},{4,0},{5,1},{6,2},{7,3},{8,12},{9,13},{10,... | collective-permute-start | bytes 1671176 | tf_op jit(solution)/shard_map/ppermute | solution.py:320
  (88 other events, 775.4 us)

commit v6 on v5

--- a/solution.py
+++ b/solution.py
@@ -415,10 +415,10 @@
     after = turn_rows(0, after, far_slots, far_share)
     after, sames[3], others[3] = move(None, 0, after, block=arriving)
     sames[2] = swap(sames[3], "expert", 2)
-    after = start_rows(1, after, *relayed[0])
+    after = start_rows(1, after)
     after, sames[2], others[2] = move(1, None, after, block=sames[2])
     after = start_rows(2, after)
-    after = turn_rows(1, after)
+    after = turn_rows(1, after, *relayed[0])
     after = finish_rows(0, after)
     after, sames[1], others[1] = move(2, 1, after, block=sames[1])
     after = start_rows(3, after)

time: 381 us -> 377 us (0.990)
    unnamed x102 -> x98, local copies, waits for them, and re-layouts: 17 us -> 16.2 us
where the time goes in v6:
time: 377 us; the launch traced here: 374 us
  Pallas kernels  183 us (49%)
  waiting for transfers between devices  108 us (29%)
  starting transfers between devices  54.9 us (15%)
  local copies, waits for them, and re-layouts  19 us (5%)
  other arithmetic  7.23 us (2%)
    ppermute x61, waiting for transfers between devices, swap(): return lax.ppermute(value, axis, [(n, n ^ bits) for n in range(count)])  108 us
    pallas_call x5, Pallas kernels, combine(): pl.pallas_call(functools.partial(combine_kernel, count, len(after)), grid...  83.6 us
    pallas_call x5, Pallas kernels, partial_sums(): pl.pallas_call(functools.partial(partial_kernel, count), grid_spec=pltpu....  77 us
    ppermute x61, starting transfers between devices, swap(): return lax.ppermute(value, axis, [(n, n ^ bits) for n in range(count)])  54.9 us
    unnamed x98, local copies, waits for them, and re-layouts  16.2 us
    pallas_call x9, Pallas kernels, between(): pl.pallas_call(functools.partial(between_kernel, len(after), *given), gri...  12.9 us
  transfers between devices with their start and end apart: 61, of which 25 were waited for; matrix products, arithmetic and copies ran while one was open for 1% of the time, Pallas kernels for 44%

profile of v6, /device:TPU:8, one launch (start us, length us, event | category | flops | bytes accessed | tf_op | source)
XLA Modules:
  0.0 373.6 jit_solution(6906198577511466850)
XLA Ops:
  11.4 10.0 %shard_map.103 = (bf16[1,80,2304]{2,1,0:T(8,128)(2,1)S(1)}, bf16[1,80,2304]{2,1,0:T(8,128)(2,1)S(1)}, bf16[1,80,2304]{2,1,0:T(8,128)(2,1)S(1)}, bf16[1,80,1152]{2,1,0:T(8,128)(2,1)S(1)}, bf16[1,80,1152]{2,1,0:T(8,128)(2,1)S(1)}) custom-call(s32[1]{0:T(128)} %bitcast.me, bf16[256,2048]{1,0:T(8,128)(2,1)S(1)} %pad_maximum_fusion.same, ...), custom_call_target="tpu_custom_call" | custom-call | flops 1000 | bytes 1000 | tf_op jit(solution)/shard_map/pallas_call | solution.py:90
  24.5 3.8 %collective-permute-done.2.refs_2_ = bf16[1,80,1152]{2,1,0:T(8,128)(2,1)S(1)} collective-permute-done((bf16[1,80,1152]{2,1,0:T(8,128)(2,1)S(1)}, bf16[1,80,1152]{2,1,0:T(8,128)(2,1)S(1)}, u32[]{:S(2)}, u32[]{:S(2)}) %collective-permute-start.2) | collective-permute-done | bytes 184352 | tf_op jit(solution)/shard_map/ppermute | solution.py:320
  33.2 6.8 %collective-permute-done.4.from_x = bf16[1,80,2304]{2,1,0:T(8,128)(2,1)S(1)} collective-permute-done((bf16[1,80,2304]{2,1,0:T(8,128)(2,1)S(1)}, bf16[1,80,2304]{2,1,0:T(8,128)(2,1)S(1)}, u32[]{:S(2)}, u32[]{:S(2)}) %collective-permute-start.4) | collective-permute-done | bytes 368672 | tf_op jit(solution)/shard_map/ppermute | solution.py:320
  45.0 10.7 %collective-permute-done.12.refs_2_ = bf16[256,2048]{1,0:T(8,128)(2,1)S(1)} collective-permute-done((bf16[256,2048]{1,0:T(8,128)(2,1)S(1)}, bf16[256,2048]{1,0:T(8,128)(2,1)S(1)}, u32[]{:S(2)}, u32[]{:S(2)}) %collective-permute-start.12) | collective-permute-done | bytes 1048608 | tf_op jit(solution)/shard_map/ppermute | solution.py:320
  59.5 18.8 %shard_map.107 = (bf16[2,80,2304]{2,1,0:T(8,128)(2,1)S(1)}, bf16[2,80,2304]{2,1,0:T(8,128)(2,1)S(1)}, bf16[2,80,2304]{2,1,0:T(8,128)(2,1)S(1)}, bf16[2,80,1152]{2,1,0:T(8,128)(2,1)S(1)}, bf16[2,80,1152]{2,1,0:T(8,128)(2,1)S(1)}) custom-call(s32[1]{0:T(128)} %bitcast.me, bf16[256,2048]{1,0:T(8,128)(2,1)} %copy-done.24, bf16[256,2048]{1,0:T(8,128)(2,1)} %copy-done.40, ...), custom_call_target="tpu_custom_call" | custom-call | flops 400000000 | bytes 400000000 | tf_op jit(solution)/shard_map/pallas_call | solution.py:90
  82.2 7.6 %collective-permute-done.16.refs_2_ = bf16[2,80,1152]{2,1,0:T(8,128)(2,1)S(1)} collective-permute-done((bf16[2,80,1152]{2,1,0:T(8,128)(2,1)S(1)}, bf16[2,80,1152]{2,1,0:T(8,128)(2,1)S(1)}, u32[]{:S(2)}, u32[]{:S(2)}) %collective-permute-start.16) | collective-permute-done | bytes 368672 | tf_op jit(solution)/shard_map/ppermute | solution.py:320
  97.9 18.9 %shard_map.109 = (bf16[2,80,2304]{2,1,0:T(8,128)(2,1)S(1)}, bf16[2,80,2304]{2,1,0:T(8,128)(2,1)S(1)}, bf16[2,80,2304]{2,1,0:T(8,128)(2,1)S(1)}, bf16[2,80,1152]{2,1,0:T(8,128)(2,1)S(1)}, bf16[2,80,1152]{2,1,0:T(8,128)(2,1)S(1)}) custom-call(s32[1]{0:T(128)} %bitcast.me, bf16[256,2048]{1,0:T(8,128)(2,1)} %get-tuple-element.82.same, ...), custom_call_target="tpu_custom_call" | custom-call | flops 400000000 | bytes 400000000 | tf_op jit(solution)/shard_map/pallas_call | solution.py:90
  122.5 11.5 %shard_map.111 = (bf16[256,2176]{1,0:T(8,128)(2,1)S(1)}, bf16[256,2176]{1,0:T(8,128)(2,1)}) custom-call(s32[1]{0:T(128)} %bitcast.me, bf16[1,80,2432]{2,1,0:T(8,128)(2,1)S(1)} %shard_map.105.refs_3_.refs_0_, bf16[1,80,2432]{2,1,0:T(8,128)(2,1)S(1)} %collective-permute-done.10.refs_0_.refs_1_, ...), custom_call_target="tpu_custom_call" | custom-call | flops 400000000 | bytes 400000000 | tf_op jit(solution)/shard_map/pallas_call | solution.py:292
  135.0 10.3 %collective-permute-done.23.refs_2_ = bf16[2,80,1152]{2,1,0:T(8,128)(2,1)S(1)} collective-permute-done((bf16[2,80,1152]{2,1,0:T(8,128)(2,1)S(1)}, bf16[2,80,1152]{2,1,0:T(8,128)(2,1)S(1)}, u32[]{:S(2)}, u32[]{:S(2)}) %collective-permute-start.23) | collective-permute-done | bytes 368672 | tf_op jit(solution)/shard_map/ppermute | solution.py:320
  154.8 19.0 %shard_map.113 = (bf16[2,80,2304]{2,1,0:T(8,128)(2,1)S(1)}, bf16[2,80,2304]{2,1,0:T(8,128)(2,1)S(1)}, bf16[2,80,2304]{2,1,0:T(8,128)(2,1)S(1)}, bf16[2,80,1152]{2,1,0:T(8,128)(2,1)S(1)}, bf16[2,80,1152]{2,1,0:T(8,128)(2,1)S(1)}) custom-call(s32[1]{0:T(128)} %bitcast.me, bf16[256,2048]{1,0:T(8,128)(2,1)} %get-tuple-element.90.same, ...), custom_call_target="tpu_custom_call" | custom-call | flops 400000000 | bytes 400000000 | tf_op jit(solution)/shard_map/pallas_call | solution.py:90
  173.8 4.0 %collective-permute-done.34.rest_2_.refs_4_ = bf16[2,80,1152]{2,1,0:T(8,128)(2,1)S(1)} collective-permute-done((bf16[2,80,1152]{2,1,0:T(8,128)(2,1)S(1)}, bf16[2,80,1152]{2,1,0:T(8,128)(2,1)S(1)}, u32[]{:S(2)}, u32[]{:S(2)}) %collective-permute-start.34) | collective-permute-done | bytes 368672 | tf_op jit(solution)/shard_map/ppermute | solution.py:320
  184.6 20.3 %shard_map.115 = (bf16[256,2176]{1,0:T(8,128)(2,1)}, bf16[256,2176]{1,0:T(8,128)(2,1)}) custom-call(s32[1]{0:T(128)} %bitcast.me, bf16[2,80,2432]{2,1,0:T(8,128)(2,1)S(1)} %shard_map.110.refs_9_.refs_0_, bf16[2,80,2432]{2,1,0:T(8,128)(2,1)S(1)} %copy-done.18, bf16[2,80,2432]{2,1,0:T(8,128)(2,1)S(1)} %copy-done.20, ...), custom_call_target="tpu_custom_call" | custom-call | flops 400000000 | bytes 400000000 | tf_op jit(solution)/shard_map/pallas_call | solution.py:292
  208.5 3.1 shard_map.116
  215.7 10.4 %shard_map.117 = (bf16[1,80,2304]{2,1,0:T(8,128)(2,1)S(1)}, bf16[1,80,2304]{2,1,0:T(8,128)(2,1)S(1)}, bf16[1,80,2304]{2,1,0:T(8,128)(2,1)S(1)}, bf16[1,80,1152]{2,1,0:T(8,128)(2,1)S(1)}, bf16[1,80,1152]{2,1,0:T(8,128)(2,1)S(1)}) custom-call(s32[1]{0:T(128)} %bitcast.me, bf16[256,2048]{1,0:T(8,128)(2,1)S(1)} %pad_maximum_fusion.same, ...), custom_call_target="tpu_custom_call" | custom-call | flops 400000000 | bytes 400000000 | tf_op jit(solution)/shard_map/pallas_call | solution.py:90
  226.1 13.8 %collective-permute-done.43.refs_4_ = bf16[2,80,1152]{2,1,0:T(8,128)(2,1)S(1)} collective-permute-done((bf16[2,80,1152]{2,1,0:T(8,128)(2,1)S(1)}, bf16[2,80,1152]{2,1,0:T(8,128)(2,1)S(1)}, u32[]{:S(2)}, u32[]{:S(2)}) %collective-permute-start.43) | collective-permute-done | bytes 368672 | tf_op jit(solution)/shard_map/ppermute | solution.py:320
  245.7 4.1 %collective-permute-done.37.rest_1_.refs_2_ = bf16[1,80,1152]{2,1,0:T(8,128)(2,1)S(1)} collective-permute-done((bf16[1,80,1152]{2,1,0:T(8,128)(2,1)S(1)}, bf16[1,80,1152]{2,1,0:T(8,128)(2,1)S(1)}, u32[]{:S(2)}, u32[]{:S(2)}) %collective-permute-start.37) | collective-permute-done | bytes 184352 | tf_op jit(solution)/shard_map/ppermute | solution.py:320
  253.4 20.4 %shard_map.120 = (bf16[256,2176]{1,0:T(8,128)(2,1)}, bf16[256,2176]{1,0:T(8,128)(2,1)}) custom-call(s32[1]{0:T(128)} %bitcast.me, bf16[2,80,2432]{2,1,0:T(8,128)(2,1)S(1)} %copy-done.1, bf16[2,80,2432]{2,1,0:T(8,128)(2,1)S(1)} %copy-done.14, bf16[2,80,2432]{2,1,0:T(8,128)(2,1)S(1)} %copy-done.16, bf16[2,80,1280]{2,1,0:T(8,128)(2,1)S(1)} %collective-permute-done.42.refs_3_, ...), custom_call_target="tpu_custom_call" | custom-call | flops 400000000 | bytes 400000000 | tf_op jit(solution)/shard_map/pallas_call | solution.py:292
  275.1 3.2 shard_map.121
  290.1 8.3 %collective-permute-done.50.refs_4_ = bf16[2,80,1152]{2,1,0:T(8,128)(2,1)} collective-permute-done((bf16[2,80,1152]{2,1,0:T(8,128)(2,1)}, bf16[2,80,1152]{2,1,0:T(8,128)(2,1)}, u32[]{:S(2)}, u32[]{:S(2)}) %collective-permute-start.50) | collective-permute-done | bytes 368672 | tf_op jit(solution)/shard_map/ppermute | solution.py:320
  299.8 20.9 %shard_map.123 = (bf16[256,2176]{1,0:T(8,128)(2,1)}, bf16[256,2176]{1,0:T(8,128)(2,1)}) custom-call(s32[1]{0:T(128)} %bitcast.me, bf16[2,80,2432]{2,1,0:T(8,128)(2,1)S(1)} %shard_map.119.refs_9_.refs_0_, bf16[2,80,2432]{2,1,0:T(8,128)(2,1)S(1)} %collective-permute-done.44.refs_4_.refs_1_, bf16[2,80,2432]{2,1,0:T(8,128)(2,1)S(1)} %copy-done.12, ...), custom_call_target="tpu_custom_call" | custom-call | flops 400000000 | bytes 400000000 | tf_op jit(solution)/shard_map/pallas_call | solution.py:292
  330.7 8.2 %collective-permute-done.53.refs_0_.refs_1_ = bf16[1,80,2432]{2,1,0:T(8,128)(2,1)S(1)} collective-permute-done((bf16[1,80,2432]{2,1,0:T(8,128)(2,1)S(1)}, bf16[1,80,2432]{2,1,0:T(8,128)(2,1)S(1)}, u32[]{:S(2)}, u32[]{:S(2)}) %collective-permute-start.53) | collective-permute-done | bytes 389152 | tf_op jit(solution)/shard_map/ppermute | solution.py:320
  342.0 4.3 %collective-permute-done.57.refs_4_ = bf16[1,80,1152]{2,1,0:T(8,128)(2,1)S(1)} collective-permute-done((bf16[1,80,1152]{2,1,0:T(8,128)(2,1)S(1)}, bf16[1,80,1152]{2,1,0:T(8,128)(2,1)S(1)}, u32[]{:S(2)}, u32[]{:S(2)}) %collective-permute-start.57) | collective-permute-done | bytes 184352 | tf_op jit(solution)/shard_map/ppermute | solution.py:320
  346.4 10.5 %shard_map.128 = (bf16[256,2176]{1,0:T(8,128)(2,1)S(1)}, bf16[256,2176]{1,0:T(8,128)(2,1)S(1)}) custom-call(s32[1]{0:T(128)} %bitcast.me, bf16[1,80,2432]{2,1,0:T(8,128)(2,1)S(1)} %shard_map.124.refs_1_.refs_0_, bf16[1,80,2432]{2,1,0:T(8,128)(2,1)S(1)} %collective-permute-done.53.refs_0_.refs_1_, ...), custom_call_target="tpu_custom_call" | custom-call | flops 400000000 | bytes 400000000 | tf_op jit(solution)/shard_map/pallas_call | solution.py:292
  356.9 8.3 %collective-permute-done.58.refs_2_ = bf16[128,2176]{1,0:T(8,128)(2,1)S(1)} collective-permute-done((bf16[128,2176]{1,0:T(8,128)(2,1)S(1)}, bf16[128,2176]{1,0:T(8,128)(2,1)S(1)}, u32[]{:S(2)}, u32[]{:S(2)}) %collective-permute-start.58) | collective-permute-done | bytes 557088 | tf_op jit(solution)/shard_map/ppermute | solution.py:320
  (268 shorter events, 114.7 us)
Async XLA Ops:
  7.6 48.1 %collective-permute-start.12 = (bf16[256,2048]{1,0:T(8,128)(2,1)S(1)}, bf16[256,2048]{1,0:T(8,128)(2,1)S(1)}, u32[]{:S(2)}, u32[]{:S(2)}) collective-permute-start(bf16[256,2048]{1,0:T(8,128)(2,1)S(1)} %pad_maximum_fusion.same), channel_id=1, source_target_pairs={{0,6},{1,7},{2,4},{3,5},{4,2},{5,3},{6,0},{7,1},{8,14},{9,15},{10,... | collective-permute-start | bytes 3145736 | tf_op jit(solution)/shard_map/ppermute | solution.py:320
  55.9 26.3 %collective-permute-start.18 = (bf16[256,2048]{1,0:T(8,128)(2,1)S(1)}, bf16[256,2048]{1,0:T(8,128)(2,1)S(1)}, u32[]{:S(2)}, u32[]{:S(2)}) collective-permute-start(bf16[256,2048]{1,0:T(8,128)(2,1)S(1)} %get-tuple-element.74.same), channel_id=1, source_target_pairs={{0,2},{1,3},{2,0},{3,1},{4,6},{5,7},{6,4},{7,5},{8,10},{9,11},{10,... | collective-permute-start | bytes 3145736 | tf_op jit(solution)/shard_map/ppermute | solution.py:320
  95.4 39.6 %collective-permute-start.27 = (bf16[256,2048]{1,0:T(8,128)(2,1)S(1)}, bf16[256,2048]{1,0:T(8,128)(2,1)S(1)}, u32[]{:S(2)}, u32[]{:S(2)}) collective-permute-start(bf16[256,2048]{1,0:T(8,128)(2,1)S(1)} %pad_maximum_fusion.same), channel_id=1, source_target_pairs={{0,2},{1,3},{2,0},{3,1},{4,6},{5,7},{6,4},{7,5},{8,10},{9,11},{10,... | collective-permute-start | bytes 3145736 | tf_op jit(solution)/shard_map/ppermute | solution.py:320
  118.4 27.2 %collective-permute-start.25 = (bf16[2,80,2432]{2,1,0:T(8,128)(2,1)S(1)}, bf16[2,80,2432]{2,1,0:T(8,128)(2,1)S(1)}, u32[]{:S(2)}, u32[]{:S(2)}) collective-permute-start(bf16[2,80,2432]{2,1,0:T(8,128)(2,1)S(1)} %shard_map.110.refs_9_.refs_0_), channel_id=1, source_target_pairs={{0,8},{8,0},{16,24},{24,16},{1,9},{9,1},{17,25},{25,17},{2,10},{10... | collective-permute-start | bytes 2334728 | tf_op jit(solution)/shard_map/ppermute | solution.py:320
  119.0 26.6 %collective-permute-start.26 = (bf16[2,80,2432]{2,1,0:T(8,128)(2,1)S(1)}, bf16[2,80,2432]{2,1,0:T(8,128)(2,1)S(1)}, u32[]{:S(2)}, u32[]{:S(2)}) collective-permute-start(bf16[2,80,2432]{2,1,0:T(8,128)(2,1)S(1)} %shard_map.110.refs_9_.refs_0_), channel_id=1, source_target_pairs={{0,16},{8,24},{16,0},{24,8},{1,17},{9,25},{17,1},{25,9},{2,18},{10... | collective-permute-start | bytes 2334728 | tf_op jit(solution)/shard_map/ppermute | solution.py:320
  120.2 25.2 %collective-permute-start.23 = (bf16[2,80,1152]{2,1,0:T(8,128)(2,1)S(1)}, bf16[2,80,1152]{2,1,0:T(8,128)(2,1)S(1)}, u32[]{:S(2)}, u32[]{:S(2)}) collective-permute-start(bf16[2,80,1152]{2,1,0:T(8,128)(2,1)S(1)} %get-tuple-element.88), channel_id=1, source_target_pairs={{0,8},{8,0},{16,24},{24,16},{1,9},{9,1},{17,25},{25,17},{2,10},{10... | collective-permute-start | bytes 1105928 | tf_op jit(solution)/shard_map/ppermute | solution.py:320
  149.8 28.0 %collective-permute-start.31 = (bf16[2,80,2304]{2,1,0:T(8,128)(2,1)S(1)}, bf16[2,80,2304]{2,1,0:T(8,128)(2,1)S(1)}, u32[]{:S(2)}, u32[]{:S(2)}) collective-permute-start(bf16[2,80,2304]{2,1,0:T(8,128)(2,1)S(1)} %get-tuple-element.91.rest_0_), channel_id=1, source_target_pairs={{0,8},{8,0},{16,24},{24,16},{1,9},{9,1},{17,25},{25,17},{2,10},{10... | collective-permute-start | bytes 2211848 | tf_op jit(solution)/shard_map/ppermute | solution.py:320
  151.3 26.5 %collective-permute-start.32 = (bf16[2,80,2304]{2,1,0:T(8,128)(2,1)S(1)}, bf16[2,80,2304]{2,1,0:T(8,128)(2,1)S(1)}, u32[]{:S(2)}, u32[]{:S(2)}) collective-permute-start(bf16[2,80,2304]{2,1,0:T(8,128)(2,1)S(1)} %get-tuple-element.96), channel_id=1, source_target_pairs={{0,16},{8,24},{16,0},{24,8},{1,17},{9,25},{17,1},{25,9},{2,18},{10... | collective-permute-start | bytes 2211848 | tf_op jit(solution)/shard_map/ppermute | solution.py:320
  152.5 25.3 %collective-permute-start.33 = (bf16[2,80,1280]{2,1,0:T(8,128)(2,1)S(1)}, bf16[2,80,1280]{2,1,0:T(8,128)(2,1)S(1)}, u32[]{:S(2)}, u32[]{:S(2)}) collective-permute-start(bf16[2,80,1280]{2,1,0:T(8,128)(2,1)S(1)} %get-tuple-element.98), channel_id=1, source_target_pairs={{0,8},{8,0},{16,24},{24,16},{1,9},{9,1},{17,25},{25,17},{2,10},{10... | collective-permute-start | bytes 1228808 | tf_op jit(solution)/shard_map/ppermute | solution.py:320
  153.0 24.8 %collective-permute-start.34 = (bf16[2,80,1152]{2,1,0:T(8,128)(2,1)S(1)}, bf16[2,80,1152]{2,1,0:T(8,128)(2,1)S(1)}, u32[]{:S(2)}, u32[]{:S(2)}) collective-permute-start(bf16[2,80,1152]{2,1,0:T(8,128)(2,1)S(1)} %get-tuple-element.99), channel_id=1, source_target_pairs={{0,16},{8,24},{16,0},{24,8},{1,17},{9,25},{17,1},{25,9},{2,18},{10... | collective-permute-start | bytes 1105928 | tf_op jit(solution)/shard_map/ppermute | solution.py:320
  179.4 28.0 %collective-permute-start.35 = (bf16[2,80,2432]{2,1,0:T(8,128)(2,1)}, bf16[2,80,2432]{2,1,0:T(8,128)(2,1)S(1)}, u32[]{:S(2)}, u32[]{:S(2)}) collective-permute-start(bf16[2,80,2432]{2,1,0:T(8,128)(2,1)} %shard_map.114.refs_9_.refs_0_), channel_id=1, source_target_pairs={{0,8},{8,0},{16,24},{24,16},{1,9},{9,1},{17,25},{25,17},{2,10},{10... | collective-permute-start | bytes 2334728 | tf_op jit(solution)/shard_map/ppermute | solution.py:320
  180.5 26.8 %collective-permute-start.36 = (bf16[2,80,2432]{2,1,0:T(8,128)(2,1)}, bf16[2,80,2432]{2,1,0:T(8,128)(2,1)S(1)}, u32[]{:S(2)}, u32[]{:S(2)}) collective-permute-start(bf16[2,80,2432]{2,1,0:T(8,128)(2,1)} %shard_map.114.refs_9_.refs_0_), channel_id=1, source_target_pairs={{0,16},{8,24},{16,0},{24,8},{1,17},{9,25},{17,1},{25,9},{2,18},{10... | collective-permute-start | bytes 2334728 | tf_op jit(solution)/shard_map/ppermute | solution.py:320
  211.7 28.3 %collective-permute-start.41 = (bf16[256,2176]{1,0:T(8,128)(2,1)}, bf16[256,2176]{1,0:T(8,128)(2,1)S(1)}, u32[]{:S(2)}, u32[]{:S(2)}) collective-permute-start(bf16[256,2176]{1,0:T(8,128)(2,1)} %get-tuple-element.109), channel_id=1, source_target_pairs={{0,1},{1,0},{2,3},{3,2},{4,5},{5,4},{6,7},{7,6},{8,9},{9,8},{10,11... | collective-permute-start | bytes 3342344 | tf_op jit(solution)/shard_map/ppermute | solution.py:320
  211.7 28.3 %collective-permute-start.42 = (bf16[2,80,1280]{2,1,0:T(8,128)(2,1)S(1)}, bf16[2,80,1280]{2,1,0:T(8,128)(2,1)S(1)}, u32[]{:S(2)}, u32[]{:S(2)}) collective-permute-start(bf16[2,80,1280]{2,1,0:T(8,128)(2,1)S(1)} %get-tuple-element.110), channel_id=1, source_target_pairs={{0,8},{8,0},{16,24},{24,16},{1,9},{9,1},{17,25},{25,17},{2,10},{10... | collective-permute-start | bytes 1228808 | tf_op jit(solution)/shard_map/ppermute | solution.py:320
  212.2 38.2 %collective-permute-start.39 = (bf16[2,80,2304]{2,1,0:T(8,128)(2,1)S(1)}, bf16[2,80,2304]{2,1,0:T(8,128)(2,1)S(1)}, u32[]{:S(2)}, u32[]{:S(2)}) collective-permute-start(bf16[2,80,2304]{2,1,0:T(8,128)(2,1)S(1)} %get-tuple-element.102.rest_0_), channel_id=1, source_target_pairs={{0,8},{8,0},{16,24},{24,16},{1,9},{9,1},{17,25},{25,17},{2,10},{10... | collective-permute-start | bytes 2211848 | tf_op jit(solution)/shard_map/ppermute | solution.py:320
  213.7 36.7 %collective-permute-start.40 = (bf16[2,80,2304]{2,1,0:T(8,128)(2,1)S(1)}, bf16[2,80,2304]{2,1,0:T(8,128)(2,1)S(1)}, u32[]{:S(2)}, u32[]{:S(2)}) collective-permute-start(bf16[2,80,2304]{2,1,0:T(8,128)(2,1)S(1)} %get-tuple-element.108), channel_id=1, source_target_pairs={{0,16},{8,24},{16,0},{24,8},{1,17},{9,25},{17,1},{25,9},{2,18},{10... | collective-permute-start | bytes 2211848 | tf_op jit(solution)/shard_map/ppermute | solution.py:320
  214.9 25.0 %collective-permute-start.43 = (bf16[2,80,1152]{2,1,0:T(8,128)(2,1)S(1)}, bf16[2,80,1152]{2,1,0:T(8,128)(2,1)S(1)}, u32[]{:S(2)}, u32[]{:S(2)}) collective-permute-start(bf16[2,80,1152]{2,1,0:T(8,128)(2,1)S(1)} %get-tuple-element.111), channel_id=1, source_target_pairs={{0,16},{8,24},{16,0},{24,8},{1,17},{9,25},{17,1},{25,9},{2,18},{10... | collective-permute-start | bytes 1105928 | tf_op jit(solution)/shard_map/ppermute | solution.py:320
  242.5 31.3 %collective-permute-start.46 = (bf16[256,2176]{1,0:T(8,128)(2,1)S(1)}, bf16[256,2176]{1,0:T(8,128)(2,1)S(1)}, u32[]{:S(2)}, u32[]{:S(2)}) collective-permute-start(bf16[256,2176]{1,0:T(8,128)(2,1)S(1)} %shard_map.118.rest_0_), channel_id=1, source_target_pairs={{0,2},{1,3},{2,0},{3,1},{4,6},{5,7},{6,4},{7,5},{8,10},{9,11},{10,... | collective-permute-start | bytes 3342344 | tf_op jit(solution)/shard_map/ppermute | solution.py:320
  284.4 36.3 %collective-permute-start.52 = (bf16[128,2176]{1,0:T(8,128)(2,1)}, bf16[128,2176]{1,0:T(8,128)(2,1)S(1)}, u32[]{:S(2)}, u32[]{:S(2)}) collective-permute-start(bf16[128,2176]{1,0:T(8,128)(2,1)} %get-tuple-element.121), channel_id=1, source_target_pairs={{0,4},{1,5},{2,6},{3,7},{4,0},{5,1},{6,2},{7,3},{8,12},{9,13},{10,... | collective-permute-start | bytes 1671176 | tf_op jit(solution)/shard_map/ppermute | solution.py:320
  287.5 33.3 %collective-permute-start.47 = (bf16[1,80,2304]{2,1,0:T(8,128)(2,1)}, bf16[1,80,2304]{2,1,0:T(8,128)(2,1)}, u32[]{:S(2)}, u32[]{:S(2)}) collective-permute-start(bf16[1,80,2304]{2,1,0:T(8,128)(2,1)} %get-tuple-element.114.refs_3_), channel_id=1, source_target_pairs={{0,8},{8,0},{16,24},{24,16},{1,9},{9,1},{17,25},{25,17},{2,10},{10... | collective-permute-start | bytes 1105928 | tf_op jit(solution)/shard_map/ppermute | solution.py:320
  288.9 31.8 %collective-permute-start.48 = (bf16[1,80,2304]{2,1,0:T(8,128)(2,1)}, bf16[1,80,2304]{2,1,0:T(8,128)(2,1)}, u32[]{:S(2)}, u32[]{:S(2)}) collective-permute-start(bf16[1,80,2304]{2,1,0:T(8,128)(2,1)} %get-tuple-element.115), channel_id=1, source_target_pairs={{0,16},{8,24},{16,0},{24,8},{1,17},{9,25},{17,1},{25,9},{2,18},{10... | collective-permute-start | bytes 1105928 | tf_op jit(solution)/shard_map/ppermute | solution.py:320
  325.2 31.7 %collective-permute-start.22 = (bf16[256,2176]{1,0:T(8,128)(2,1)S(1)}, bf16[256,2176]{1,0:T(8,128)(2,1)S(1)}, u32[]{:S(2)}, u32[]{:S(2)}) collective-permute-start(bf16[256,2176]{1,0:T(8,128)(2,1)S(1)} %copy-done.47), channel_id=1, source_target_pairs={{0,1},{1,0},{2,3},{3,2},{4,5},{5,4},{6,7},{7,6},{8,9},{9,8},{10,11... | collective-permute-start | bytes 3342344 | tf_op jit(solution)/shard_map/ppermute | solution.py:320
  326.7 38.5 %collective-permute-start.59 = (bf16[256,2176]{1,0:T(8,128)(2,1)S(1)}, bf16[256,2176]{1,0:T(8,128)(2,1)S(1)}, u32[]{:S(2)}, u32[]{:S(2)}) collective-permute-start(bf16[256,2176]{1,0:T(8,128)(2,1)S(1)} %shard_map.126.refs_2_), channel_id=1, source_target_pairs={{0,2},{1,3},{2,0},{3,1},{4,6},{5,7},{6,4},{7,5},{8,10},{9,11},{10,... | collective-permute-start | bytes 3342344 | tf_op jit(solution)/shard_map/ppermute | solution.py:320
  330.6 34.7 %collective-permute-start.58 = (bf16[128,2176]{1,0:T(8,128)(2,1)S(1)}, bf16[128,2176]{1,0:T(8,128)(2,1)S(1)}, u32[]{:S(2)}, u32[]{:S(2)}) collective-permute-start(bf16[128,2176]{1,0:T(8,128)(2,1)S(1)} %copy-done.29), channel_id=1, source_target_pairs={{0,4},{1,5},{2,6},{3,7},{4,0},{5,1},{6,2},{7,3},{8,12},{9,13},{10,... | collective-permute-start | bytes 1671176 | tf_op jit(solution)/shard_map/ppermute | solution.py:320
  (86 other events, 774.6 us)

commit v7 on v6

--- a/solution.py
+++ b/solution.py
@@ -9,7 +9,7 @@
 EXPERTS = 64
 TOPK = 8
 CAP = 40
-VMEM_BYTES = 50 * 1024 * 1024
+VMEM_BYTES = 40 * 1024 * 1024
 
 
 def moves(ample):

time: 377 us -> 350 us (0.928)
  Pallas kernels: 183 us -> 162 us
  local copies, waits for them, and re-layouts: 19 us -> 7.17 us
  waiting for transfers between devices: 108 us -> 116 us
    unnamed x98 -> x28, local copies, waits for them, and re-layouts: 16.2 us -> 4.11 us
    ppermute x61, waiting for transfers between devices: 108 us -> 116 us  [swap(): return lax.ppermute(value, axis, [(n, n ^ bits) for n in range(count)])]
    pallas_call x9, Pallas kernels: 12.9 us -> 4.64 us  [between(): pl.pallas_call(functools.partial(between_kernel, len(after), *given), gri...]
    pallas_call x5, Pallas kernels: 83.6 us -> 78.9 us  [combine(): pl.pallas_call(functools.partial(combine_kernel, count, len(after)), grid...]
    pallas_call x5, Pallas kernels: 77 us -> 72.6 us  [partial_sums(): pl.pallas_call(functools.partial(partial_kernel, count), grid_spec=pltpu....]
  transfers between devices with their start and end apart: 61 -> 61, of which waited for: 25 -> 29; matrix products, arithmetic and copies ran while one was open for 1% -> 2% of each run, Pallas kernels for 44% -> 45%
where the time goes in v7:
time: 350 us; the launch traced here: 348 us
  Pallas kernels  162 us (46%)
  waiting for transfers between devices  116 us (33%)
  starting transfers between devices  55.2 us (16%)
  local copies, waits for them, and re-layouts  7.17 us (2%)
  other arithmetic  5.87 us (2%)
    ppermute x61, waiting for transfers between devices, swap(): return lax.ppermute(value, axis, [(n, n ^ bits) for n in range(count)])  116 us
    pallas_call x5, Pallas kernels, combine(): pl.pallas_call(functools.partial(combine_kernel, count, len(after)), grid...  78.9 us
    pallas_call x5, Pallas kernels, partial_sums(): pl.pallas_call(functools.partial(partial_kernel, count), grid_spec=pltpu....  72.6 us
    ppermute x61, starting transfers between devices, swap(): return lax.ppermute(value, axis, [(n, n ^ bits) for n in range(count)])  55.2 us
  transfers between devices with their start and end apart: 61, of which 29 were waited for; matrix products, arithmetic and copies ran while one was open for 2% of the time, Pallas kernels for 45%

profile of v7, /device:TPU:8, one launch (start us, length us, event | category | flops | bytes accessed | tf_op | source)
XLA Modules:
  0.0 347.9 jit_solution(6503612815945776225)
XLA Ops:
  1.4 3.0 collective-permute-start.7
  10.4 9.6 %shard_map.103 = (bf16[1,80,2304]{2,1,0:T(8,128)(2,1)S(1)}, bf16[1,80,2304]{2,1,0:T(8,128)(2,1)S(1)}, bf16[1,80,2304]{2,1,0:T(8,128)(2,1)S(1)}, bf16[1,80,1152]{2,1,0:T(8,128)(2,1)S(1)}, bf16[1,80,1152]{2,1,0:T(8,128)(2,1)S(1)}) custom-call(s32[1]{0:T(128)} %bitcast.me, bf16[256,2048]{1,0:T(8,128)(2,1)S(1)} %pad_maximum_fusion.same, ...), custom_call_target="tpu_custom_call" | custom-call | flops 1000 | bytes 1000 | tf_op jit(solution)/shard_map/pallas_call | solution.py:90
  23.2 3.7 %collective-permute-done.2.refs_2_ = bf16[1,80,1152]{2,1,0:T(8,128)(2,1)S(1)} collective-permute-done((bf16[1,80,1152]{2,1,0:T(8,128)(2,1)S(1)}, bf16[1,80,1152]{2,1,0:T(8,128)(2,1)S(1)}, u32[]{:S(2)}, u32[]{:S(2)}) %collective-permute-start.2) | collective-permute-done | bytes 184352 | tf_op jit(solution)/shard_map/ppermute | solution.py:320
  34.0 4.5 %collective-permute-done.4.from_x = bf16[1,80,2304]{2,1,0:T(8,128)(2,1)S(1)} collective-permute-done((bf16[1,80,2304]{2,1,0:T(8,128)(2,1)S(1)}, bf16[1,80,2304]{2,1,0:T(8,128)(2,1)S(1)}, u32[]{:S(2)}, u32[]{:S(2)}) %collective-permute-start.4) | collective-permute-done | bytes 368672 | tf_op jit(solution)/shard_map/ppermute | solution.py:320
  43.5 11.7 %collective-permute-done.12.refs_2_ = bf16[256,2048]{1,0:T(8,128)(2,1)} collective-permute-done((bf16[256,2048]{1,0:T(8,128)(2,1)S(1)}, bf16[256,2048]{1,0:T(8,128)(2,1)}, u32[]{:S(2)}, u32[]{:S(2)}) %collective-permute-start.12) | collective-permute-done | bytes 1048608 | tf_op jit(solution)/shard_map/ppermute | solution.py:320
  59.3 17.8 %shard_map.107 = (bf16[2,80,2304]{2,1,0:T(8,128)(2,1)S(1)}, bf16[2,80,2304]{2,1,0:T(8,128)(2,1)S(1)}, bf16[2,80,2304]{2,1,0:T(8,128)(2,1)S(1)}, bf16[2,80,1152]{2,1,0:T(8,128)(2,1)S(1)}, bf16[2,80,1152]{2,1,0:T(8,128)(2,1)S(1)}) custom-call(s32[1]{0:T(128)} %bitcast.me, bf16[256,2048]{1,0:T(8,128)(2,1)S(1)} %get-tuple-element.74.same, ...), custom_call_target="tpu_custom_call" | custom-call | flops 400000000 | bytes 400000000 | tf_op jit(solution)/shard_map/pallas_call | solution.py:90
  82.2 5.5 %collective-permute-done.16.refs_2_ = bf16[2,80,1152]{2,1,0:T(8,128)(2,1)S(1)} collective-permute-done((bf16[2,80,1152]{2,1,0:T(8,128)(2,1)S(1)}, bf16[2,80,1152]{2,1,0:T(8,128)(2,1)S(1)}, u32[]{:S(2)}, u32[]{:S(2)}) %collective-permute-start.16) | collective-permute-done | bytes 368672 | tf_op jit(solution)/shard_map/ppermute | solution.py:320
  93.6 17.8 %shard_map.109 = (bf16[2,80,2304]{2,1,0:T(8,128)(2,1)S(1)}, bf16[2,80,2304]{2,1,0:T(8,128)(2,1)S(1)}, bf16[2,80,2304]{2,1,0:T(8,128)(2,1)S(1)}, bf16[2,80,1152]{2,1,0:T(8,128)(2,1)S(1)}, bf16[2,80,1152]{2,1,0:T(8,128)(2,1)S(1)}) custom-call(s32[1]{0:T(128)} %bitcast.me, bf16[256,2048]{1,0:T(8,128)(2,1)S(1)} %get-tuple-element.82.same, ...), custom_call_target="tpu_custom_call" | custom-call | flops 400000000 | bytes 400000000 | tf_op jit(solution)/shard_map/pallas_call | solution.py:90
  117.4 10.5 %shard_map.111 = (bf16[256,2176]{1,0:T(8,128)(2,1)S(1)}, bf16[256,2176]{1,0:T(8,128)(2,1)S(1)}) custom-call(s32[1]{0:T(128)} %bitcast.me, bf16[1,80,2432]{2,1,0:T(8,128)(2,1)S(1)} %shard_map.105.refs_3_.refs_0_, bf16[1,80,2432]{2,1,0:T(8,128)(2,1)S(1)} %collective-permute-done.10.refs_0_.refs_1_, ...), custom_call_target="tpu_custom_call" | custom-call | flops 400000000 | bytes 400000000 | tf_op jit(solution)/shard_map/pallas_call | solution.py:292
  128.0 12.2 %collective-permute-done.23.refs_2_ = bf16[2,80,1152]{2,1,0:T(8,128)(2,1)S(1)} collective-permute-done((bf16[2,80,1152]{2,1,0:T(8,128)(2,1)S(1)}, bf16[2,80,1152]{2,1,0:T(8,128)(2,1)S(1)}, u32[]{:S(2)}, u32[]{:S(2)}) %collective-permute-start.23) | collective-permute-done | bytes 368672 | tf_op jit(solution)/shard_map/ppermute | solution.py:320
  145.5 17.8 %shard_map.113 = (bf16[2,80,2304]{2,1,0:T(8,128)(2,1)S(1)}, bf16[2,80,2304]{2,1,0:T(8,128)(2,1)S(1)}, bf16[2,80,2304]{2,1,0:T(8,128)(2,1)S(1)}, bf16[2,80,1152]{2,1,0:T(8,128)(2,1)S(1)}, bf16[2,80,1152]{2,1,0:T(8,128)(2,1)S(1)}) custom-call(s32[1]{0:T(128)} %bitcast.me, bf16[256,2048]{1,0:T(8,128)(2,1)S(1)} %get-tuple-element.90.same, ...), custom_call_target="tpu_custom_call" | custom-call | flops 400000000 | bytes 400000000 | tf_op jit(solution)/shard_map/pallas_call | solution.py:90
  163.3 5.6 %collective-permute-done.34.rest_2_.refs_4_ = bf16[2,80,1152]{2,1,0:T(8,128)(2,1)S(1)} collective-permute-done((bf16[2,80,1152]{2,1,0:T(8,128)(2,1)S(1)}, bf16[2,80,1152]{2,1,0:T(8,128)(2,1)S(1)}, u32[]{:S(2)}, u32[]{:S(2)}) %collective-permute-start.34) | collective-permute-done | bytes 368672 | tf_op jit(solution)/shard_map/ppermute | solution.py:320
  173.8 19.0 %shard_map.115 = (bf16[256,2176]{1,0:T(8,128)(2,1)S(1)}, bf16[256,2176]{1,0:T(8,128)(2,1)S(1)}) custom-call(s32[1]{0:T(128)} %bitcast.me, bf16[2,80,2432]{2,1,0:T(8,128)(2,1)S(1)} %shard_map.110.refs_9_.refs_0_, bf16[2,80,2432]{2,1,0:T(8,128)(2,1)S(1)} %collective-permute-done.25.refs_4_.refs_1_, ...), custom_call_target="tpu_custom_call" | custom-call | flops 400000000 | bytes 400000000 | tf_op jit(solution)/shard_map/pallas_call | solution.py:292
  192.8 3.8 %collective-permute-done.29.refs_2_ = bf16[2,80,1152]{2,1,0:T(8,128)(2,1)S(1)} collective-permute-done((bf16[2,80,1152]{2,1,0:T(8,128)(2,1)S(1)}, bf16[2,80,1152]{2,1,0:T(8,128)(2,1)S(1)}, u32[]{:S(2)}, u32[]{:S(2)}) %collective-permute-start.29) | collective-permute-done | bytes 368672 | tf_op jit(solution)/shard_map/ppermute | solution.py:320
  201.8 9.6 %shard_map.117 = (bf16[1,80,2304]{2,1,0:T(8,128)(2,1)S(1)}, bf16[1,80,2304]{2,1,0:T(8,128)(2,1)S(1)}, bf16[1,80,2304]{2,1,0:T(8,128)(2,1)S(1)}, bf16[1,80,1152]{2,1,0:T(8,128)(2,1)S(1)}, bf16[1,80,1152]{2,1,0:T(8,128)(2,1)S(1)}) custom-call(s32[1]{0:T(128)} %bitcast.me, bf16[256,2048]{1,0:T(8,128)(2,1)S(1)} %pad_maximum_fusion.same, ...), custom_call_target="tpu_custom_call" | custom-call | flops 400000000 | bytes 400000000 | tf_op jit(solution)/shard_map/pallas_call | solution.py:90
  211.5 14.5 %collective-permute-done.43.refs_4_ = bf16[2,80,1152]{2,1,0:T(8,128)(2,1)S(1)} collective-permute-done((bf16[2,80,1152]{2,1,0:T(8,128)(2,1)S(1)}, bf16[2,80,1152]{2,1,0:T(8,128)(2,1)S(1)}, u32[]{:S(2)}, u32[]{:S(2)}) %collective-permute-start.43) | collective-permute-done | bytes 368672 | tf_op jit(solution)/shard_map/ppermute | solution.py:320
  228.9 3.1 collective-permute-done.37.rest_1_.refs_2_
  236.3 19.0 %shard_map.120 = (bf16[256,2176]{1,0:T(8,128)(2,1)S(1)}, bf16[256,2176]{1,0:T(8,128)(2,1)S(1)}) custom-call(s32[1]{0:T(128)} %bitcast.me, bf16[2,80,2432]{2,1,0:T(8,128)(2,1)S(1)} %shard_map.114.refs_9_.refs_0_, bf16[2,80,2432]{2,1,0:T(8,128)(2,1)S(1)} %collective-permute-done.35.refs_4_.refs_1_, ...), custom_call_target="tpu_custom_call" | custom-call | flops 400000000 | bytes 400000000 | tf_op jit(solution)/shard_map/pallas_call | solution.py:292
  268.2 8.8 %collective-permute-done.50.refs_4_ = bf16[2,80,1152]{2,1,0:T(8,128)(2,1)} collective-permute-done((bf16[2,80,1152]{2,1,0:T(8,128)(2,1)}, bf16[2,80,1152]{2,1,0:T(8,128)(2,1)}, u32[]{:S(2)}, u32[]{:S(2)}) %collective-permute-start.50) | collective-permute-done | bytes 368672 | tf_op jit(solution)/shard_map/ppermute | solution.py:320
  279.1 19.9 %shard_map.123 = (bf16[256,2176]{1,0:T(8,128)(2,1)S(1)}, bf16[256,2176]{1,0:T(8,128)(2,1)S(1)}) custom-call(s32[1]{0:T(128)} %bitcast.me, bf16[2,80,2432]{2,1,0:T(8,128)(2,1)S(1)} %shard_map.119.refs_9_.refs_0_, bf16[2,80,2432]{2,1,0:T(8,128)(2,1)S(1)} %collective-permute-done.44.refs_4_.refs_1_, bf16[2,80,2432]{2,1,0:T(8,128)(2,1)S(1)} %copy-done.1, ...), custom_call_target="tpu_custom_call" | custom-call | flops 400000000 | bytes 400000000 | tf_op jit(solution)/shard_map/pallas_call | solution.py:292
  307.2 7.7 %collective-permute-done.53.refs_0_.refs_1_ = bf16[1,80,2432]{2,1,0:T(8,128)(2,1)S(1)} collective-permute-done((bf16[1,80,2432]{2,1,0:T(8,128)(2,1)S(1)}, bf16[1,80,2432]{2,1,0:T(8,128)(2,1)S(1)}, u32[]{:S(2)}, u32[]{:S(2)}) %collective-permute-start.53) | collective-permute-done | bytes 389152 | tf_op jit(solution)/shard_map/ppermute | solution.py:320
  317.3 5.0 %collective-permute-done.57.refs_4_ = bf16[1,80,1152]{2,1,0:T(8,128)(2,1)S(1)} collective-permute-done((bf16[1,80,1152]{2,1,0:T(8,128)(2,1)S(1)}, bf16[1,80,1152]{2,1,0:T(8,128)(2,1)S(1)}, u32[]{:S(2)}, u32[]{:S(2)}) %collective-permute-start.57) | collective-permute-done | bytes 184352 | tf_op jit(solution)/shard_map/ppermute | solution.py:320
  322.3 10.5 %shard_map.128 = (bf16[256,2176]{1,0:T(8,128)(2,1)S(1)}, bf16[256,2176]{1,0:T(8,128)(2,1)S(1)}) custom-call(s32[1]{0:T(128)} %bitcast.me, bf16[1,80,2432]{2,1,0:T(8,128)(2,1)S(1)} %shard_map.124.refs_1_.refs_0_, bf16[1,80,2432]{2,1,0:T(8,128)(2,1)S(1)} %collective-permute-done.53.refs_0_.refs_1_, ...), custom_call_target="tpu_custom_call" | custom-call | flops 400000000 | bytes 400000000 | tf_op jit(solution)/shard_map/pallas_call | solution.py:292
  332.8 9.3 %collective-permute-done.58.refs_2_ = bf16[128,2176]{1,0:T(8,128)(2,1)S(1)} collective-permute-done((bf16[128,2176]{1,0:T(8,128)(2,1)S(1)}, bf16[128,2176]{1,0:T(8,128)(2,1)S(1)}, u32[]{:S(2)}, u32[]{:S(2)}) %collective-permute-start.58) | collective-permute-done | bytes 557088 | tf_op jit(solution)/shard_map/ppermute | solution.py:320
  (198 shorter events, 96.5 us)
Async XLA Ops:
  7.0 48.2 %collective-permute-start.12 = (bf16[256,2048]{1,0:T(8,128)(2,1)S(1)}, bf16[256,2048]{1,0:T(8,128)(2,1)}, u32[]{:S(2)}, u32[]{:S(2)}) collective-permute-start(bf16[256,2048]{1,0:T(8,128)(2,1)S(1)} %pad_maximum_fusion.same), channel_id=1, source_target_pairs={{0,6},{1,7},{2,4},{3,5},{4,2},{5,3},{6,0},{7,1},{8,14},{9,15},{10,... | collective-permute-start | bytes 3145736 | tf_op jit(solution)/shard_map/ppermute | solution.py:320
  56.7 25.6 %collective-permute-start.18 = (bf16[256,2048]{1,0:T(8,128)(2,1)S(1)}, bf16[256,2048]{1,0:T(8,128)(2,1)S(1)}, u32[]{:S(2)}, u32[]{:S(2)}) collective-permute-start(bf16[256,2048]{1,0:T(8,128)(2,1)S(1)} %get-tuple-element.74.same), channel_id=1, source_target_pairs={{0,2},{1,3},{2,0},{3,1},{4,6},{5,7},{6,4},{7,5},{8,10},{9,11},{10,... | collective-permute-start | bytes 3145736 | tf_op jit(solution)/shard_map/ppermute | solution.py:320
  91.5 36.5 %collective-permute-start.27 = (bf16[256,2048]{1,0:T(8,128)(2,1)S(1)}, bf16[256,2048]{1,0:T(8,128)(2,1)S(1)}, u32[]{:S(2)}, u32[]{:S(2)}) collective-permute-start(bf16[256,2048]{1,0:T(8,128)(2,1)S(1)} %pad_maximum_fusion.same), channel_id=1, source_target_pairs={{0,2},{1,3},{2,0},{3,1},{4,6},{5,7},{6,4},{7,5},{8,10},{9,11},{10,... | collective-permute-start | bytes 3145736 | tf_op jit(solution)/shard_map/ppermute | solution.py:320
  113.3 27.6 %collective-permute-start.25 = (bf16[2,80,2432]{2,1,0:T(8,128)(2,1)S(1)}, bf16[2,80,2432]{2,1,0:T(8,128)(2,1)S(1)}, u32[]{:S(2)}, u32[]{:S(2)}) collective-permute-start(bf16[2,80,2432]{2,1,0:T(8,128)(2,1)S(1)} %shard_map.110.refs_9_.refs_0_), channel_id=1, source_target_pairs={{0,8},{8,0},{16,24},{24,16},{1,9},{9,1},{17,25},{25,17},{2,10},{10... | collective-permute-start | bytes 2334728 | tf_op jit(solution)/shard_map/ppermute | solution.py:320
  114.7 26.2 %collective-permute-start.26 = (bf16[2,80,2432]{2,1,0:T(8,128)(2,1)S(1)}, bf16[2,80,2432]{2,1,0:T(8,128)(2,1)S(1)}, u32[]{:S(2)}, u32[]{:S(2)}) collective-permute-start(bf16[2,80,2432]{2,1,0:T(8,128)(2,1)S(1)} %shard_map.110.refs_9_.refs_0_), channel_id=1, source_target_pairs={{0,16},{8,24},{16,0},{24,8},{1,17},{9,25},{17,1},{25,9},{2,18},{10... | collective-permute-start | bytes 2334728 | tf_op jit(solution)/shard_map/ppermute | solution.py:320
  141.3 27.7 %collective-permute-start.31 = (bf16[2,80,2304]{2,1,0:T(8,128)(2,1)S(1)}, bf16[2,80,2304]{2,1,0:T(8,128)(2,1)S(1)}, u32[]{:S(2)}, u32[]{:S(2)}) collective-permute-start(bf16[2,80,2304]{2,1,0:T(8,128)(2,1)S(1)} %get-tuple-element.91.rest_0_), channel_id=1, source_target_pairs={{0,8},{8,0},{16,24},{24,16},{1,9},{9,1},{17,25},{25,17},{2,10},{10... | collective-permute-start | bytes 2211848 | tf_op jit(solution)/shard_map/ppermute | solution.py:320
  142.4 26.6 %collective-permute-start.32 = (bf16[2,80,2304]{2,1,0:T(8,128)(2,1)S(1)}, bf16[2,80,2304]{2,1,0:T(8,128)(2,1)S(1)}, u32[]{:S(2)}, u32[]{:S(2)}) collective-permute-start(bf16[2,80,2304]{2,1,0:T(8,128)(2,1)S(1)} %get-tuple-element.96), channel_id=1, source_target_pairs={{0,16},{8,24},{16,0},{24,8},{1,17},{9,25},{17,1},{25,9},{2,18},{10... | collective-permute-start | bytes 2211848 | tf_op jit(solution)/shard_map/ppermute | solution.py:320
  143.9 25.1 %collective-permute-start.33 = (bf16[2,80,1280]{2,1,0:T(8,128)(2,1)S(1)}, bf16[2,80,1280]{2,1,0:T(8,128)(2,1)S(1)}, u32[]{:S(2)}, u32[]{:S(2)}) collective-permute-start(bf16[2,80,1280]{2,1,0:T(8,128)(2,1)S(1)} %get-tuple-element.98), channel_id=1, source_target_pairs={{0,8},{8,0},{16,24},{24,16},{1,9},{9,1},{17,25},{25,17},{2,10},{10... | collective-permute-start | bytes 1228808 | tf_op jit(solution)/shard_map/ppermute | solution.py:320
  169.6 27.7 %collective-permute-start.35 = (bf16[2,80,2432]{2,1,0:T(8,128)(2,1)S(1)}, bf16[2,80,2432]{2,1,0:T(8,128)(2,1)S(1)}, u32[]{:S(2)}, u32[]{:S(2)}) collective-permute-start(bf16[2,80,2432]{2,1,0:T(8,128)(2,1)S(1)} %shard_map.114.refs_9_.refs_0_), channel_id=1, source_target_pairs={{0,8},{8,0},{16,24},{24,16},{1,9},{9,1},{17,25},{25,17},{2,10},{10... | collective-permute-start | bytes 2334728 | tf_op jit(solution)/shard_map/ppermute | solution.py:320
  170.7 26.6 %collective-permute-start.36 = (bf16[2,80,2432]{2,1,0:T(8,128)(2,1)S(1)}, bf16[2,80,2432]{2,1,0:T(8,128)(2,1)S(1)}, u32[]{:S(2)}, u32[]{:S(2)}) collective-permute-start(bf16[2,80,2432]{2,1,0:T(8,128)(2,1)S(1)} %shard_map.114.refs_9_.refs_0_), channel_id=1, source_target_pairs={{0,16},{8,24},{16,0},{24,8},{1,17},{9,25},{17,1},{25,9},{2,18},{10... | collective-permute-start | bytes 2334728 | tf_op jit(solution)/shard_map/ppermute | solution.py:320
  172.3 24.3 %collective-permute-start.29 = (bf16[2,80,1152]{2,1,0:T(8,128)(2,1)S(1)}, bf16[2,80,1152]{2,1,0:T(8,128)(2,1)S(1)}, u32[]{:S(2)}, u32[]{:S(2)}) collective-permute-start(bf16[2,80,1152]{2,1,0:T(8,128)(2,1)S(1)} %get-tuple-element.94), channel_id=1, source_target_pairs={{0,8},{8,0},{16,24},{24,16},{1,9},{9,1},{17,25},{25,17},{2,10},{10... | collective-permute-start | bytes 1105928 | tf_op jit(solution)/shard_map/ppermute | solution.py:320
  173.3 24.0 %collective-permute-start.30 = (bf16[2,80,1152]{2,1,0:T(8,128)(2,1)S(1)}, bf16[2,80,1152]{2,1,0:T(8,128)(2,1)S(1)}, u32[]{:S(2)}, u32[]{:S(2)}) collective-permute-start(bf16[2,80,1152]{2,1,0:T(8,128)(2,1)S(1)} %get-tuple-element.95), channel_id=1, source_target_pairs={{0,16},{8,24},{16,0},{24,8},{1,17},{9,25},{17,1},{25,9},{2,18},{10... | collective-permute-start | bytes 1105928 | tf_op jit(solution)/shard_map/ppermute | solution.py:320
  197.6 28.4 %collective-permute-start.41 = (bf16[256,2176]{1,0:T(8,128)(2,1)S(1)}, bf16[256,2176]{1,0:T(8,128)(2,1)S(1)}, u32[]{:S(2)}, u32[]{:S(2)}) collective-permute-start(bf16[256,2176]{1,0:T(8,128)(2,1)S(1)} %get-tuple-element.109), channel_id=1, source_target_pairs={{0,1},{1,0},{2,3},{3,2},{4,5},{5,4},{6,7},{7,6},{8,9},{9,8},{10,11... | collective-permute-start | bytes 3342344 | tf_op jit(solution)/shard_map/ppermute | solution.py:320
  197.7 28.3 %collective-permute-start.42 = (bf16[2,80,1280]{2,1,0:T(8,128)(2,1)S(1)}, bf16[2,80,1280]{2,1,0:T(8,128)(2,1)S(1)}, u32[]{:S(2)}, u32[]{:S(2)}) collective-permute-start(bf16[2,80,1280]{2,1,0:T(8,128)(2,1)S(1)} %get-tuple-element.110), channel_id=1, source_target_pairs={{0,8},{8,0},{16,24},{24,16},{1,9},{9,1},{17,25},{25,17},{2,10},{10... | collective-permute-start | bytes 1228808 | tf_op jit(solution)/shard_map/ppermute | solution.py:320
  198.8 34.2 %collective-permute-start.39 = (bf16[2,80,2304]{2,1,0:T(8,128)(2,1)S(1)}, bf16[2,80,2304]{2,1,0:T(8,128)(2,1)S(1)}, u32[]{:S(2)}, u32[]{:S(2)}) collective-permute-start(bf16[2,80,2304]{2,1,0:T(8,128)(2,1)S(1)} %get-tuple-element.102.rest_0_), channel_id=1, source_target_pairs={{0,8},{8,0},{16,24},{24,16},{1,9},{9,1},{17,25},{25,17},{2,10},{10... | collective-permute-start | bytes 2211848 | tf_op jit(solution)/shard_map/ppermute | solution.py:320
  199.8 33.1 %collective-permute-start.40 = (bf16[2,80,2304]{2,1,0:T(8,128)(2,1)S(1)}, bf16[2,80,2304]{2,1,0:T(8,128)(2,1)S(1)}, u32[]{:S(2)}, u32[]{:S(2)}) collective-permute-start(bf16[2,80,2304]{2,1,0:T(8,128)(2,1)S(1)} %get-tuple-element.108), channel_id=1, source_target_pairs={{0,16},{8,24},{16,0},{24,8},{1,17},{9,25},{17,1},{25,9},{2,18},{10... | collective-permute-start | bytes 2211848 | tf_op jit(solution)/shard_map/ppermute | solution.py:320
  201.3 24.7 %collective-permute-start.43 = (bf16[2,80,1152]{2,1,0:T(8,128)(2,1)S(1)}, bf16[2,80,1152]{2,1,0:T(8,128)(2,1)S(1)}, u32[]{:S(2)}, u32[]{:S(2)}) collective-permute-start(bf16[2,80,1152]{2,1,0:T(8,128)(2,1)S(1)} %get-tuple-element.111), channel_id=1, source_target_pairs={{0,16},{8,24},{16,0},{24,8},{1,17},{9,25},{17,1},{25,9},{2,18},{10... | collective-permute-start | bytes 1105928 | tf_op jit(solution)/shard_map/ppermute | solution.py:320
  226.3 29.0 %collective-permute-start.46 = (bf16[256,2176]{1,0:T(8,128)(2,1)S(1)}, bf16[256,2176]{1,0:T(8,128)(2,1)S(1)}, u32[]{:S(2)}, u32[]{:S(2)}) collective-permute-start(bf16[256,2176]{1,0:T(8,128)(2,1)S(1)} %shard_map.118.rest_0_), channel_id=1, source_target_pairs={{0,2},{1,3},{2,0},{3,1},{4,6},{5,7},{6,4},{7,5},{8,10},{9,11},{10,... | collective-permute-start | bytes 3342344 | tf_op jit(solution)/shard_map/ppermute | solution.py:320
  261.2 37.8 %collective-permute-start.52 = (bf16[128,2176]{1,0:T(8,128)(2,1)}, bf16[128,2176]{1,0:T(8,128)(2,1)S(1)}, u32[]{:S(2)}, u32[]{:S(2)}) collective-permute-start(bf16[128,2176]{1,0:T(8,128)(2,1)} %get-tuple-element.121), channel_id=1, source_target_pairs={{0,4},{1,5},{2,6},{3,7},{4,0},{5,1},{6,2},{7,3},{8,12},{9,13},{10,... | collective-permute-start | bytes 1671176 | tf_op jit(solution)/shard_map/ppermute | solution.py:320
  265.6 33.4 %collective-permute-start.47 = (bf16[1,80,2304]{2,1,0:T(8,128)(2,1)}, bf16[1,80,2304]{2,1,0:T(8,128)(2,1)}, u32[]{:S(2)}, u32[]{:S(2)}) collective-permute-start(bf16[1,80,2304]{2,1,0:T(8,128)(2,1)} %get-tuple-element.114.refs_3_), channel_id=1, source_target_pairs={{0,8},{8,0},{16,24},{24,16},{1,9},{9,1},{17,25},{25,17},{2,10},{10... | collective-permute-start | bytes 1105928 | tf_op jit(solution)/shard_map/ppermute | solution.py:320
  266.7 32.4 %collective-permute-start.48 = (bf16[1,80,2304]{2,1,0:T(8,128)(2,1)}, bf16[1,80,2304]{2,1,0:T(8,128)(2,1)}, u32[]{:S(2)}, u32[]{:S(2)}) collective-permute-start(bf16[1,80,2304]{2,1,0:T(8,128)(2,1)} %get-tuple-element.115), channel_id=1, source_target_pairs={{0,16},{8,24},{16,0},{24,8},{1,17},{9,25},{17,1},{25,9},{2,18},{10... | collective-permute-start | bytes 1105928 | tf_op jit(solution)/shard_map/ppermute | solution.py:320
  301.8 31.1 %collective-permute-start.22 = (bf16[256,2176]{1,0:T(8,128)(2,1)S(1)}, bf16[256,2176]{1,0:T(8,128)(2,1)S(1)}, u32[]{:S(2)}, u32[]{:S(2)}) collective-permute-start(bf16[256,2176]{1,0:T(8,128)(2,1)S(1)} %copy-done.8), channel_id=1, source_target_pairs={{0,1},{1,0},{2,3},{3,2},{4,5},{5,4},{6,7},{7,6},{8,9},{9,8},{10,11... | collective-permute-start | bytes 3342344 | tf_op jit(solution)/shard_map/ppermute | solution.py:320
  303.7 38.5 %collective-permute-start.59 = (bf16[256,2176]{1,0:T(8,128)(2,1)S(1)}, bf16[256,2176]{1,0:T(8,128)(2,1)S(1)}, u32[]{:S(2)}, u32[]{:S(2)}) collective-permute-start(bf16[256,2176]{1,0:T(8,128)(2,1)S(1)} %shard_map.126.refs_2_), channel_id=1, source_target_pairs={{0,2},{1,3},{2,0},{3,1},{4,6},{5,7},{6,4},{7,5},{8,10},{9,11},{10,... | collective-permute-start | bytes 3342344 | tf_op jit(solution)/shard_map/ppermute | solution.py:320
  305.4 36.7 %collective-permute-start.58 = (bf16[128,2176]{1,0:T(8,128)(2,1)S(1)}, bf16[128,2176]{1,0:T(8,128)(2,1)S(1)}, u32[]{:S(2)}, u32[]{:S(2)}) collective-permute-start(bf16[128,2176]{1,0:T(8,128)(2,1)S(1)} %copy-done.6), channel_id=1, source_target_pairs={{0,4},{1,5},{2,6},{3,7},{4,0},{5,1},{6,2},{7,3},{8,12},{9,13},{10,... | collective-permute-start | bytes 1671176 | tf_op jit(solution)/shard_map/ppermute | solution.py:320
  (51 other events, 496.6 us)
